TPU v7x, 32 devices: a whole 2x2x4 slice. The times are simulated.
32 devices in a mesh: col: 8 (over z, x), row: 4 (over y, core).
Axes of the slice: x: 2, y: 2, z: 4, core: 2. Of those that a mesh axis runs over, the one named last changes fastest.
Arguments:
- amplitudes: bfloat16 [512, 16384], P(None, ('col', 'row')), may hold values from -6 to 6
- integrals: bfloat16 [4096, 8192], P('row', 'col'), may hold values from -0.09375 to 0.09375
- wanted: int32 [8, 4, 8], replicated, may hold values from 0 to 31, as said below
- owner: int32 [64], replicated, may hold values from 0 to 63, each once
Outputs:
- ladder: bfloat16 [512, 8192], P(('col', 'row'))
Inputs may be any that keep to these rules, and one draw needn't show every extreme that they name: Each list wanted[c, r, :] names 8 distinct values; at most 2 of them share one value of w // 4, and every list has 2 for at least one such value. `owner`: A permutation of the result tiles.
All inputs are finite; a program needn't handle non-finite values.
Results may differ from a plain program's by a relative error of at most 0.001.
Values may be sent and summed in bfloat16 or wider, within the bound.
No kernel may reach another device: no remote copies, remote signals or barrier semaphores. Data moves between devices by JAX's collectives and lax.ppermute only.
A program may use at most 128 MiB of HBM per device.

v0:
```python
import jax
import jax.numpy as jnp
from jax import lax
from jax.sharding import PartitionSpec as P

TILE = 128


def body(amplitudes, integrals, wanted, owner):
    col_count = lax.axis_size("col")
    col_index = lax.axis_index("col")
    row_index = lax.axis_index("row")
    pair_count = amplitudes.shape[0]
    per_source = amplitudes.shape[1] // TILE
    group_lists = wanted[:, row_index, :]
    own_list = group_lists[col_index]
    everything = lax.all_gather(amplitudes, "col", axis=1, tiled=True)
    everything = everything.reshape(pair_count, col_count * per_source, TILE)
    chosen = jnp.take(everything, own_list, axis=1)
    selected = chosen.reshape(pair_count, -1)
    partial_value = jnp.dot(selected, integrals, preferred_element_type=jnp.float32)
    width = partial_value.shape[1]
    partial_value = partial_value.reshape(col_count, pair_count // col_count, width)
    summed = lax.psum_scatter(partial_value, "row", scatter_dimension=1, tiled=True)
    held_tiles = summed.astype(jnp.bfloat16)
    received = lax.all_to_all(held_tiles, "col", split_axis=0, concat_axis=0, tiled=True)
    per_device = received.shape[1]
    tiles_held = width // TILE
    received = received.reshape(col_count, per_device, tiles_held, TILE)
    source_dev = owner // tiles_held
    slot_ids = owner % tiles_held
    ordered = received[source_dev[None, :], jnp.arange(per_device)[:, None], slot_ids[None, :]]
    return ordered.reshape(per_device, owner.shape[0] * TILE)


def solution(mesh):
    in_specs = (P(None, ("col", "row")), P("row", "col"), P(), P())
    out_specs = P(("col", "row"), None)
    return jax.shard_map(body, mesh=mesh, in_specs=in_specs, out_specs=out_specs, check_vma=False)
```

profile of v0, /device:TPU:0, one launch (start us, length us, event | category | flops | bytes accessed | tf_op | source)
XLA Modules:
  0.0 161.3 jit_solution(6432169339603240235)
XLA Ops:
  6.5 0.0 copy-start
  6.5 0.0 all-gather.2.cloned.1.call-start
  6.5 2.2 %copy.5 = bf16[512,512]{0,1:T(8,128)(2,1)} copy(bf16[512,512]{1,0:T(8,128)(2,1)} %param.4) | data formatting | bytes 1048576 | tf_op args[0]
  8.8 0.0 all-gather.2.cloned.1.call-update
  8.8 0.0 reduce-scatter.2.cloned.1.call-start
  8.8 0.7 fusion.5
  9.5 0.7 compare_and_fusion
  10.2 0.1 broadcast_bitcast_fusion
  10.3 75.3 %all-gather.2.cloned.1.call-done = bf16[512,4096]{0,1:T(8,128)(2,1)} async-done(((bf16[512,512]{0,1:T(8,128)(2,1)}), bf16[512,4096]{0,1:T(8,128)(2,1)}) %all-gather.2.cloned.1.call-update) | async-done | bytes 4194320 | tf_op jit(solution)/shard_map/all_gather | solution.py:17
  85.6 6.5 %copy.6 = bf16[512,32,128]{2,0,1:T(8,128)(2,1)} copy(bf16[512,32,128]{0,2,1:T(8,128)(2,1)} %bitcast.21) | data formatting | bytes 8388608 | tf_op jit(solution)/shard_map/reshape | solution.py:18
  92.1 2.9 %gather_fusion = bf16[8,512,128]{2,1,0:T(8,128)(2,1)S(1)} fusion(bf16[512,32,128]{2,0,1:T(8,128)(2,1)} %copy.6, s32[1024]{0:T(1024)S(1)} %pad_clamp_fusion), kind=kCustom, calls=%fused_computation | custom fusion | bytes 2097184 | tf_op jit(solution)/shard_map/jit(_take)/gather | solution.py:19
  95.0 1.6 %copy.7 = bf16[512,8,128]{2,1,0:T(8,128)(2,1)} copy(bf16[512,8,128]{2,0,1:T(8,128)(2,1)S(1)} %bitcast.20) | data formatting | bytes 2097152 | tf_op jit(solution)/shard_map/jit(_take)/gather | solution.py:19
  96.7 1.5 gather.10
  98.2 0.0 copy-done
  98.2 2.6 %fusion = f32[8,64,1024]{2,1,0:T(8,128)} fusion(bf16[1024,1024]{1,0:T(8,128)(2,1)S(1)} %copy-done, bf16[8,64,1024]{2,1,0:T(8,128)(2,1)S(1)} %gather.10, pred[1024]{0:T(1024)(128)(4,1)S(1)} %broadcast_bitcast_fusion), kind=kOutput, calls=%fused_computation.2 | convolution fusion | flops 1074266112 | bytes 5243904 | tf_op jit(solution)/shard_map/dot_general | solution.py:21
  100.8 0.0 reduce-scatter.2.cloned.1.call-update
  100.8 29.9 %reduce-scatter.2.cloned.1.call-done = f32[8,16,1024]{2,1,0:T(8,128)} async-done(((f32[8,64,1024]{2,1,0:T(8,128)}), f32[8,16,1024]{2,1,0:T(8,128)}) %reduce-scatter.2.cloned.1.call-update) | async-done | bytes 524304 | tf_op jit(solution)/shard_map/reduce_scatter | solution.py:24
  130.7 1.8 %convert_element_type.3 = bf16[8,16,1024]{2,1,0:T(8,128)(2,1)} convert(f32[8,16,1024]{2,1,0:T(8,128)} %reduce-scatter.2.cloned.1.call-done) | non-fusion elementwise | flops 131072 | bytes 786432 | tf_op jit(solution)/shard_map/convert_element_type | solution.py:25
  132.5 5.5 %all-to-all-start = ((bf16[8,16,1024]{2,1,0:T(8,128)(2,1)}), bf16[8,16,1024]{2,1,0:T(8,128)(2,1)S(1)}, u32[]{:S(2)}, u32[]{:S(2)}) async-start(bf16[8,16,1024]{2,1,0:T(8,128)(2,1)} %convert_element_type.3), calls=%async_computation.1 | async-start | bytes 524288 | tf_op jit(solution)/shard_map/all_to_all | solution.py:26
  138.0 0.0 copy-done.1
  138.0 0.1 reshape.85
  138.1 8.8 %all-to-all-done = bf16[8,16,1024]{2,1,0:T(8,128)(2,1)S(1)} async-done(((bf16[8,16,1024]{2,1,0:T(8,128)(2,1)}), bf16[8,16,1024]{2,1,0:T(8,128)(2,1)S(1)}, u32[]{:S(2)}, u32[]{:S(2)}) %all-to-all-start) | async-done | bytes 262176 | tf_op jit(solution)/shard_map/all_to_all | solution.py:26
  146.9 6.7 %gather_fusion.1 = bf16[1024,128]{1,0:T(8,128)(2,1)S(1)} fusion(bf16[8,16,8,128]{3,2,1,0:T(8,128)(2,1)S(1)} %bitcast.19, s32[1024]{0:T(1024)S(1)} %reshape.85), kind=kCustom, calls=%fused_computation.1 | custom fusion | bytes 536576 | tf_op jit(solution)/shard_map/gather | solution.py:32
  153.7 0.8 reshape.76
  (5 shorter events, 0.1 us)
Async XLA Ops:
  6.5 91.7 %copy-start = (bf16[1024,1024]{1,0:T(8,128)(2,1)S(1)}, bf16[1024,1024]{1,0:T(8,128)(2,1)}, u32[]{:S(2)}) copy-start(bf16[1024,1024]{1,0:T(8,128)(2,1)} %param.5) | copy-start | bytes 6291460
  6.5 79.1 %all-gather.2.cloned.1.call-start = ((), (), s32[]{:S(2)}) async-start(), calls=%async_computation.2 | async-start | bytes 4718592 | tf_op jit(solution)/shard_map/all_gather | solution.py:17
  8.8 121.9 %reduce-scatter.2.cloned.1.call-start = ((), (), s32[]{:S(2)}) async-start(), calls=%async_computation.3 | async-start | bytes 2621440 | tf_op jit(solution)/shard_map/reduce_scatter | solution.py:24
  100.8 37.2 %copy-start.1 = (s32[64]{0:T(128)S(1)}, s32[64]{0:T(128)}, u32[]{:S(2)}) copy-start(s32[64]{0:T(128)} %param.7) | copy-start | bytes 772
  132.5 14.4 %all-to-all-start = ((bf16[8,16,1024]{2,1,0:T(8,128)(2,1)}), bf16[8,16,1024]{2,1,0:T(8,128)(2,1)S(1)}, u32[]{:S(2)}, u32[]{:S(2)}) async-start(bf16[8,16,1024]{2,1,0:T(8,128)(2,1)} %convert_element_type.3), calls=%async_computation.1 | async-start | bytes 524288 | tf_op jit(solution)/shard_map/all_to_all | solution.py:26
Sparse Core Ops, SparseCore 0:
  9.5 76.0 all-gather.1
  100.9 29.7 reduce-scatter.1
where the time goes:
time: 162 us; the launch traced here: 161 us
  waiting for transfers between devices  114 us (70%)
  local copies, waits for them, and re-layouts  22.5 us (14%)
  between operations  13.5 us (8%)
  starting transfers between devices  5.53 us (3%)
  other arithmetic  3.19 us (2%)
  matrix products  2.6 us (2%)
    all_gather x1, waiting for transfers between devices, body(): everything = lax.all_gather(amplitudes, 'col', axis=1, tiled=True)  75.3 us
    reduce_scatter x1, waiting for transfers between devices, body(): lax.psum_scatter(partial_value, 'row', scatter_dimension=1, tiled=True)  29.9 us
    all_to_all x1, waiting for transfers between devices, body(): lax.all_to_all(held_tiles, 'col', split_axis=0, concat_axis=0, tiled=True)  8.82 us
    gather x1, local copies, waits for them, and re-layouts, body(): received[source_dev[None, :], jnp.arange(per_device)[:, None], slot_ids[N...  6.71 us
    reshape x1, local copies, waits for them, and re-layouts, body(): everything = everything.reshape(pair_count, col_count * per_source, TILE)  6.46 us
    gather x3, local copies, waits for them, and re-layouts, body(): chosen = jnp.take(everything, own_list, axis=1)  6.09 us
    all_to_all x1, starting transfers between devices, body(): lax.all_to_all(held_tiles, 'col', split_axis=0, concat_axis=0, tiled=True)  5.49 us
  transfers between devices with their start and end apart: 3, of which 3 were waited for; matrix products, arithmetic and copies ran while one was open for 1% of the time, Pallas kernels for 0%

commit v1 on v0

v1 whole, which is shorter than its diff:
```python
import functools

import jax
import jax.numpy as jnp
from jax import lax
from jax.experimental import pallas as pl
from jax.experimental.pallas import tpu as pltpu
from jax.sharding import PartitionSpec as P

TILE = 128
CAP = 2
ANY = pl.BlockSpec(memory_space=pl.ANY)
SMEM = pl.BlockSpec(memory_space=pltpu.SMEM)
VMEM = pl.BlockSpec(memory_space=pltpu.VMEM)
LIMIT = 48 * 1024 * 1024


def halving_order(count):
    bits = count.bit_length() - 1
    return [int(format(count - 1 - j, "b").zfill(bits)[::-1], 2) for j in range(count)]


def select_kernel(per_source, wanted, amps, *rest):
    outs, sem = rest[:-1], rest[-1]
    me, row = lax.axis_index("col"), lax.axis_index("row")
    length = wanted.shape[2]
    copies = []
    for d in range(1, len(outs) + 1):
        other = me ^ d

        def step(k, found):
            first, second, count = found
            w = wanted[other, row, k]
            mine = w // per_source == me
            tile = w % per_source
            first = jnp.where(mine & (count == 0), tile, first)
            second = jnp.where(mine & (count == 1), tile, second)
            return first, second, count + mine.astype(jnp.int32)

        zero = jnp.int32(0)
        found = lax.fori_loop(0, length, step, (zero, zero, zero), unroll=length <= 8)
        for slot in range(CAP):
            start = pl.multiple_of(found[slot] * TILE, TILE)
            copy = pltpu.make_async_copy(amps.at[:, pl.ds(start, TILE)], outs[d - 1].at[slot], sem.at[d - 1, slot])
            copy.start()
            copies.append(copy)
    for copy in copies:
        copy.wait()


def select(wanted, amps, per_source, count):
    shape = jax.ShapeDtypeStruct((CAP, amps.shape[0], TILE), amps.dtype)
    return pl.pallas_call(
        functools.partial(select_kernel, per_source),
        out_shape=[shape] * count,
        in_specs=[SMEM, VMEM],
        out_specs=[ANY] * count,
        scratch_shapes=[pltpu.SemaphoreType.DMA((count, CAP))],
        compiler_params=pltpu.CompilerParams(vmem_limit_bytes=LIMIT),
        name="select_tiles",
    )(wanted, amps)


def contract_kernel(per_source, sources, wanted, own, *rest):
    received = rest[:sources - 1]
    block, send, keep, left, right, result, sem_left, sem_right, sem_out = rest[sources - 1:]
    me, row = lax.axis_index("col"), lax.axis_index("row")
    length = wanted.shape[2]
    parts = left.shape[0]
    order = halving_order(parts)
    load_block = pltpu.make_async_copy(block, right, sem_right)
    load_block.start()

    def fetch(k, carry):
        w = wanted[me, row, k]
        source = w // per_source
        slot = lax.fori_loop(0, k, lambda i, n: n + (wanted[me, row, i] // per_source == source).astype(jnp.int32), jnp.int32(0))
        away = source ^ me
        columns = pl.ds(pl.multiple_of(k * TILE, TILE), TILE)
        own_columns = pl.ds(pl.multiple_of((w % per_source) * TILE, TILE), TILE)

        @pl.when(away == 0)
        def _():
            for j in range(parts):
                pltpu.make_async_copy(own.at[:, row ^ order[j], :, own_columns], left.at[j, :, :, columns], sem_left).start()

        for d in range(1, sources):
            @pl.when(away == d)
            def _():
                for j in range(parts):
                    pltpu.make_async_copy(received[d - 1].at[slot, :, row ^ order[j]], left.at[j, :, :, columns], sem_left).start()
        return carry

    lax.fori_loop(0, length, fetch, 0)
    load_block.wait()
    pltpu.make_async_copy(left, left, sem_left).wait()
    half = parts // 2
    rows = result.shape[1]
    depth = left.shape[3]
    outs = []
    for h, target in ((0, send), (1, keep)):
        a = left[h * half:(h + 1) * half].reshape(rows, depth)
        result[h] = jnp.dot(a, right[...], preferred_element_type=jnp.float32)
        copy = pltpu.make_async_copy(result.at[h], target, sem_out.at[h])
        copy.start()
        outs.append(copy)
    for copy in outs:
        copy.wait()


def contract(wanted, own, received, block, per_source):
    a, parts, b, _ = own.shape
    depth, width = block.shape
    rows = a * parts * b // 2
    shape = jax.ShapeDtypeStruct((rows, width), jnp.float32)
    return pl.pallas_call(
        functools.partial(contract_kernel, per_source, len(received) + 1),
        out_shape=[shape, shape],
        in_specs=[SMEM] + [ANY] * (len(received) + 2),
        out_specs=[ANY, ANY],
        scratch_shapes=[
            pltpu.VMEM((parts, a, b, depth), own.dtype),
            pltpu.VMEM((depth, width), block.dtype),
            pltpu.VMEM((2, rows, width), jnp.float32),
            pltpu.SemaphoreType.DMA,
            pltpu.SemaphoreType.DMA,
            pltpu.SemaphoreType.DMA((2,)),
        ],
        compiler_params=pltpu.CompilerParams(vmem_limit_bytes=LIMIT),
        name="contract_tiles",
    )(wanted, own, *received, block)


def reorder_kernel(tiles_held, owner, received, out):
    for t in range(owner.shape[0]):
        at = owner[t]
        start = pl.multiple_of((at % tiles_held) * TILE, TILE)
        out[:, t * TILE:(t + 1) * TILE] = received[at // tiles_held, :, pl.ds(start, TILE)]


def reorder(owner, received):
    columns, rows, width = received.shape
    return pl.pallas_call(
        functools.partial(reorder_kernel, width // TILE),
        out_shape=jax.ShapeDtypeStruct((rows, columns * width), received.dtype),
        in_specs=[SMEM, VMEM],
        out_specs=VMEM,
        compiler_params=pltpu.CompilerParams(vmem_limit_bytes=LIMIT),
        name="reorder_tiles",
    )(owner, received)


def body(amplitudes, integrals, wanted, owner):
    columns = lax.axis_size("col")
    parts = lax.axis_size("row")
    pairs = amplitudes.shape[0]
    per_source = amplitudes.shape[1] // TILE
    per_device = pairs // (columns * parts)
    if per_device % 16 == 0:
        rows_view = (columns, parts, per_device)
    else:
        amplitudes = amplitudes.reshape(columns, parts, per_device, -1).transpose(1, 0, 2, 3).reshape(pairs, -1)
        rows_view = (1, parts, columns * per_device)
    parcels = select(wanted, amplitudes, per_source, columns - 1)
    received = []
    for d in range(1, columns):
        moved = lax.ppermute(parcels[d - 1], "col", [(c, c ^ d) for c in range(columns)])
        received.append(moved.reshape((CAP,) + rows_view + (TILE,)))
    send, keep = contract(wanted, amplitudes.reshape(rows_view + (-1,)), received, integrals, per_source)
    bit = 1
    while True:
        arrived = lax.ppermute(send, "row", [(r, r ^ bit) for r in range(parts)])
        bit *= 2
        if bit == parts:
            break
        half = keep.shape[0] // 2
        send = keep[:half] + arrived[:half]
        keep = keep[half:] + arrived[half:]
    held = (keep + arrived).astype(jnp.bfloat16)
    held = held.reshape(columns, per_device, -1)
    exchanged = lax.all_to_all(held, "col", split_axis=0, concat_axis=0, tiled=True)
    return reorder(owner, exchanged)


def solution(mesh):
    in_specs = (P(None, ("col", "row")), P("row", "col"), P(), P())
    out_specs = P(("col", "row"), None)
    return jax.shard_map(body, mesh=mesh, in_specs=in_specs, out_specs=out_specs, check_vma=False)
```

time: 162 us -> 92.2 us (0.57)
  waiting for transfers between devices: 114 us -> 45.5 us
  blocking collectives: 0 us -> 21.5 us
  local copies, waits for them, and re-layouts: 22.5 us -> 1.76 us
  between operations: 13.5 us -> 0.05 us
  starting transfers between devices: 5.53 us -> 15.4 us
  Pallas kernels: 0 us -> 7.46 us
  other arithmetic: 3.19 us -> 0.21 us
  matrix products: 2.6 us -> 0 us
    all_gather x1 -> x0, waiting for transfers between devices: 75.3 us -> none  [body(): everything = lax.all_gather(amplitudes, 'col', axis=1, tiled=True)]
    ppermute x0 -> x9, waiting for transfers between devices: none -> 45.5 us  [the longest x7 30.4 us: body(): lax.ppermute(parcels[d - 1], 'col', [(c, c ^ d) for c in range(columns)])]
    reduce_scatter x1 -> x0, waiting for transfers between devices: 29.9 us -> none  [body(): lax.psum_scatter(partial_value, 'row', scatter_dimension=1, tiled=True)]
    all_to_all x0 -> x1, blocking collectives: none -> 21.5 us  [body(): lax.all_to_all(held, 'col', split_axis=0, concat_axis=0, tiled=True)]
    ppermute x0 -> x9, starting transfers between devices: none -> 15.4 us  [the longest x7 13.8 us: body(): lax.ppermute(parcels[d - 1], 'col', [(c, c ^ d) for c in range(columns)])]
    gather x4 -> x0, local copies, waits for them, and re-layouts: 12.8 us -> none  [the longest x1 6.71 us: body(): received[source_dev[None, :], jnp.arange(per_device)[:, None], slot_ids[N...]
    all_to_all x1 -> x0, waiting for transfers between devices: 8.82 us -> none  [body(): lax.all_to_all(held_tiles, 'col', split_axis=0, concat_axis=0, tiled=True)]
    pallas_call x0 -> x3, Pallas kernels: none -> 7.46 us  [the longest x1 4 us: contract(): pl.pallas_call(functools.partial(contract_kernel, per_source, len(receive...]
  transfers between devices with their start and end apart: 3 -> 9, of which waited for: 3 -> 6; matrix products, arithmetic and copies ran while one was open for 1% -> 0% of each run, Pallas kernels for 0% -> 0%
where the time goes in v1:
time: 92.2 us; the launch traced here: 91.9 us
  waiting for transfers between devices  45.5 us (49%)
  blocking collectives  21.5 us (23%)
  starting transfers between devices  15.4 us (17%)
  Pallas kernels  7.46 us (8%)
  local copies, waits for them, and re-layouts  1.76 us (2%)
    ppermute x7, waiting for transfers between devices, body(): lax.ppermute(parcels[d - 1], 'col', [(c, c ^ d) for c in range(columns)])  30.4 us
    all_to_all x1, blocking collectives, body(): lax.all_to_all(held, 'col', split_axis=0, concat_axis=0, tiled=True)  21.5 us
    ppermute x2, waiting for transfers between devices, body(): arrived = lax.ppermute(send, 'row', [(r, r ^ bit) for r in range(parts)])  15.1 us
    ppermute x7, starting transfers between devices, body(): lax.ppermute(parcels[d - 1], 'col', [(c, c ^ d) for c in range(columns)])  13.8 us
    pallas_call x1, Pallas kernels, contract(): pl.pallas_call(functools.partial(contract_kernel, per_source, len(receive...  4 us
  transfers between devices with their start and end apart: 9, of which 6 were waited for; matrix products, arithmetic and copies ran while one was open for 0% of the time, Pallas kernels for 0%

profile of v1, /device:TPU:0, one launch (start us, length us, event | category | flops | bytes accessed | tf_op | source)
XLA Modules:
  0.0 91.9 jit_solution(1854910215684459664)
XLA Ops:
  0.0 1.0 %copy-done = bf16[512,512]{1,0:T(8,128)(2,1)S(1)} copy-done((bf16[512,512]{1,0:T(8,128)(2,1)S(1)}, bf16[512,512]{1,0:T(8,128)(2,1)}, u32[]{:S(2)}) %copy-start) | copy-done | bytes 524312
  1.0 0.7 copy-done.1
  1.8 1.8 %select_tiles.1 = (bf16[2,512,128]{2,1,0:T(8,128)(2,1)S(1)}, bf16[2,512,128]{2,1,0:T(8,128)(2,1)S(1)}, bf16[2,512,128]{2,1,0:T(8,128)(2,1)S(1)}, bf16[2,512,128]...) custom-call(s32[8,4,8]{2,1,0:T(4,128)S(1)} %copy-done.1, ...), custom_call_target="tpu_custom_call" | custom-call | tf_op jit(solution)/shard_map/select_tiles/pallas_call | solution.py:53
  3.5 3.0 %collective-permute-start = (bf16[2,512,128]{2,1,0:T(8,128)(2,1)S(1)}, bf16[2,512,128]{2,1,0:T(8,128)(2,1)S(1)}, u32[]{:S(2)}, u32[]{:S(2)}) collective-permute-start(bf16[2,512,128]{2,1,0:T(8,128)(2,1)S(1)} %get-tuple-element.14), channel_id=1, source_target_pairs={{0,4},{4,0},{8,12},{12,8},{16,20},{20,16},{24,28},{28,24},{1,5},{5... | collective-permute-start | bytes 786440 | tf_op jit(solution)/shard_map/ppermute | solution.py:167
  6.5 1.6 %collective-permute-start.1 = (bf16[2,512,128]{2,1,0:T(8,128)(2,1)S(1)}, bf16[2,512,128]{2,1,0:T(8,128)(2,1)S(1)}, u32[]{:S(2)}, u32[]{:S(2)}) collective-permute-start(bf16[2,512,128]{2,1,0:T(8,128)(2,1)S(1)} %get-tuple-element.15), channel_id=1, source_target_pairs={{0,8},{4,12},{8,0},{12,4},{16,24},{20,28},{24,16},{28,20},{1,9},{5... | collective-permute-start | bytes 786440 | tf_op jit(solution)/shard_map/ppermute | solution.py:167
  8.1 0.0 collective-permute-start.2
  8.1 3.0 %collective-permute-start.3 = (bf16[2,512,128]{2,1,0:T(8,128)(2,1)S(1)}, bf16[2,512,128]{2,1,0:T(8,128)(2,1)S(1)}, u32[]{:S(2)}, u32[]{:S(2)}) collective-permute-start(bf16[2,512,128]{2,1,0:T(8,128)(2,1)S(1)} %get-tuple-element.17), channel_id=1, source_target_pairs={{0,16},{4,20},{8,24},{12,28},{16,0},{20,4},{24,8},{28,12},{1,17},{... | collective-permute-start | bytes 786440 | tf_op jit(solution)/shard_map/ppermute | solution.py:167
  11.1 1.3 %collective-permute-start.4 = (bf16[2,512,128]{2,1,0:T(8,128)(2,1)S(1)}, bf16[2,512,128]{2,1,0:T(8,128)(2,1)S(1)}, u32[]{:S(2)}, u32[]{:S(2)}) collective-permute-start(bf16[2,512,128]{2,1,0:T(8,128)(2,1)S(1)} %get-tuple-element.18), channel_id=1, source_target_pairs={{0,20},{4,16},{8,28},{12,24},{16,4},{20,0},{24,12},{28,8},{1,21},{... | collective-permute-start | bytes 786440 | tf_op jit(solution)/shard_map/ppermute | solution.py:167
  12.4 0.5 collective-permute-done
  12.9 3.9 %collective-permute-start.5 = (bf16[2,512,128]{2,1,0:T(8,128)(2,1)S(1)}, bf16[2,512,128]{2,1,0:T(8,128)(2,1)S(1)}, u32[]{:S(2)}, u32[]{:S(2)}) collective-permute-start(bf16[2,512,128]{2,1,0:T(8,128)(2,1)S(1)} %get-tuple-element.19), channel_id=1, source_target_pairs={{0,24},{4,28},{8,16},{12,20},{16,8},{20,12},{24,0},{28,4},{1,25},{... | collective-permute-start | bytes 786440 | tf_op jit(solution)/shard_map/ppermute | solution.py:167
  16.7 9.3 %collective-permute-done.1 = bf16[2,512,128]{2,1,0:T(8,128)(2,1)S(1)} collective-permute-done((bf16[2,512,128]{2,1,0:T(8,128)(2,1)S(1)}, bf16[2,512,128]{2,1,0:T(8,128)(2,1)S(1)}, u32[]{:S(2)}, u32[]{:S(2)}) %collective-permute-start.1) | collective-permute-done | bytes 262176 | tf_op jit(solution)/shard_map/ppermute | solution.py:167
  26.1 1.1 %collective-permute-start.6 = (bf16[2,512,128]{2,1,0:T(8,128)(2,1)S(1)}, bf16[2,512,128]{2,1,0:T(8,128)(2,1)S(1)}, u32[]{:S(2)}, u32[]{:S(2)}) collective-permute-start(bf16[2,512,128]{2,1,0:T(8,128)(2,1)S(1)} %get-tuple-element.20), channel_id=1, source_target_pairs={{0,28},{4,24},{8,20},{12,16},{16,12},{20,8},{24,4},{28,0},{1,29},{... | collective-permute-start | bytes 786440 | tf_op jit(solution)/shard_map/ppermute | solution.py:167
  27.1 2.2 %collective-permute-done.2 = bf16[2,512,128]{2,1,0:T(8,128)(2,1)S(1)} collective-permute-done((bf16[2,512,128]{2,1,0:T(8,128)(2,1)S(1)}, bf16[2,512,128]{2,1,0:T(8,128)(2,1)S(1)}, u32[]{:S(2)}, u32[]{:S(2)}) %collective-permute-start.2) | collective-permute-done | bytes 262176 | tf_op jit(solution)/shard_map/ppermute | solution.py:167
  29.4 18.3 %collective-permute-done.4 = bf16[2,512,128]{2,1,0:T(8,128)(2,1)S(1)} collective-permute-done((bf16[2,512,128]{2,1,0:T(8,128)(2,1)S(1)}, bf16[2,512,128]{2,1,0:T(8,128)(2,1)S(1)}, u32[]{:S(2)}, u32[]{:S(2)}) %collective-permute-start.4) | collective-permute-done | bytes 262176 | tf_op jit(solution)/shard_map/ppermute | solution.py:167
  47.7 4.0 %contract_tiles.1 = (f32[256,1024]{1,0:T(8,128)S(1)}, f32[256,1024]{1,0:T(8,128)S(1)}) custom-call(s32[8,4,8]{2,1,0:T(4,128)S(1)} %copy-done.1, bf16[8,4,16,512]{3,2,1,0:T(8,128)(2,1)S(1)} %bitcast.9, bf16[2,8,4,16,128]{4,3,2,1,0:T(8,128)(2,1)S(1)} %bitcast.10, bf16[2,8,4,16,128]{4,3,2,1,0:T(8,128)(2,1)S(1)} %bitcast.11, ...), custom_call_target="tpu_custom_call" | custom-call | tf_op jit(solution)/shard_map/contract_tiles/pallas_call | solution.py:116
  51.7 0.0 copy-start.2
  51.7 0.1 collective-permute-start.7
  51.8 2.6 %collective-permute-done.7 = f32[256,1024]{1,0:T(8,128)S(1)} collective-permute-done((f32[256,1024]{1,0:T(8,128)S(1)}, f32[256,1024]{1,0:T(8,128)S(1)}, u32[]{:S(2)}, u32[]{:S(2)}) %collective-permute-start.7) | collective-permute-done | bytes 1048608 | tf_op jit(solution)/shard_map/ppermute | solution.py:172
  54.5 0.1 slice_add_fusion
  54.5 1.6 %collective-permute-start.8 = (f32[128,1024]{1,0:T(8,128)S(1)}, f32[128,1024]{1,0:T(8,128)S(1)}, u32[]{:S(2)}, u32[]{:S(2)}) collective-permute-start(f32[128,1024]{1,0:T(8,128)S(1)} %slice_add_fusion), channel_id=1, source_target_pairs={{0,2},{1,3},{2,0},{3,1},{4,6},{5,7},{6,4},{7,5},{8,10},{9,11},{10,... | collective-permute-start | bytes 1572872 | tf_op jit(solution)/shard_map/ppermute | solution.py:172
  56.1 12.4 %collective-permute-done.8 = f32[128,1024]{1,0:T(8,128)S(1)} collective-permute-done((f32[128,1024]{1,0:T(8,128)S(1)}, f32[128,1024]{1,0:T(8,128)S(1)}, u32[]{:S(2)}, u32[]{:S(2)}) %collective-permute-start.8) | collective-permute-done | bytes 524320 | tf_op jit(solution)/shard_map/ppermute | solution.py:172
  68.6 0.1 fusion.1
  68.7 21.5 %all_to_all.5.received = bf16[8,16,1024]{2,1,0:T(8,128)(2,1)S(1)} all-to-all(bf16[8,16,1024]{2,1,0:T(8,128)(2,1)S(1)} %bitcast.17), channel_id=1, replica_groups=mesh['col'=8,'row'=4] {'col'}, dimensions={0} | all-to-all | bytes 524288 | tf_op jit(solution)/shard_map/all_to_all | solution.py:181
  90.2 1.7 %reorder_tiles.1 = bf16[16,8192]{1,0:T(8,128)(2,1)} custom-call(s32[64]{0:T(128)S(1)} %copy-done.2, bf16[8,16,1024]{2,1,0:T(8,128)(2,1)S(1)} %all_to_all.5.received), custom_call_target="tpu_custom_call" | custom-call | tf_op jit(solution)/shard_map/reorder_tiles/pallas_call | solution.py:143
  (6 shorter events, 0.0 us)
Async XLA Ops:
  0.0 1.0 %copy-start = (bf16[512,512]{1,0:T(8,128)(2,1)S(1)}, bf16[512,512]{1,0:T(8,128)(2,1)}, u32[]{:S(2)}) copy-start(bf16[512,512]{1,0:T(8,128)(2,1)} %amps.1) | copy-start | bytes 1572868
  1.0 0.7 copy-start.1
  3.5 9.3 %collective-permute-start = (bf16[2,512,128]{2,1,0:T(8,128)(2,1)S(1)}, bf16[2,512,128]{2,1,0:T(8,128)(2,1)S(1)}, u32[]{:S(2)}, u32[]{:S(2)}) collective-permute-start(bf16[2,512,128]{2,1,0:T(8,128)(2,1)S(1)} %get-tuple-element.14), channel_id=1, source_target_pairs={{0,4},{4,0},{8,12},{12,8},{16,20},{20,16},{24,28},{28,24},{1,5},{5... | collective-permute-start | bytes 786440 | tf_op jit(solution)/shard_map/ppermute | solution.py:167
  6.5 19.5 %collective-permute-start.1 = (bf16[2,512,128]{2,1,0:T(8,128)(2,1)S(1)}, bf16[2,512,128]{2,1,0:T(8,128)(2,1)S(1)}, u32[]{:S(2)}, u32[]{:S(2)}) collective-permute-start(bf16[2,512,128]{2,1,0:T(8,128)(2,1)S(1)} %get-tuple-element.15), channel_id=1, source_target_pairs={{0,8},{4,12},{8,0},{12,4},{16,24},{20,28},{24,16},{28,20},{1,9},{5... | collective-permute-start | bytes 786440 | tf_op jit(solution)/shard_map/ppermute | solution.py:167
  8.1 21.2 %collective-permute-start.2 = (bf16[2,512,128]{2,1,0:T(8,128)(2,1)S(1)}, bf16[2,512,128]{2,1,0:T(8,128)(2,1)S(1)}, u32[]{:S(2)}, u32[]{:S(2)}) collective-permute-start(bf16[2,512,128]{2,1,0:T(8,128)(2,1)S(1)} %get-tuple-element.16), channel_id=1, source_target_pairs={{0,12},{4,8},{8,4},{12,0},{16,28},{20,24},{24,20},{28,16},{1,13},{... | collective-permute-start | bytes 786440 | tf_op jit(solution)/shard_map/ppermute | solution.py:167
  8.1 21.2 %collective-permute-start.3 = (bf16[2,512,128]{2,1,0:T(8,128)(2,1)S(1)}, bf16[2,512,128]{2,1,0:T(8,128)(2,1)S(1)}, u32[]{:S(2)}, u32[]{:S(2)}) collective-permute-start(bf16[2,512,128]{2,1,0:T(8,128)(2,1)S(1)} %get-tuple-element.17), channel_id=1, source_target_pairs={{0,16},{4,20},{8,24},{12,28},{16,0},{20,4},{24,8},{28,12},{1,17},{... | collective-permute-start | bytes 786440 | tf_op jit(solution)/shard_map/ppermute | solution.py:167
  11.1 36.6 %collective-permute-start.4 = (bf16[2,512,128]{2,1,0:T(8,128)(2,1)S(1)}, bf16[2,512,128]{2,1,0:T(8,128)(2,1)S(1)}, u32[]{:S(2)}, u32[]{:S(2)}) collective-permute-start(bf16[2,512,128]{2,1,0:T(8,128)(2,1)S(1)} %get-tuple-element.18), channel_id=1, source_target_pairs={{0,20},{4,16},{8,28},{12,24},{16,4},{20,0},{24,12},{28,8},{1,21},{... | collective-permute-start | bytes 786440 | tf_op jit(solution)/shard_map/ppermute | solution.py:167
  12.9 34.9 %collective-permute-start.5 = (bf16[2,512,128]{2,1,0:T(8,128)(2,1)S(1)}, bf16[2,512,128]{2,1,0:T(8,128)(2,1)S(1)}, u32[]{:S(2)}, u32[]{:S(2)}) collective-permute-start(bf16[2,512,128]{2,1,0:T(8,128)(2,1)S(1)} %get-tuple-element.19), channel_id=1, source_target_pairs={{0,24},{4,28},{8,16},{12,20},{16,8},{20,12},{24,0},{28,4},{1,25},{... | collective-permute-start | bytes 786440 | tf_op jit(solution)/shard_map/ppermute | solution.py:167
  26.1 21.7 %collective-permute-start.6 = (bf16[2,512,128]{2,1,0:T(8,128)(2,1)S(1)}, bf16[2,512,128]{2,1,0:T(8,128)(2,1)S(1)}, u32[]{:S(2)}, u32[]{:S(2)}) collective-permute-start(bf16[2,512,128]{2,1,0:T(8,128)(2,1)S(1)} %get-tuple-element.20), channel_id=1, source_target_pairs={{0,28},{4,24},{8,20},{12,16},{16,12},{20,8},{24,4},{28,0},{1,29},{... | collective-permute-start | bytes 786440 | tf_op jit(solution)/shard_map/ppermute | solution.py:167
  51.7 38.5 %copy-start.2 = (s32[64]{0:T(128)S(1)}, s32[64]{0:T(128)}, u32[]{:S(2)}) copy-start(s32[64]{0:T(128)} %owner.1) | copy-start | bytes 772
  51.7 2.7 %collective-permute-start.7 = (f32[256,1024]{1,0:T(8,128)S(1)}, f32[256,1024]{1,0:T(8,128)S(1)}, u32[]{:S(2)}, u32[]{:S(2)}) collective-permute-start(f32[256,1024]{1,0:T(8,128)S(1)} %get-tuple-element.22), channel_id=1, source_target_pairs={{0,1},{1,0},{2,3},{3,2},{4,5},{5,4},{6,7},{7,6},{8,9},{9,8},{10,11... | collective-permute-start | bytes 3145736 | tf_op jit(solution)/shard_map/ppermute | solution.py:172
  54.5 14.0 %collective-permute-start.8 = (f32[128,1024]{1,0:T(8,128)S(1)}, f32[128,1024]{1,0:T(8,128)S(1)}, u32[]{:S(2)}, u32[]{:S(2)}) collective-permute-start(f32[128,1024]{1,0:T(8,128)S(1)} %slice_add_fusion), channel_id=1, source_target_pairs={{0,2},{1,3},{2,0},{3,1},{4,6},{5,7},{6,4},{7,5},{8,10},{9,11},{10,... | collective-permute-start | bytes 1572872 | tf_op jit(solution)/shard_map/ppermute | solution.py:172

commit v2 on v0

v2 whole, which is shorter than its diff:
```python
import functools

import jax
import jax.numpy as jnp
from jax import lax
from jax.experimental import pallas as pl
from jax.experimental.pallas import tpu as pltpu
from jax.sharding import PartitionSpec as P

TILE = 128
CAP = 2
CORES = 2
SMALL = 8 * 1024 * 1024
LEAST = 2.0 ** -125
STEPS = 32766.0
ANY = pl.BlockSpec(memory_space=pl.ANY)
SMEM = pl.BlockSpec(memory_space=pltpu.SMEM)
VMEM = pl.BlockSpec(memory_space=pltpu.VMEM)


def params(size=0):
    return pltpu.CompilerParams(vmem_limit_bytes=size + SMALL)


def halving_order(count):
    bits = count.bit_length() - 1
    return [int(format(count - 1 - j, "b").zfill(bits)[::-1], 2) for j in range(count)] if bits else [0]


def split_kernel(amps, mine, theirs, sem):
    core = lax.axis_index("row") % CORES
    copies = [
        pltpu.make_async_copy(amps.at[:, :, core], mine, sem.at[0]),
        pltpu.make_async_copy(amps.at[:, :, 1 - core], theirs, sem.at[1]),
    ]
    for copy in copies:
        copy.start()
    for copy in copies:
        copy.wait()


def split(amps):
    shape = jax.ShapeDtypeStruct(amps.shape[:2] + amps.shape[3:], amps.dtype)
    return pl.pallas_call(
        split_kernel,
        out_shape=[shape, shape],
        in_specs=[ANY],
        out_specs=[ANY, ANY],
        scratch_shapes=[pltpu.SemaphoreType.DMA((2,))],
        compiler_params=params(),
        name="split_rows",
    )(amps)


def select_kernel(per_source, away, flips, wanted, *rest):
    groups, outs, sem = rest[:CORES], rest[CORES:-1], rest[-1]
    me, row = lax.axis_index("col"), lax.axis_index("row")
    length = wanted.shape[2]
    source = me ^ away
    copies = []
    for n, flip in enumerate(flips):
        other = me ^ flip
        for g in range(CORES):

            def step(k, found):
                first, second, count = found
                w = wanted[other, row ^ g, k]
                mine = w // per_source == source
                tile = w % per_source
                first = jnp.where(mine & (count == 0), tile, first)
                second = jnp.where(mine & (count == 1), tile, second)
                return first, second, count + mine.astype(jnp.int32)

            zero = jnp.int32(0)
            found = lax.fori_loop(0, length, step, (zero, zero, zero), unroll=length <= 8)
            for slot in range(CAP):
                start = pl.multiple_of(found[slot] * TILE, TILE)
                copy = pltpu.make_async_copy(groups[g].at[:, pl.ds(start, TILE)], outs[n].at[g, slot], sem.at[n, g, slot])
                copy.start()
                copies.append(copy)
    for copy in copies:
        copy.wait()


def select(wanted, groups, per_source, away, flips):
    rows = groups[0].shape[0]
    shape = jax.ShapeDtypeStruct((CORES, CAP, rows, TILE), groups[0].dtype)
    return pl.pallas_call(
        functools.partial(select_kernel, per_source, away, flips),
        out_shape=[shape] * len(flips),
        in_specs=[SMEM] + [ANY] * CORES,
        out_specs=[ANY] * len(flips),
        scratch_shapes=[pltpu.SemaphoreType.DMA((len(flips), CORES, CAP))],
        compiler_params=params(),
        name="select_tiles",
    )(wanted, *groups)


def arrange_kernel(per_source, top, wanted, *refs):
    blocks, (early, far) = refs[:CORES], refs[CORES:]
    me, row = lax.axis_index("col"), lax.axis_index("row")
    length = wanted.shape[2]
    for part in (early, far):
        part[...] = jnp.zeros_like(part)
    near_base = CORES * per_source
    whole_base = near_base + CORES * CAP * (top - 1)
    for g in range(CORES):

        def place(k, carry):
            w = wanted[me, row ^ g, k]
            source = w // per_source
            slot = lax.fori_loop(0, k, lambda i, n: n + (wanted[me, row ^ g, i] // per_source == source).astype(jnp.int32), jnp.int32(0))
            away, tile = source ^ me, w % per_source
            passed = CAP * (CORES * (lax.rem(away, top) - 1) + g) + slot
            rows = blocks[g][pl.ds(pl.multiple_of(k * TILE, TILE), TILE)]

            def put(part, condition, at):
                @pl.when(condition)
                def _():
                    part[pl.ds(pl.multiple_of(at * TILE, TILE), TILE)] = rows

            put(early, away == 0, g * per_source + tile)
            put(early, (away > 0) & (away < top), near_base + passed)
            put(early, away == top, whole_base + g * per_source + tile)
            put(far, away > top, passed)
            return carry

        lax.fori_loop(0, length, place, 0)


def arrange(wanted, blocks, per_source, top):
    depth, width = blocks[0].shape
    passed = CORES * CAP * (top - 1)
    depths = [TILE * n for n in (2 * CORES * per_source + passed, passed)]
    part = width if depth <= 1024 else width // 4
    size = 4 * part * (CORES * depth + sum(depths))
    return pl.pallas_call(
        functools.partial(arrange_kernel, per_source, top),
        grid=(width // part,),
        out_shape=[jax.ShapeDtypeStruct((n, width), blocks[0].dtype) for n in depths],
        in_specs=[SMEM] + [pl.BlockSpec((depth, part), lambda n: (0, n))] * CORES,
        out_specs=[pl.BlockSpec((n, part), lambda n: (0, n)) for n in depths],
        compiler_params=params(size),
        name="arrange_block",
    )(wanted, *blocks)


def code(x):
    most = jnp.max(jnp.abs(x), axis=1, keepdims=True)
    power = jnp.clip(jnp.ceil(jnp.log2(jnp.maximum(most, LEAST))), -125.0, 120.0)
    scaled = jnp.floor(x * jnp.exp2(-power) * STEPS + 0.5)
    scaled = jnp.clip(scaled, -32767.0, 32767.0).astype(jnp.int32).astype(jnp.int16)
    powers = jnp.broadcast_to(power, (x.shape[0], TILE)).astype(jnp.int32).astype(jnp.int16)
    return scaled, powers


def decode(coded):
    width = coded.shape[1] - TILE
    power = coded[:, width:].astype(jnp.int32).astype(jnp.float32)[:, :1]
    return coded[:, :width].astype(jnp.int32).astype(jnp.float32) * (1 / STEPS) * jnp.exp2(power)


def steps(rows):
    size = 64 if rows % 64 == 0 else 32 if rows % 32 == 0 else 16
    return [slice(start, start + size) for start in range(0, rows, size)]


def put_coded(out, at, x):
    width = x.shape[1]
    out[at, :width], out[at, width:] = code(x)


def fill(left, source, flip, depth, at):
    y = (lax.axis_index("row") // CORES) ^ flip
    rows = pl.ds(at, source.shape[-4] * source.shape[-2])
    if len(source.shape) == 4:
        tiles = [source[:, y]]
    else:
        tiles = [source[g, slot, :, y] for g in range(CORES) for slot in range(CAP)]
    for tile in tiles:
        width = tile.shape[-1]
        left[rows, depth:depth + width] = tile.reshape(-1, width)
        depth += width
    return depth


def contract_kernel(count, slots, coded, *refs):
    sources, block = refs[:count], refs[count]
    before, outs, left = refs[count + 1:-1 - len(slots)], refs[-1 - len(slots):-1], refs[-1]
    for n, flips in enumerate(slots):
        for j, flip in enumerate(flips):
            depth = 0
            for source in sources:
                depth = fill(left, source, flip, depth, j * (left.shape[0] // len(flips)))
        x = jnp.dot(left[...], block[...], preferred_element_type=jnp.float32)
        if before:
            x = before[n][...] + x
        if coded:
            put_coded(outs[n], slice(None), x)
        else:
            outs[n][...] = x


def contract(sources, block, slots, before=(), coded=False):
    depth, width = block.shape
    rows = sources[0].shape[-4] * sources[0].shape[-2] * len(slots[0])
    if coded:
        shape = jax.ShapeDtypeStruct((rows, width + TILE), jnp.int16)
    else:
        shape = jax.ShapeDtypeStruct((rows, width), jnp.float32)
    size = 2 * depth * (width + rows) + 12 * width * rows * len(slots) + sum(2 * x.size for x in sources)
    return pl.pallas_call(
        functools.partial(contract_kernel, len(sources), slots, coded),
        out_shape=[shape] * len(slots),
        in_specs=[VMEM] * (len(sources) + 1 + len(before)),
        out_specs=[VMEM] * len(slots),
        scratch_shapes=[pltpu.VMEM((rows, depth), block.dtype)],
        compiler_params=params(size),
        name="contract_tiles",
    )(*sources, block, *before)


def fold_kernel(keep, arrived, send, kept):
    half = kept.shape[0]
    for at in steps(half):
        put_coded(send, at, keep[at] + decode(arrived[at]))
    for at in steps(half):
        low = slice(at.start + half, at.stop + half)
        kept[at] = keep[low] + decode(arrived[low])


def fold(keep, arrived):
    half, width = keep.shape[0] // 2, keep.shape[1]
    return pl.pallas_call(
        fold_kernel,
        out_shape=[jax.ShapeDtypeStruct((half, width + TILE), jnp.int16), jax.ShapeDtypeStruct((half, width), jnp.float32)],
        in_specs=[VMEM, VMEM],
        out_specs=[VMEM, VMEM],
        compiler_params=params(),
        name="fold_rows",
    )(keep, arrived)


def finish_kernel(keep, arrived, out):
    for at in steps(keep.shape[0]):
        out[at] = (keep[at] + decode(arrived[at])).astype(out.dtype)


def finish(keep, arrived):
    return pl.pallas_call(
        finish_kernel,
        out_shape=jax.ShapeDtypeStruct(keep.shape, jnp.bfloat16),
        in_specs=[VMEM, VMEM],
        out_specs=VMEM,
        compiler_params=params(),
        name="finish_rows",
    )(keep, arrived)


def reorder_kernel(tiles_held, owner, received, out):
    for t in range(owner.shape[0]):
        at = owner[t]
        start = pl.multiple_of((at % tiles_held) * TILE, TILE)
        out[:, t * TILE:(t + 1) * TILE] = received[at // tiles_held, :, pl.ds(start, TILE)]


def reorder(owner, received):
    columns, rows, width = received.shape
    return pl.pallas_call(
        functools.partial(reorder_kernel, width // TILE),
        out_shape=jax.ShapeDtypeStruct((rows, columns * width), received.dtype),
        in_specs=[SMEM, VMEM],
        out_specs=VMEM,
        compiler_params=params(),
        name="reorder_tiles",
    )(owner, received)


def swap(x, axis, flip):
    return lax.ppermute(x, axis, [(i, i ^ flip) for i in range(lax.axis_size(axis))])


def body(amplitudes, integrals, wanted, owner):
    columns = lax.axis_size("col")
    parts = lax.axis_size("row")
    ys = parts // CORES
    pairs = amplitudes.shape[0]
    per_source = amplitudes.shape[1] // TILE
    per_device = pairs // (columns * parts)
    top = columns // 2
    low = list(range(1, top))
    b = max(per_device, 16)
    units = pairs // (parts * b)
    if b != per_device:
        amplitudes = amplitudes.reshape(units, columns // units, parts, per_device, -1).transpose(0, 2, 1, 3, 4)
    order = halving_order(ys)
    slots = [order[:ys // 2], order[ys // 2:]]

    def whole(x):
        return x.reshape(units, ys, b, -1)

    def near(groups, away):
        picked = select(wanted, [x.reshape(units * ys * b, -1) for x in groups], per_source, away, low)
        return [swap(x, "col", f).reshape(CORES, CAP, units, ys, b, TILE) for x, f in zip(picked, low)]

    mine, theirs = split(amplitudes.reshape(units, ys, CORES, b, -1))
    own = [mine, swap(theirs, "row", 1)]
    mirrors = [whole(swap(x, "col", top)) for x in own]
    nearby = near(own, 0)
    blocks = arrange(wanted, [integrals, swap(integrals, "row", 1)], per_source, top)
    *mirrors, early_block, far_block = lax.optimization_barrier((*mirrors, *blocks))
    far = near(mirrors, top)
    sums = contract(own + nearby + mirrors, early_block, slots)
    send, = contract(far, far_block, slots[:1], sums[:1], coded=True)
    keep, = contract(far, far_block, slots[1:], sums[1:])
    bit = CORES
    while True:
        arrived = swap(send, "row", bit)
        bit *= 2
        if bit == parts:
            break
        send, keep = fold(keep, arrived)
    held = finish(keep, arrived).reshape(columns, per_device, -1)
    exchanged = lax.all_to_all(held, "col", split_axis=0, concat_axis=0, tiled=True)
    return reorder(owner, exchanged)


def solution(mesh):
    in_specs = (P(None, ("col", "row")), P("row", "col"), P(), P())
    out_specs = P(("col", "row"), None)
    return jax.shard_map(body, mesh=mesh, in_specs=in_specs, out_specs=out_specs, check_vma=False)
```

time: 162 us -> 70.3 us (0.43)
  waiting for transfers between devices: 114 us -> 25.4 us
  local copies, waits for them, and re-layouts: 22.5 us -> 4.07 us
  between operations: 13.5 us -> 0.08 us
  blocking collectives: 0 us -> 12.5 us
  Pallas kernels: 0 us -> 11.7 us
  starting transfers between devices: 5.53 us -> 16.1 us
  other arithmetic: 3.19 us -> 0 us
  matrix products: 2.6 us -> 0 us
    all_gather x1 -> x0, waiting for transfers between devices: 75.3 us -> none  [body(): everything = lax.all_gather(amplitudes, 'col', axis=1, tiled=True)]
    reduce_scatter x1 -> x0, waiting for transfers between devices: 29.9 us -> none  [body(): lax.psum_scatter(partial_value, 'row', scatter_dimension=1, tiled=True)]
    ppermute x0 -> x11, waiting for transfers between devices: none -> 25.4 us  [swap(): lax.ppermute(x, axis, [(i, i ^ flip) for i in range(lax.axis_size(axis))])]
    ppermute x0 -> x11, starting transfers between devices: none -> 16.1 us  [swap(): lax.ppermute(x, axis, [(i, i ^ flip) for i in range(lax.axis_size(axis))])]
    gather x4 -> x0, local copies, waits for them, and re-layouts: 12.8 us -> none  [the longest x1 6.71 us: body(): received[source_dev[None, :], jnp.arange(per_device)[:, None], slot_ids[N...]
    all_to_all x0 -> x1, blocking collectives: none -> 12.5 us  [body(): lax.all_to_all(held, 'col', split_axis=0, concat_axis=0, tiled=True)]
    pallas_call x0 -> x9, Pallas kernels: none -> 11.7 us  [the longest x3 3.52 us: contract(): pl.pallas_call(functools.partial(contract_kernel, len(sources), slots, co...]
    all_to_all x1 -> x0, waiting for transfers between devices: 8.82 us -> none  [body(): lax.all_to_all(held_tiles, 'col', split_axis=0, concat_axis=0, tiled=True)]
  transfers between devices with their start and end apart: 3 -> 11, of which waited for: 3 -> 6; matrix products, arithmetic and copies ran while one was open for 1% -> 0% of each run, Pallas kernels for 0% -> 13%
where the time goes in v2:
time: 70.3 us; the launch traced here: 70 us
  waiting for transfers between devices  25.4 us (36%)
  starting transfers between devices  16.1 us (23%)
  blocking collectives  12.5 us (18%)
  Pallas kernels  11.7 us (17%)
  local copies, waits for them, and re-layouts  4.07 us (6%)
    ppermute x11, waiting for transfers between devices, swap(): lax.ppermute(x, axis, [(i, i ^ flip) for i in range(lax.axis_size(axis))])  25.4 us
    ppermute x11, starting transfers between devices, swap(): lax.ppermute(x, axis, [(i, i ^ flip) for i in range(lax.axis_size(axis))])  16.1 us
    all_to_all x1, blocking collectives, body(): lax.all_to_all(held, 'col', split_axis=0, concat_axis=0, tiled=True)  12.5 us
    unnamed x10, local copies, waits for them, and re-layouts  4.07 us
    pallas_call x3, Pallas kernels, contract(): pl.pallas_call(functools.partial(contract_kernel, len(sources), slots, co...  3.52 us
    pallas_call x1, Pallas kernels, arrange(): pl.pallas_call(functools.partial(arrange_kernel, per_source, top), grid=(...  3.33 us
    pallas_call x2, Pallas kernels, select(): pl.pallas_call(functools.partial(select_kernel, per_source, away, flips),...  2.99 us
    pallas_call x1, Pallas kernels, reorder(): pl.pallas_call(functools.partial(reorder_kernel, width // TILE), out_shap...  1.68 us
  transfers between devices with their start and end apart: 11, of which 6 were waited for; matrix products, arithmetic and copies ran while one was open for 0% of the time, Pallas kernels for 13%

profile of v2, /device:TPU:0, one launch (start us, length us, event | category | flops | bytes accessed | tf_op | source)
XLA Modules:
  0.0 70.0 jit_solution(13407595159142630728)
XLA Ops:
  0.5 1.0 %copy-done.1 = bf16[512,512]{1,0:T(8,128)(2,1)S(1)} copy-done((bf16[512,512]{1,0:T(8,128)(2,1)S(1)}, bf16[512,512]{1,0:T(8,128)(2,1)}, u32[]{:S(2)}) %copy-start.1) | copy-done | bytes 524312
  1.7 4.0 %collective-permute-start = (bf16[8,2,16,512]{3,2,1,0:T(8,128)(2,1)S(1)}, bf16[8,2,16,512]{3,2,1,0:T(8,128)(2,1)S(1)}, u32[]{:S(2)}, u32[]{:S(2)}) collective-permute-start(bf16[8,2,16,512]{3,2,1,0:T(8,128)(2,1)S(1)} %get-tuple-element.21.refs_0_), channel_id=1, source_target_pairs={{0,16},{4,20},{8,24},{12,28},{16,0},{20,4},{24,8},{28,12},{1,17},{... | collective-permute-start | bytes 786440 | tf_op jit(solution)/shard_map/ppermute | solution.py:280
  5.7 2.8 %collective-permute-start.2 = (bf16[8,2,16,512]{3,2,1,0:T(8,128)(2,1)S(1)}, bf16[8,2,16,512]{3,2,1,0:T(8,128)(2,1)S(1)}, u32[]{:S(2)}, u32[]{:S(2)}) collective-permute-start(bf16[8,2,16,512]{3,2,1,0:T(8,128)(2,1)S(1)} %collective-permute-done.1.refs_1_), channel_id=1, source_target_pairs={{0,16},{4,20},{8,24},{12,28},{16,0},{20,4},{24,8},{28,12},{1,17},{... | collective-permute-start | bytes 786440 | tf_op jit(solution)/shard_map/ppermute | solution.py:280
  8.6 0.7 %copy-done.2 = s32[8,4,8]{2,1,0:T(4,128)S(1)} copy-done((s32[8,4,8]{2,1,0:T(4,128)S(1)}, s32[8,4,8]{2,1,0:T(4,128)}, u32[]{:S(2)}) %copy-start.2) | copy-done | bytes 1048
  9.3 1.5 %select_tiles.3 = (bf16[2,2,256,128]{3,2,1,0:T(8,128)(2,1)S(1)}, bf16[2,2,256,128]{3,2,1,0:T(8,128)(2,1)S(1)}, bf16[2,2,256,128]{3,2,1,0:T(8,128)(2,1)S(1)}) custom-call(s32[8,4,8]{2,1,0:T(4,128)S(1)} %copy-done.2, bf16[256,512]{1,0:T(8,128)(2,1)S(1)} %bitcast.18, bf16[256,512]{1,0:T(8,128)(2,1)S(1)} %bitcast.19), custom_call_target="tpu_custom_call" | custom-call | tf_op jit(solution)/shard_map/select_tiles/pallas_call | solution.py:88
  10.8 2.6 %collective-permute-start.9 = (bf16[2,2,256,128]{3,2,1,0:T(8,128)(2,1)S(1)}, bf16[2,2,256,128]{3,2,1,0:T(8,128)(2,1)S(1)}, u32[]{:S(2)}, u32[]{:S(2)}) collective-permute-start(bf16[2,2,256,128]{3,2,1,0:T(8,128)(2,1)S(1)} %get-tuple-element.33), channel_id=1, source_target_pairs={{0,12},{4,8},{8,4},{12,0},{16,28},{20,24},{24,20},{28,16},{1,13},{... | collective-permute-start | bytes 786440 | tf_op jit(solution)/shard_map/ppermute | solution.py:280
  14.4 1.6 %copy-done = bf16[1024,1024]{1,0:T(8,128)(2,1)S(1)} copy-done((bf16[1024,1024]{1,0:T(8,128)(2,1)S(1)}, bf16[1024,1024]{1,0:T(8,128)(2,1)}, u32[]{:S(2)}) %copy-start) | copy-done | bytes 2097176
  15.9 0.7 %copy-done.3 = s32[8,4,8]{2,1,0:T(4,128)S(1)} copy-done((s32[8,4,8]{2,1,0:T(4,128)S(1)}, s32[8,4,8]{2,1,0:T(4,128)}, u32[]{:S(2)}) %copy-start.3) | copy-done | bytes 1048
  16.7 3.3 %arrange_block.1 = (bf16[3584,1024]{1,0:T(8,128)(2,1)S(1)}, bf16[1536,1024]{1,0:T(8,128)(2,1)S(1)}) custom-call(s32[8,4,8]{2,1,0:T(4,128)S(1)} %copy-done.3, bf16[1024,1024]{1,0:T(8,128)(2,1)S(1)} %copy-done, bf16[1024,1024]{1,0:T(8,128)(2,1)S(1)} %collective-permute-done.3.refs_1_), custom_call_target="tpu_custom_call" | custom-call | tf_op jit(solution)/shard_map/arrange_block/pallas_call | solution.py:137
  20.0 4.2 %collective-permute-done.refs_5_ = bf16[8,2,16,512]{3,2,1,0:T(8,128)(2,1)S(1)} collective-permute-done((bf16[8,2,16,512]{3,2,1,0:T(8,128)(2,1)S(1)}, bf16[8,2,16,512]{3,2,1,0:T(8,128)(2,1)S(1)}, u32[]{:S(2)}, u32[]{:S(2)}) %collective-permute-start) | collective-permute-done | bytes 262176 | tf_op jit(solution)/shard_map/ppermute | solution.py:280
  24.2 5.1 %collective-permute-done.2.refs_6_ = bf16[8,2,16,512]{3,2,1,0:T(8,128)(2,1)S(1)} collective-permute-done((bf16[8,2,16,512]{3,2,1,0:T(8,128)(2,1)S(1)}, bf16[8,2,16,512]{3,2,1,0:T(8,128)(2,1)S(1)}, u32[]{:S(2)}, u32[]{:S(2)}) %collective-permute-start.2) | collective-permute-done | bytes 262176 | tf_op jit(solution)/shard_map/ppermute | solution.py:280
  29.2 1.5 %select_tiles.2 = (bf16[2,2,256,128]{3,2,1,0:T(8,128)(2,1)S(1)}, bf16[2,2,256,128]{3,2,1,0:T(8,128)(2,1)S(1)}, bf16[2,2,256,128]{3,2,1,0:T(8,128)(2,1)S(1)}) custom-call(s32[8,4,8]{2,1,0:T(4,128)S(1)} %copy-done.3, bf16[256,512]{1,0:T(8,128)(2,1)S(1)} %bitcast.20, bf16[256,512]{1,0:T(8,128)(2,1)S(1)} %bitcast.21), custom_call_target="tpu_custom_call" | custom-call | tf_op jit(solution)/shard_map/select_tiles/pallas_call | solution.py:88
  30.7 1.6 %collective-permute-start.4 = (bf16[2,2,256,128]{3,2,1,0:T(8,128)(2,1)S(1)}, bf16[2,2,256,128]{3,2,1,0:T(8,128)(2,1)S(1)}, u32[]{:S(2)}, u32[]{:S(2)}) collective-permute-start(bf16[2,2,256,128]{3,2,1,0:T(8,128)(2,1)S(1)} %get-tuple-element.27), channel_id=1, source_target_pairs={{0,4},{4,0},{8,12},{12,8},{16,20},{20,16},{24,28},{28,24},{1,5},{5... | collective-permute-start | bytes 786440 | tf_op jit(solution)/shard_map/ppermute | solution.py:280
  32.3 0.6 collective-permute-start.5
  33.0 1.3 %collective-permute-start.6 = (bf16[2,2,256,128]{3,2,1,0:T(8,128)(2,1)S(1)}, bf16[2,2,256,128]{3,2,1,0:T(8,128)(2,1)S(1)}, u32[]{:S(2)}, u32[]{:S(2)}) collective-permute-start(bf16[2,2,256,128]{3,2,1,0:T(8,128)(2,1)S(1)} %get-tuple-element.29), channel_id=1, source_target_pairs={{0,12},{4,8},{8,4},{12,0},{16,28},{20,24},{24,20},{28,16},{1,13},{... | collective-permute-start | bytes 786440 | tf_op jit(solution)/shard_map/ppermute | solution.py:280
  34.3 2.4 %collective-permute-done.8 = bf16[2,2,256,128]{3,2,1,0:T(8,128)(2,1)S(1)} collective-permute-done((bf16[2,2,256,128]{3,2,1,0:T(8,128)(2,1)S(1)}, bf16[2,2,256,128]{3,2,1,0:T(8,128)(2,1)S(1)}, u32[]{:S(2)}, u32[]{:S(2)}) %collective-permute-start.8) | collective-permute-done | bytes 262176 | tf_op jit(solution)/shard_map/ppermute | solution.py:280
  36.7 2.1 %contract_tiles.3 = (f32[128,1024]{1,0:T(8,128)S(1)}, f32[128,1024]{1,0:T(8,128)S(1)}) custom-call(bf16[8,2,16,512]{3,2,1,0:T(8,128)(2,1)S(1)} %get-tuple-element.21.refs_0_, bf16[8,2,16,512]{3,2,1,0:T(8,128)(2,1)S(1)} %collective-permute-done.1.refs_1_, bf16[2,2,8,2,16,128]{5,4,3,2,1,0:T(8,128)(2,1)S(1)} %bitcast.25, ...), custom_call_target="tpu_custom_call" | custom-call | tf_op jit(solution)/shard_map/contract_tiles/pallas_call | solution.py:212
  38.9 3.5 %collective-permute-done.5 = bf16[2,2,256,128]{3,2,1,0:T(8,128)(2,1)S(1)} collective-permute-done((bf16[2,2,256,128]{3,2,1,0:T(8,128)(2,1)S(1)}, bf16[2,2,256,128]{3,2,1,0:T(8,128)(2,1)S(1)}, u32[]{:S(2)}, u32[]{:S(2)}) %collective-permute-start.5) | collective-permute-done | bytes 262176 | tf_op jit(solution)/shard_map/ppermute | solution.py:280
  42.3 4.5 %collective-permute-done.6 = bf16[2,2,256,128]{3,2,1,0:T(8,128)(2,1)S(1)} collective-permute-done((bf16[2,2,256,128]{3,2,1,0:T(8,128)(2,1)S(1)}, bf16[2,2,256,128]{3,2,1,0:T(8,128)(2,1)S(1)}, u32[]{:S(2)}, u32[]{:S(2)}) %collective-permute-start.6) | collective-permute-done | bytes 262176 | tf_op jit(solution)/shard_map/ppermute | solution.py:280
  46.8 0.8 %contract_tiles.5 = s16[128,1152]{1,0:T(8,128)(2,1)S(1)} custom-call(bf16[2,2,8,2,16,128]{5,4,3,2,1,0:T(8,128)(2,1)S(1)} %bitcast.12, bf16[2,2,8,2,16,128]{5,4,3,2,1,0:T(8,128)(2,1)S(1)} %bitcast.14, bf16[2,2,8,2,16,128]{5,4,3,2,1,0:T(8,128)(2,1)S(1)} %bitcast.16, bf16[1536,1024]{1,0:T(8,128)(2,1)S(1)} %get-tuple-element.30.refs_3_, ...), custom_call_target="tpu_custom_call" | custom-call | tf_op jit(solution)/shard_map/contract_tiles/pallas_call | solution.py:212
  47.7 1.6 %collective-permute-start.10 = (s16[128,1152]{1,0:T(8,128)(2,1)S(1)}, s16[128,1152]{1,0:T(8,128)(2,1)S(1)}, u32[]{:S(2)}, u32[]{:S(2)}) collective-permute-start(s16[128,1152]{1,0:T(8,128)(2,1)S(1)} %contract_tiles.5), channel_id=1, source_target_pairs={{0,2},{1,3},{2,0},{3,1},{4,6},{5,7},{6,4},{7,5},{8,10},{9,11},{10,... | collective-permute-start | bytes 884744 | tf_op jit(solution)/shard_map/ppermute | solution.py:280
  49.8 5.8 %collective-permute-done.10.arrived = s16[128,1152]{1,0:T(8,128)(2,1)S(1)} collective-permute-done((s16[128,1152]{1,0:T(8,128)(2,1)S(1)}, s16[128,1152]{1,0:T(8,128)(2,1)S(1)}, u32[]{:S(2)}, u32[]{:S(2)}) %collective-permute-start.10) | collective-permute-done | bytes 294944 | tf_op jit(solution)/shard_map/ppermute | solution.py:280
  55.8 12.5 %all_to_all.5.received = bf16[8,16,1024]{2,1,0:T(8,128)(2,1)S(1)} all-to-all(bf16[8,16,1024]{2,1,0:T(8,128)(2,1)S(1)} %bitcast.22), channel_id=1, replica_groups=mesh['col'=8,'row'=4] {'col'}, dimensions={0} | all-to-all | bytes 524288 | tf_op jit(solution)/shard_map/all_to_all | solution.py:324
  68.3 1.7 %reorder_tiles.1 = bf16[16,8192]{1,0:T(8,128)(2,1)} custom-call(s32[64]{0:T(128)S(1)} %copy-done.4, bf16[8,16,1024]{2,1,0:T(8,128)(2,1)S(1)} %all_to_all.5.received), custom_call_target="tpu_custom_call" | custom-call | tf_op jit(solution)/shard_map/reorder_tiles/pallas_call | solution.py:269
  (18 shorter events, 2.4 us)
Async XLA Ops:
  0.0 13.9 %collective-permute-start.3 = (bf16[1024,1024]{1,0:T(8,128)(2,1)}, bf16[1024,1024]{1,0:T(8,128)(2,1)S(1)}, u32[]{:S(2)}, u32[]{:S(2)}) collective-permute-start(bf16[1024,1024]{1,0:T(8,128)(2,1)} %refs_0_.1), channel_id=1, source_target_pairs={{0,1},{1,0},{2,3},{3,2},{4,5},{5,4},{6,7},{7,6},{8,9},{9,8},{10,11... | collective-permute-start | bytes 6291464 | tf_op jit(solution)/shard_map/ppermute | solution.py:280
  0.5 1.0 %copy-start.1 = (bf16[512,512]{1,0:T(8,128)(2,1)S(1)}, bf16[512,512]{1,0:T(8,128)(2,1)}, u32[]{:S(2)}) copy-start(bf16[512,512]{1,0:T(8,128)(2,1)} %param.4) | copy-start | bytes 1572868
  1.6 4.2 %collective-permute-start.1 = (bf16[8,2,16,512]{3,2,1,0:T(8,128)(2,1)S(1)}, bf16[8,2,16,512]{3,2,1,0:T(8,128)(2,1)S(1)}, u32[]{:S(2)}, u32[]{:S(2)}) collective-permute-start(bf16[8,2,16,512]{3,2,1,0:T(8,128)(2,1)S(1)} %get-tuple-element.22), channel_id=1, source_target_pairs={{0,1},{1,0},{2,3},{3,2},{4,5},{5,4},{6,7},{7,6},{8,9},{9,8},{10,11... | collective-permute-start | bytes 786440 | tf_op jit(solution)/shard_map/ppermute | solution.py:280
  1.7 22.5 %collective-permute-start = (bf16[8,2,16,512]{3,2,1,0:T(8,128)(2,1)S(1)}, bf16[8,2,16,512]{3,2,1,0:T(8,128)(2,1)S(1)}, u32[]{:S(2)}, u32[]{:S(2)}) collective-permute-start(bf16[8,2,16,512]{3,2,1,0:T(8,128)(2,1)S(1)} %get-tuple-element.21.refs_0_), channel_id=1, source_target_pairs={{0,16},{4,20},{8,24},{12,28},{16,0},{20,4},{24,8},{28,12},{1,17},{... | collective-permute-start | bytes 786440 | tf_op jit(solution)/shard_map/ppermute | solution.py:280
  5.7 23.5 %collective-permute-start.2 = (bf16[8,2,16,512]{3,2,1,0:T(8,128)(2,1)S(1)}, bf16[8,2,16,512]{3,2,1,0:T(8,128)(2,1)S(1)}, u32[]{:S(2)}, u32[]{:S(2)}) collective-permute-start(bf16[8,2,16,512]{3,2,1,0:T(8,128)(2,1)S(1)} %collective-permute-done.1.refs_1_), channel_id=1, source_target_pairs={{0,16},{4,20},{8,24},{12,28},{16,0},{20,4},{24,8},{28,12},{1,17},{... | collective-permute-start | bytes 786440 | tf_op jit(solution)/shard_map/ppermute | solution.py:280
  8.6 0.7 %copy-start.2 = (s32[8,4,8]{2,1,0:T(4,128)S(1)}, s32[8,4,8]{2,1,0:T(4,128)}, u32[]{:S(2)}) copy-start(s32[8,4,8]{2,1,0:T(4,128)} %wanted.5) | copy-start | bytes 3076
  10.8 22.2 %collective-permute-start.9 = (bf16[2,2,256,128]{3,2,1,0:T(8,128)(2,1)S(1)}, bf16[2,2,256,128]{3,2,1,0:T(8,128)(2,1)S(1)}, u32[]{:S(2)}, u32[]{:S(2)}) collective-permute-start(bf16[2,2,256,128]{3,2,1,0:T(8,128)(2,1)S(1)} %get-tuple-element.33), channel_id=1, source_target_pairs={{0,12},{4,8},{8,4},{12,0},{16,28},{20,24},{24,20},{28,16},{1,13},{... | collective-permute-start | bytes 786440 | tf_op jit(solution)/shard_map/ppermute | solution.py:280
  13.4 20.9 %collective-permute-start.7 = (bf16[2,2,256,128]{3,2,1,0:T(8,128)(2,1)S(1)}, bf16[2,2,256,128]{3,2,1,0:T(8,128)(2,1)S(1)}, u32[]{:S(2)}, u32[]{:S(2)}) collective-permute-start(bf16[2,2,256,128]{3,2,1,0:T(8,128)(2,1)S(1)} %get-tuple-element.31), channel_id=1, source_target_pairs={{0,4},{4,0},{8,12},{12,8},{16,20},{20,16},{24,28},{28,24},{1,5},{5... | collective-permute-start | bytes 786440 | tf_op jit(solution)/shard_map/ppermute | solution.py:280
  13.9 22.8 %collective-permute-start.8 = (bf16[2,2,256,128]{3,2,1,0:T(8,128)(2,1)S(1)}, bf16[2,2,256,128]{3,2,1,0:T(8,128)(2,1)S(1)}, u32[]{:S(2)}, u32[]{:S(2)}) collective-permute-start(bf16[2,2,256,128]{3,2,1,0:T(8,128)(2,1)S(1)} %get-tuple-element.32), channel_id=1, source_target_pairs={{0,8},{4,12},{8,0},{12,4},{16,24},{20,28},{24,16},{28,20},{1,9},{5... | collective-permute-start | bytes 786440 | tf_op jit(solution)/shard_map/ppermute | solution.py:280
  14.4 1.6 %copy-start = (bf16[1024,1024]{1,0:T(8,128)(2,1)S(1)}, bf16[1024,1024]{1,0:T(8,128)(2,1)}, u32[]{:S(2)}) copy-start(bf16[1024,1024]{1,0:T(8,128)(2,1)} %refs_0_.1) | copy-start | bytes 6291460
  15.9 0.7 %copy-start.3 = (s32[8,4,8]{2,1,0:T(4,128)S(1)}, s32[8,4,8]{2,1,0:T(4,128)}, u32[]{:S(2)}) copy-start(s32[8,4,8]{2,1,0:T(4,128)} %wanted.5) | copy-start | bytes 3076
  30.7 8.1 %collective-permute-start.4 = (bf16[2,2,256,128]{3,2,1,0:T(8,128)(2,1)S(1)}, bf16[2,2,256,128]{3,2,1,0:T(8,128)(2,1)S(1)}, u32[]{:S(2)}, u32[]{:S(2)}) collective-permute-start(bf16[2,2,256,128]{3,2,1,0:T(8,128)(2,1)S(1)} %get-tuple-element.27), channel_id=1, source_target_pairs={{0,4},{4,0},{8,12},{12,8},{16,20},{20,16},{24,28},{28,24},{1,5},{5... | collective-permute-start | bytes 786440 | tf_op jit(solution)/shard_map/ppermute | solution.py:280
  32.3 10.0 %collective-permute-start.5 = (bf16[2,2,256,128]{3,2,1,0:T(8,128)(2,1)S(1)}, bf16[2,2,256,128]{3,2,1,0:T(8,128)(2,1)S(1)}, u32[]{:S(2)}, u32[]{:S(2)}) collective-permute-start(bf16[2,2,256,128]{3,2,1,0:T(8,128)(2,1)S(1)} %get-tuple-element.28), channel_id=1, source_target_pairs={{0,8},{4,12},{8,0},{12,4},{16,24},{20,28},{24,16},{28,20},{1,9},{5... | collective-permute-start | bytes 786440 | tf_op jit(solution)/shard_map/ppermute | solution.py:280
  33.0 13.9 %collective-permute-start.6 = (bf16[2,2,256,128]{3,2,1,0:T(8,128)(2,1)S(1)}, bf16[2,2,256,128]{3,2,1,0:T(8,128)(2,1)S(1)}, u32[]{:S(2)}, u32[]{:S(2)}) collective-permute-start(bf16[2,2,256,128]{3,2,1,0:T(8,128)(2,1)S(1)} %get-tuple-element.29), channel_id=1, source_target_pairs={{0,12},{4,8},{8,4},{12,0},{16,28},{20,24},{24,20},{28,16},{1,13},{... | collective-permute-start | bytes 786440 | tf_op jit(solution)/shard_map/ppermute | solution.py:280
  47.7 8.0 %collective-permute-start.10 = (s16[128,1152]{1,0:T(8,128)(2,1)S(1)}, s16[128,1152]{1,0:T(8,128)(2,1)S(1)}, u32[]{:S(2)}, u32[]{:S(2)}) collective-permute-start(s16[128,1152]{1,0:T(8,128)(2,1)S(1)} %contract_tiles.5), channel_id=1, source_target_pairs={{0,2},{1,3},{2,0},{3,1},{4,6},{5,7},{6,4},{7,5},{8,10},{9,11},{10,... | collective-permute-start | bytes 884744 | tf_op jit(solution)/shard_map/ppermute | solution.py:280
  49.2 19.0 %copy-start.4 = (s32[64]{0:T(128)S(1)}, s32[64]{0:T(128)}, u32[]{:S(2)}) copy-start(s32[64]{0:T(128)} %owner.1) | copy-start | bytes 772

commit v3 on v2

--- a/solution.py
+++ b/solution.py
@@ -10,6 +10,7 @@
 TILE = 128
 CAP = 2
 CORES = 2
+FIRST = 2
 SMALL = 8 * 1024 * 1024
 LEAST = 2.0 ** -125
 STEPS = 32766.0
@@ -96,6 +97,70 @@
     )(wanted, *groups)
 
 
+def choice_kernel(per_source, away, flips, wanted, *outs):
+    me, row = lax.axis_index("col"), lax.axis_index("row")
+    length = wanted.shape[2]
+    source = me ^ away
+    one = (lax.broadcasted_iota(jnp.int32, (TILE, TILE), 0) == lax.broadcasted_iota(jnp.int32, (TILE, TILE), 1)).astype(outs[0].dtype)
+    for g, out in enumerate(outs):
+        out[...] = jnp.zeros_like(out)
+        for n, flip in enumerate(flips):
+            other = me ^ flip
+
+            def step(k, count):
+                w = wanted[other, row ^ g, k]
+                mine = w // per_source == source
+                at = pl.ds(pl.multiple_of((w % per_source) * TILE, TILE), TILE)
+                for slot in range(CAP):
+
+                    @pl.when(mine & (count == slot))
+                    def _():
+                        low = (n * CAP + slot) * TILE
+                        out[at, low:low + TILE] = one
+
+                return count + mine.astype(jnp.int32)
+
+            lax.fori_loop(0, length, step, jnp.int32(0))
+
+
+def choice(wanted, per_source, away, flips, dtype):
+    shape = jax.ShapeDtypeStruct((per_source * TILE, len(flips) * CAP * TILE), dtype)
+    return pl.pallas_call(
+        functools.partial(choice_kernel, per_source, away, flips),
+        out_shape=[shape] * CORES,
+        in_specs=[SMEM],
+        out_specs=[VMEM] * CORES,
+        compiler_params=params(4 * shape.size * CORES),
+        name="choice_matrices",
+    )(wanted)
+
+
+def pass_on_kernel(ranges, *refs):
+    groups, choices, outs = refs[:CORES], refs[CORES:2 * CORES], refs[2 * CORES:]
+    count = len(outs) // len(ranges)
+    for g in range(CORES):
+        x = jnp.dot(groups[g][...], choices[g][...], preferred_element_type=jnp.float32).astype(outs[0].dtype)
+        for m, (start, stop) in enumerate(ranges):
+            for n in range(count):
+                for slot in range(CAP):
+                    low = (n * CAP + slot) * TILE
+                    outs[m * count + n][g, slot] = x[start:stop, low:low + TILE]
+
+
+def pass_on(groups, choices, ranges):
+    rows, chosen = groups[0].shape[0], choices[0].shape[1]
+    shapes = [jax.ShapeDtypeStruct((CORES, CAP, stop - start, TILE), groups[0].dtype) for start, stop in ranges for _ in range(chosen // (CAP * TILE))]
+    size = sum(2 * x.size for x in (*groups, *choices)) + 4 * CORES * rows * chosen * 2
+    return pl.pallas_call(
+        functools.partial(pass_on_kernel, ranges),
+        out_shape=shapes,
+        in_specs=[VMEM] * (2 * CORES),
+        out_specs=[VMEM] * len(shapes),
+        compiler_params=params(size),
+        name="pass_on_tiles",
+    )(*groups, *choices)
+
+
 def arrange_kernel(per_source, top, wanted, *refs):
     blocks, (early, far) = refs[:CORES], refs[CORES:]
     me, row = lax.axis_index("col"), lax.axis_index("row")
@@ -170,13 +235,15 @@
     out[at, :width], out[at, width:] = code(x)
 
 
-def fill(left, source, flip, depth, at):
+def fill(left, source, units, flip, depth, at):
     y = (lax.axis_index("row") // CORES) ^ flip
-    rows = pl.ds(at, source.shape[-4] * source.shape[-2])
+    span = units[1] - units[0]
+    low = units[0] if source.shape[-4] > span else 0
+    rows = pl.ds(at, span * source.shape[-2])
     if len(source.shape) == 4:
-        tiles = [source[:, y]]
+        tiles = [source[low:low + span, y]]
     else:
-        tiles = [source[g, slot, :, y] for g in range(CORES) for slot in range(CAP)]
+        tiles = [source[g, slot, low:low + span, y] for g in range(source.shape[0]) for slot in range(CAP)]
     for tile in tiles:
         width = tile.shape[-1]
         left[rows, depth:depth + width] = tile.reshape(-1, width)
@@ -184,15 +251,23 @@
     return depth
 
 
-def contract_kernel(count, slots, coded, *refs):
+def contract_kernel(count, pieces, coded, *refs):
     sources, block = refs[:count], refs[count]
-    before, outs, left = refs[count + 1:-1 - len(slots)], refs[-1 - len(slots):-1], refs[-1]
-    for n, flips in enumerate(slots):
+    before, outs, left = refs[count + 1:-1 - len(pieces)], refs[-1 - len(pieces):-1], refs[-1]
+    base = 0
+    for n, (units, flips) in enumerate(pieces):
+        rows = outs[n].shape[0] // len(flips)
         for j, flip in enumerate(flips):
             depth = 0
             for source in sources:
-                depth = fill(left, source, flip, depth, j * (left.shape[0] // len(flips)))
-        x = jnp.dot(left[...], block[...], preferred_element_type=jnp.float32)
+                depth = fill(left, source, units, flip, depth, base + j * rows)
+        base += outs[n].shape[0]
+    product = jnp.dot(left[...], block[...], preferred_element_type=jnp.float32)
+    base = 0
+    for n in range(len(pieces)):
+        rows = outs[n].shape[0]
+        x = product[base:base + rows]
+        base += rows
         if before:
             x = before[n][...] + x
         if coded:
@@ -201,20 +276,20 @@
             outs[n][...] = x
 
 
-def contract(sources, block, slots, before=(), coded=False):
+def contract(sources, block, pieces, before=(), coded=False):
     depth, width = block.shape
-    rows = sources[0].shape[-4] * sources[0].shape[-2] * len(slots[0])
+    rows = [(units[1] - units[0]) * sources[0].shape[-2] * len(flips) for units, flips in pieces]
     if coded:
-        shape = jax.ShapeDtypeStruct((rows, width + TILE), jnp.int16)
+        shapes = [jax.ShapeDtypeStruct((n, width + TILE), jnp.int16) for n in rows]
     else:
-        shape = jax.ShapeDtypeStruct((rows, width), jnp.float32)
-    size = 2 * depth * (width + rows) + 12 * width * rows * len(slots) + sum(2 * x.size for x in sources)
-    return pl.pallas_call(
-        functools.partial(contract_kernel, len(sources), slots, coded),
-        out_shape=[shape] * len(slots),
+        shapes = [jax.ShapeDtypeStruct((n, width), jnp.float32) for n in rows]
+    size = 2 * depth * (width + sum(rows)) + 16 * width * sum(rows) + sum(2 * x.size for x in sources)
+    return pl.pallas_call(
+        functools.partial(contract_kernel, len(sources), pieces, coded),
+        out_shape=shapes,
         in_specs=[VMEM] * (len(sources) + 1 + len(before)),
-        out_specs=[VMEM] * len(slots),
-        scratch_shapes=[pltpu.VMEM((rows, depth), block.dtype)],
+        out_specs=[VMEM] * len(shapes),
+        scratch_shapes=[pltpu.VMEM((sum(rows), depth), block.dtype)],
         compiler_params=params(size),
         name="contract_tiles",
     )(*sources, block, *before)
@@ -241,20 +316,25 @@
     )(keep, arrived)
 
 
-def finish_kernel(keep, arrived, out):
-    for at in steps(keep.shape[0]):
-        out[at] = (keep[at] + decode(arrived[at])).astype(out.dtype)
-
-
-def finish(keep, arrived):
+def finish_kernel(*refs):
+    out, base = refs[-1], 0
+    for keep, arrived in zip(refs[:-1:2], refs[1:-1:2]):
+        for at in steps(keep.shape[0]):
+            out[base + at.start:base + at.stop] = (keep[at] + decode(arrived[at])).astype(out.dtype)
+        base += keep.shape[0]
+
+
+def finish(pieces):
+    flat = [x for piece in pieces for x in piece]
+    rows = sum(keep.shape[0] for keep, _ in pieces)
     return pl.pallas_call(
         finish_kernel,
-        out_shape=jax.ShapeDtypeStruct(keep.shape, jnp.bfloat16),
-        in_specs=[VMEM, VMEM],
+        out_shape=jax.ShapeDtypeStruct((rows, flat[0].shape[1]), jnp.bfloat16),
+        in_specs=[VMEM] * len(flat),
         out_specs=VMEM,
         compiler_params=params(),
         name="finish_rows",
-    )(keep, arrived)
+    )(*flat)
 
 
 def reorder_kernel(tiles_held, owner, received, out):
@@ -295,32 +375,50 @@
         amplitudes = amplitudes.reshape(units, columns // units, parts, per_device, -1).transpose(0, 2, 1, 3, 4)
     order = halving_order(ys)
     slots = [order[:ys // 2], order[ys // 2:]]
+    first = units * FIRST // 4
+    bounds = [(0, first), (first, units)] if first < units else [(0, units)]
 
     def whole(x):
         return x.reshape(units, ys, b, -1)
 
-    def near(groups, away):
-        picked = select(wanted, [x.reshape(units * ys * b, -1) for x in groups], per_source, away, low)
-        return [swap(x, "col", f).reshape(CORES, CAP, units, ys, b, TILE) for x, f in zip(picked, low)]
+    def flat(x):
+        return x.reshape(units * ys * b, -1)
+
+    def spread(picked):
+        return [swap(x, "col", f).reshape(CORES, CAP, -1, ys, b, TILE) for x, f in zip(picked, low)]
 
     mine, theirs = split(amplitudes.reshape(units, ys, CORES, b, -1))
     own = [mine, swap(theirs, "row", 1)]
-    mirrors = [whole(swap(x, "col", top)) for x in own]
-    nearby = near(own, 0)
+    early = swap(mine, "col", top)
+    picked = select(wanted, [flat(x) for x in own], per_source, 0, low)
+    nearby = spread(picked)
+    mirrors = [early, swap(own[1], "col", top)]
     blocks = arrange(wanted, [integrals, swap(integrals, "row", 1)], per_source, top)
-    *mirrors, early_block, far_block = lax.optimization_barrier((*mirrors, *blocks))
-    far = near(mirrors, top)
-    sums = contract(own + nearby + mirrors, early_block, slots)
-    send, = contract(far, far_block, slots[:1], sums[:1], coded=True)
-    keep, = contract(far, far_block, slots[1:], sums[1:])
-    bit = CORES
-    while True:
-        arrived = swap(send, "row", bit)
-        bit *= 2
-        if bit == parts:
-            break
-        send, keep = fold(keep, arrived)
-    held = finish(keep, arrived).reshape(columns, per_device, -1)
+    late_wanted, *blocks = lax.optimization_barrier((wanted, *blocks))
+    choices = choice(late_wanted, per_source, top, low, amplitudes.dtype)
+    *mirrors, early_block, far_block, choices = lax.optimization_barrier((*mirrors, *blocks, choices))
+    mirrors = [whole(x) for x in mirrors]
+    height = ys * b
+    passed = pass_on([flat(x) for x in mirrors], choices, [(lo * height, hi * height) for lo, hi in bounds])
+    groups = [passed[n:n + len(low)] for n in range(0, len(passed), len(low))]
+    far = [spread(groups[0])]
+    sums = contract(own + nearby + mirrors, early_block, [(at, flips) for at in bounds for flips in slots])
+    for group in groups[1:]:
+        far.append(spread(group))
+    pieces = []
+    for n, (lo, hi) in enumerate(bounds):
+        span = (0, hi - lo)
+        send, = contract(far[n], far_block, [(span, slots[0])], sums[2 * n:2 * n + 1], coded=True)
+        keep, = contract(far[n], far_block, [(span, slots[1])], sums[2 * n + 1:2 * n + 2])
+        bit = CORES
+        while True:
+            arrived = swap(send, "row", bit)
+            bit *= 2
+            if bit == parts:
+                break
+            send, keep = fold(keep, arrived)
+        pieces.append((keep, arrived))
+    held = finish(pieces).reshape(columns, per_device, -1)
     exchanged = lax.all_to_all(held, "col", split_axis=0, concat_axis=0, tiled=True)
     return reorder(owner, exchanged)
 

time: 70.3 us -> 67.9 us (0.966)
  waiting for transfers between devices: 25.4 us -> 16.8 us
  starting transfers between devices: 16.1 us -> 19.4 us
  Pallas kernels: 11.7 us -> 14.7 us
    ppermute x11 -> x15, waiting for transfers between devices: 25.4 us -> 16.8 us  [swap(): lax.ppermute(x, axis, [(i, i ^ flip) for i in range(lax.axis_size(axis))])]
    pallas_call x4 -> x8, Pallas kernels: 3.66 us -> 8.09 us  [the longest x5 5.03 us: contract(): pl.pallas_call(functools.partial(contract_kernel, len(sources), pieces, c...]
    ppermute x11 -> x15, starting transfers between devices: 16.1 us -> 19.4 us  [swap(): lax.ppermute(x, axis, [(i, i ^ flip) for i in range(lax.axis_size(axis))])]
    pallas_call x2 -> x1, Pallas kernels: 2.99 us -> 1.5 us  [select(): pl.pallas_call(functools.partial(select_kernel, per_source, away, flips),...]
  transfers between devices with their start and end apart: 11 -> 15, of which waited for: 6 -> 7; matrix products, arithmetic and copies ran while one was open for 0% -> 0% of each run, Pallas kernels for 13% -> 19%
where the time goes in v3:
time: 67.9 us; the launch traced here: 67.5 us
  starting transfers between devices  19.4 us (29%)
  waiting for transfers between devices  16.8 us (25%)
  Pallas kernels  14.7 us (22%)
  blocking collectives  12.5 us (18%)
  local copies, waits for them, and re-layouts  4.07 us (6%)
    ppermute x15, starting transfers between devices, swap(): lax.ppermute(x, axis, [(i, i ^ flip) for i in range(lax.axis_size(axis))])  19.4 us
    ppermute x15, waiting for transfers between devices, swap(): lax.ppermute(x, axis, [(i, i ^ flip) for i in range(lax.axis_size(axis))])  16.8 us
    all_to_all x1, blocking collectives, body(): lax.all_to_all(held, 'col', split_axis=0, concat_axis=0, tiled=True)  12.5 us
    pallas_call x5, Pallas kernels, contract(): pl.pallas_call(functools.partial(contract_kernel, len(sources), pieces, c...  5.03 us
    unnamed x10, local copies, waits for them, and re-layouts  4.07 us
    pallas_call x1, Pallas kernels, arrange(): pl.pallas_call(functools.partial(arrange_kernel, per_source, top), grid=(...  3.33 us
    pallas_call x1, Pallas kernels, choice(): pl.pallas_call(functools.partial(choice_kernel, per_source, away, flips),...  2.35 us
    pallas_call x1, Pallas kernels, reorder(): pl.pallas_call(functools.partial(reorder_kernel, width // TILE), out_shap...  1.68 us
  transfers between devices with their start and end apart: 15, of which 7 were waited for; matrix products, arithmetic and copies ran while one was open for 0% of the time, Pallas kernels for 19%

profile of v3, /device:TPU:0, one launch (start us, length us, event | category | flops | bytes accessed | tf_op | source)
XLA Modules:
  0.0 67.5 jit_solution(18243522384022752951)
XLA Ops:
  0.5 1.0 %copy-done.1 = bf16[512,512]{1,0:T(8,128)(2,1)S(1)} copy-done((bf16[512,512]{1,0:T(8,128)(2,1)S(1)}, bf16[512,512]{1,0:T(8,128)(2,1)}, u32[]{:S(2)}) %copy-start.1) | copy-done | bytes 524312
  1.7 4.0 %collective-permute-start = (bf16[8,2,16,512]{3,2,1,0:T(8,128)(2,1)S(1)}, bf16[8,2,16,512]{3,2,1,0:T(8,128)(2,1)S(1)}, u32[]{:S(2)}, u32[]{:S(2)}) collective-permute-start(bf16[8,2,16,512]{3,2,1,0:T(8,128)(2,1)S(1)} %get-tuple-element.33.refs_0_), channel_id=1, source_target_pairs={{0,16},{4,20},{8,24},{12,28},{16,0},{20,4},{24,8},{28,12},{1,17},{... | collective-permute-start | bytes 786440 | tf_op jit(solution)/shard_map/ppermute | solution.py:360
  5.7 2.8 %collective-permute-start.2 = (bf16[8,2,16,512]{3,2,1,0:T(8,128)(2,1)S(1)}, bf16[8,2,16,512]{3,2,1,0:T(8,128)(2,1)S(1)}, u32[]{:S(2)}, u32[]{:S(2)}) collective-permute-start(bf16[8,2,16,512]{3,2,1,0:T(8,128)(2,1)S(1)} %collective-permute-done.1.refs_1_), channel_id=1, source_target_pairs={{0,16},{4,20},{8,24},{12,28},{16,0},{20,4},{24,8},{28,12},{1,17},{... | collective-permute-start | bytes 786440 | tf_op jit(solution)/shard_map/ppermute | solution.py:360
  9.3 1.5 %select_tiles.1 = (bf16[2,2,256,128]{3,2,1,0:T(8,128)(2,1)S(1)}, bf16[2,2,256,128]{3,2,1,0:T(8,128)(2,1)S(1)}, bf16[2,2,256,128]{3,2,1,0:T(8,128)(2,1)S(1)}) custom-call(s32[8,4,8]{2,1,0:T(4,128)S(1)} %copy-done.2, bf16[256,512]{1,0:T(8,128)(2,1)S(1)} %bitcast.15, bf16[256,512]{1,0:T(8,128)(2,1)S(1)} %bitcast.16), custom_call_target="tpu_custom_call" | custom-call | tf_op jit(solution)/shard_map/select_tiles/pallas_call | solution.py:89
  10.8 1.6 %collective-permute-start.7 = (bf16[2,2,256,128]{3,2,1,0:T(8,128)(2,1)S(1)}, bf16[2,2,256,128]{3,2,1,0:T(8,128)(2,1)S(1)}, u32[]{:S(2)}, u32[]{:S(2)}) collective-permute-start(bf16[2,2,256,128]{3,2,1,0:T(8,128)(2,1)S(1)} %get-tuple-element.50), channel_id=1, source_target_pairs={{0,4},{4,0},{8,12},{12,8},{16,20},{20,16},{24,28},{28,24},{1,5},{5... | collective-permute-start | bytes 786440 | tf_op jit(solution)/shard_map/ppermute | solution.py:360
  12.4 1.6 %collective-permute-start.8 = (bf16[2,2,256,128]{3,2,1,0:T(8,128)(2,1)S(1)}, bf16[2,2,256,128]{3,2,1,0:T(8,128)(2,1)S(1)}, u32[]{:S(2)}, u32[]{:S(2)}) collective-permute-start(bf16[2,2,256,128]{3,2,1,0:T(8,128)(2,1)S(1)} %get-tuple-element.51), channel_id=1, source_target_pairs={{0,8},{4,12},{8,0},{12,4},{16,24},{20,28},{24,16},{28,20},{1,9},{5... | collective-permute-start | bytes 786440 | tf_op jit(solution)/shard_map/ppermute | solution.py:360
  14.4 1.6 %copy-done = bf16[1024,1024]{1,0:T(8,128)(2,1)S(1)} copy-done((bf16[1024,1024]{1,0:T(8,128)(2,1)S(1)}, bf16[1024,1024]{1,0:T(8,128)(2,1)}, u32[]{:S(2)}) %copy-start) | copy-done | bytes 2097176
  16.7 3.3 %arrange_block.1 = (bf16[3584,1024]{1,0:T(8,128)(2,1)S(1)}, bf16[1536,1024]{1,0:T(8,128)(2,1)S(1)}) custom-call(s32[8,4,8]{2,1,0:T(4,128)S(1)} %copy-done.3, bf16[1024,1024]{1,0:T(8,128)(2,1)S(1)} %copy-done, bf16[1024,1024]{1,0:T(8,128)(2,1)S(1)} %collective-permute-done.3.refs_1_), custom_call_target="tpu_custom_call" | custom-call | tf_op jit(solution)/shard_map/arrange_block/pallas_call | solution.py:202
  20.0 2.4 %choice_matrices.1 = (bf16[512,768]{1,0:T(8,128)(2,1)S(1)}, bf16[512,768]{1,0:T(8,128)(2,1)S(1)}) custom-call(s32[8,4,8]{2,1,0:T(4,128)S(1)} %copy-done.3), custom_call_target="tpu_custom_call" | custom-call | tf_op jit(solution)/shard_map/choice_matrices/pallas_call | solution.py:128
  22.4 1.8 %collective-permute-done.refs_5_ = bf16[8,2,16,512]{3,2,1,0:T(8,128)(2,1)S(1)} collective-permute-done((bf16[8,2,16,512]{3,2,1,0:T(8,128)(2,1)S(1)}, bf16[8,2,16,512]{3,2,1,0:T(8,128)(2,1)S(1)}, u32[]{:S(2)}, u32[]{:S(2)}) %collective-permute-start) | collective-permute-done | bytes 262176 | tf_op jit(solution)/shard_map/ppermute | solution.py:360
  24.2 5.1 %collective-permute-done.2.refs_6_ = bf16[8,2,16,512]{3,2,1,0:T(8,128)(2,1)S(1)} collective-permute-done((bf16[8,2,16,512]{3,2,1,0:T(8,128)(2,1)S(1)}, bf16[8,2,16,512]{3,2,1,0:T(8,128)(2,1)S(1)}, u32[]{:S(2)}, u32[]{:S(2)}) %collective-permute-start.2) | collective-permute-done | bytes 262176 | tf_op jit(solution)/shard_map/ppermute | solution.py:360
  29.8 1.6 %collective-permute-start.4 = (bf16[2,2,128,128]{3,2,1,0:T(8,128)(2,1)S(1)}, bf16[2,2,128,128]{3,2,1,0:T(8,128)(2,1)S(1)}, u32[]{:S(2)}, u32[]{:S(2)}) collective-permute-start(bf16[2,2,128,128]{3,2,1,0:T(8,128)(2,1)S(1)} %get-tuple-element.46), channel_id=1, source_target_pairs={{0,4},{4,0},{8,12},{12,8},{16,20},{20,16},{24,28},{28,24},{1,5},{5... | collective-permute-start | bytes 393224 | tf_op jit(solution)/shard_map/ppermute | solution.py:360
  32.0 1.3 %collective-permute-start.6 = (bf16[2,2,128,128]{3,2,1,0:T(8,128)(2,1)S(1)}, bf16[2,2,128,128]{3,2,1,0:T(8,128)(2,1)S(1)}, u32[]{:S(2)}, u32[]{:S(2)}) collective-permute-start(bf16[2,2,128,128]{3,2,1,0:T(8,128)(2,1)S(1)} %get-tuple-element.48), channel_id=1, source_target_pairs={{0,12},{4,8},{8,4},{12,0},{16,28},{20,24},{24,20},{28,16},{1,13},{... | collective-permute-start | bytes 393224 | tf_op jit(solution)/shard_map/ppermute | solution.py:360
  33.4 1.5 %collective-permute-start.11 = (bf16[2,2,128,128]{3,2,1,0:T(8,128)(2,1)S(1)}, bf16[2,2,128,128]{3,2,1,0:T(8,128)(2,1)S(1)}, u32[]{:S(2)}, u32[]{:S(2)}) collective-permute-start(bf16[2,2,128,128]{3,2,1,0:T(8,128)(2,1)S(1)} %get-tuple-element.56), channel_id=1, source_target_pairs={{0,4},{4,0},{8,12},{12,8},{16,20},{20,16},{24,28},{28,24},{1,5},{5... | collective-permute-start | bytes 393224 | tf_op jit(solution)/shard_map/ppermute | solution.py:360
  34.9 2.4 %collective-permute-done.9 = bf16[2,2,256,128]{3,2,1,0:T(8,128)(2,1)S(1)} collective-permute-done((bf16[2,2,256,128]{3,2,1,0:T(8,128)(2,1)S(1)}, bf16[2,2,256,128]{3,2,1,0:T(8,128)(2,1)S(1)}, u32[]{:S(2)}, u32[]{:S(2)}) %collective-permute-start.9) | collective-permute-done | bytes 262176 | tf_op jit(solution)/shard_map/ppermute | solution.py:360
  37.3 2.8 %collective-permute-done.4 = bf16[2,2,128,128]{3,2,1,0:T(8,128)(2,1)S(1)} collective-permute-done((bf16[2,2,128,128]{3,2,1,0:T(8,128)(2,1)S(1)}, bf16[2,2,128,128]{3,2,1,0:T(8,128)(2,1)S(1)}, u32[]{:S(2)}, u32[]{:S(2)}) %collective-permute-start.4) | collective-permute-done | bytes 131104 | tf_op jit(solution)/shard_map/ppermute | solution.py:360
  40.3 2.1 %contract_tiles.5 = (f32[64,1024]{1,0:T(8,128)S(1)}, f32[64,1024]{1,0:T(8,128)S(1)}, f32[64,1024]{1,0:T(8,128)S(1)}, f32[64,1024]{1,0:T(8,128)S(1)}) custom-call(bf16[8,2,16,512]{3,2,1,0:T(8,128)(2,1)S(1)} %get-tuple-element.33.refs_0_, bf16[8,2,16,512]{3,2,1,0:T(8,128)(2,1)S(1)} %collective-permute-done.1.refs_1_, ...), custom_call_target="tpu_custom_call" | custom-call | tf_op jit(solution)/shard_map/contract_tiles/pallas_call | solution.py:287
  42.9 0.8 %contract_tiles.7 = s16[64,1152]{1,0:T(8,128)(2,1)S(1)} custom-call(bf16[2,2,4,2,16,128]{5,4,3,2,1,0:T(8,128)(2,1)S(1)} %bitcast.20, bf16[2,2,4,2,16,128]{5,4,3,2,1,0:T(8,128)(2,1)S(1)} %bitcast.22, bf16[2,2,4,2,16,128]{5,4,3,2,1,0:T(8,128)(2,1)S(1)} %bitcast.24, bf16[1536,1024]{1,0:T(8,128)(2,1)S(1)} %get-tuple-element.49.refs_3_, ...), custom_call_target="tpu_custom_call" | custom-call | tf_op jit(solution)/shard_map/contract_tiles/pallas_call | solution.py:287
  43.7 1.6 %collective-permute-start.10 = (s16[64,1152]{1,0:T(8,128)(2,1)S(1)}, s16[64,1152]{1,0:T(8,128)(2,1)S(1)}, u32[]{:S(2)}, u32[]{:S(2)}) collective-permute-start(s16[64,1152]{1,0:T(8,128)(2,1)S(1)} %contract_tiles.7), channel_id=1, source_target_pairs={{0,2},{1,3},{2,0},{3,1},{4,6},{5,7},{6,4},{7,5},{8,10},{9,11},{10,... | collective-permute-start | bytes 442376 | tf_op jit(solution)/shard_map/ppermute | solution.py:360
  45.3 1.8 %collective-permute-done.13 = bf16[2,2,128,128]{3,2,1,0:T(8,128)(2,1)S(1)} collective-permute-done((bf16[2,2,128,128]{3,2,1,0:T(8,128)(2,1)S(1)}, bf16[2,2,128,128]{3,2,1,0:T(8,128)(2,1)S(1)}, u32[]{:S(2)}, u32[]{:S(2)}) %collective-permute-start.13) | collective-permute-done | bytes 131104 | tf_op jit(solution)/shard_map/ppermute | solution.py:360
  48.0 1.6 %collective-permute-start.14 = (s16[64,1152]{1,0:T(8,128)(2,1)S(1)}, s16[64,1152]{1,0:T(8,128)(2,1)S(1)}, u32[]{:S(2)}, u32[]{:S(2)}) collective-permute-start(s16[64,1152]{1,0:T(8,128)(2,1)S(1)} %contract_tiles.9), channel_id=1, source_target_pairs={{0,2},{1,3},{2,0},{3,1},{4,6},{5,7},{6,4},{7,5},{8,10},{9,11},{10,... | collective-permute-start | bytes 442376 | tf_op jit(solution)/shard_map/ppermute | solution.py:360
  50.9 2.3 %collective-permute-done.14.refs_3_ = s16[64,1152]{1,0:T(8,128)(2,1)S(1)} collective-permute-done((s16[64,1152]{1,0:T(8,128)(2,1)S(1)}, s16[64,1152]{1,0:T(8,128)(2,1)S(1)}, u32[]{:S(2)}, u32[]{:S(2)}) %collective-permute-start.14) | collective-permute-done | bytes 147488 | tf_op jit(solution)/shard_map/ppermute | solution.py:360
  53.3 12.5 %all_to_all.5.received = bf16[8,16,1024]{2,1,0:T(8,128)(2,1)S(1)} all-to-all(bf16[8,16,1024]{2,1,0:T(8,128)(2,1)S(1)} %bitcast.17), channel_id=1, replica_groups=mesh['col'=8,'row'=4] {'col'}, dimensions={0} | all-to-all | bytes 524288 | tf_op jit(solution)/shard_map/all_to_all | solution.py:422
  65.9 1.7 %reorder_tiles.1 = bf16[16,8192]{1,0:T(8,128)(2,1)} custom-call(s32[64]{0:T(128)S(1)} %copy-done.4, bf16[8,16,1024]{2,1,0:T(8,128)(2,1)S(1)} %all_to_all.5.received), custom_call_target="tpu_custom_call" | custom-call | tf_op jit(solution)/shard_map/reorder_tiles/pallas_call | solution.py:349
  (29 shorter events, 6.6 us)
Async XLA Ops:
  0.0 13.9 %collective-permute-start.3 = (bf16[1024,1024]{1,0:T(8,128)(2,1)}, bf16[1024,1024]{1,0:T(8,128)(2,1)S(1)}, u32[]{:S(2)}, u32[]{:S(2)}) collective-permute-start(bf16[1024,1024]{1,0:T(8,128)(2,1)} %refs_0_.1), channel_id=1, source_target_pairs={{0,1},{1,0},{2,3},{3,2},{4,5},{5,4},{6,7},{7,6},{8,9},{9,8},{10,11... | collective-permute-start | bytes 6291464 | tf_op jit(solution)/shard_map/ppermute | solution.py:360
  0.5 1.0 %copy-start.1 = (bf16[512,512]{1,0:T(8,128)(2,1)S(1)}, bf16[512,512]{1,0:T(8,128)(2,1)}, u32[]{:S(2)}) copy-start(bf16[512,512]{1,0:T(8,128)(2,1)} %param.4) | copy-start | bytes 1572868
  1.6 4.2 %collective-permute-start.1 = (bf16[8,2,16,512]{3,2,1,0:T(8,128)(2,1)S(1)}, bf16[8,2,16,512]{3,2,1,0:T(8,128)(2,1)S(1)}, u32[]{:S(2)}, u32[]{:S(2)}) collective-permute-start(bf16[8,2,16,512]{3,2,1,0:T(8,128)(2,1)S(1)} %get-tuple-element.34), channel_id=1, source_target_pairs={{0,1},{1,0},{2,3},{3,2},{4,5},{5,4},{6,7},{7,6},{8,9},{9,8},{10,11... | collective-permute-start | bytes 786440 | tf_op jit(solution)/shard_map/ppermute | solution.py:360
  1.7 22.5 %collective-permute-start = (bf16[8,2,16,512]{3,2,1,0:T(8,128)(2,1)S(1)}, bf16[8,2,16,512]{3,2,1,0:T(8,128)(2,1)S(1)}, u32[]{:S(2)}, u32[]{:S(2)}) collective-permute-start(bf16[8,2,16,512]{3,2,1,0:T(8,128)(2,1)S(1)} %get-tuple-element.33.refs_0_), channel_id=1, source_target_pairs={{0,16},{4,20},{8,24},{12,28},{16,0},{20,4},{24,8},{28,12},{1,17},{... | collective-permute-start | bytes 786440 | tf_op jit(solution)/shard_map/ppermute | solution.py:360
  5.7 23.5 %collective-permute-start.2 = (bf16[8,2,16,512]{3,2,1,0:T(8,128)(2,1)S(1)}, bf16[8,2,16,512]{3,2,1,0:T(8,128)(2,1)S(1)}, u32[]{:S(2)}, u32[]{:S(2)}) collective-permute-start(bf16[8,2,16,512]{3,2,1,0:T(8,128)(2,1)S(1)} %collective-permute-done.1.refs_1_), channel_id=1, source_target_pairs={{0,16},{4,20},{8,24},{12,28},{16,0},{20,4},{24,8},{28,12},{1,17},{... | collective-permute-start | bytes 786440 | tf_op jit(solution)/shard_map/ppermute | solution.py:360
  8.6 0.7 %copy-start.2 = (s32[8,4,8]{2,1,0:T(4,128)S(1)}, s32[8,4,8]{2,1,0:T(4,128)}, u32[]{:S(2)}) copy-start(s32[8,4,8]{2,1,0:T(4,128)} %wanted.4) | copy-start | bytes 3076
  10.8 21.2 %collective-permute-start.7 = (bf16[2,2,256,128]{3,2,1,0:T(8,128)(2,1)S(1)}, bf16[2,2,256,128]{3,2,1,0:T(8,128)(2,1)S(1)}, u32[]{:S(2)}, u32[]{:S(2)}) collective-permute-start(bf16[2,2,256,128]{3,2,1,0:T(8,128)(2,1)S(1)} %get-tuple-element.50), channel_id=1, source_target_pairs={{0,4},{4,0},{8,12},{12,8},{16,20},{20,16},{24,28},{28,24},{1,5},{5... | collective-permute-start | bytes 786440 | tf_op jit(solution)/shard_map/ppermute | solution.py:360
  12.4 21.0 %collective-permute-start.8 = (bf16[2,2,256,128]{3,2,1,0:T(8,128)(2,1)S(1)}, bf16[2,2,256,128]{3,2,1,0:T(8,128)(2,1)S(1)}, u32[]{:S(2)}, u32[]{:S(2)}) collective-permute-start(bf16[2,2,256,128]{3,2,1,0:T(8,128)(2,1)S(1)} %get-tuple-element.51), channel_id=1, source_target_pairs={{0,8},{4,12},{8,0},{12,4},{16,24},{20,28},{24,16},{28,20},{1,9},{5... | collective-permute-start | bytes 786440 | tf_op jit(solution)/shard_map/ppermute | solution.py:360
  13.9 23.4 %collective-permute-start.9 = (bf16[2,2,256,128]{3,2,1,0:T(8,128)(2,1)S(1)}, bf16[2,2,256,128]{3,2,1,0:T(8,128)(2,1)S(1)}, u32[]{:S(2)}, u32[]{:S(2)}) collective-permute-start(bf16[2,2,256,128]{3,2,1,0:T(8,128)(2,1)S(1)} %get-tuple-element.52), channel_id=1, source_target_pairs={{0,12},{4,8},{8,4},{12,0},{16,28},{20,24},{24,20},{28,16},{1,13},{... | collective-permute-start | bytes 786440 | tf_op jit(solution)/shard_map/ppermute | solution.py:360
  14.4 1.6 %copy-start = (bf16[1024,1024]{1,0:T(8,128)(2,1)S(1)}, bf16[1024,1024]{1,0:T(8,128)(2,1)}, u32[]{:S(2)}) copy-start(bf16[1024,1024]{1,0:T(8,128)(2,1)} %refs_0_.1) | copy-start | bytes 6291460
  15.9 0.7 %copy-start.3 = (s32[8,4,8]{2,1,0:T(4,128)S(1)}, s32[8,4,8]{2,1,0:T(4,128)}, u32[]{:S(2)}) copy-start(s32[8,4,8]{2,1,0:T(4,128)} %wanted.4) | copy-start | bytes 3076
  29.8 10.4 %collective-permute-start.4 = (bf16[2,2,128,128]{3,2,1,0:T(8,128)(2,1)S(1)}, bf16[2,2,128,128]{3,2,1,0:T(8,128)(2,1)S(1)}, u32[]{:S(2)}, u32[]{:S(2)}) collective-permute-start(bf16[2,2,128,128]{3,2,1,0:T(8,128)(2,1)S(1)} %get-tuple-element.46), channel_id=1, source_target_pairs={{0,4},{4,0},{8,12},{12,8},{16,20},{20,16},{24,28},{28,24},{1,5},{5... | collective-permute-start | bytes 393224 | tf_op jit(solution)/shard_map/ppermute | solution.py:360
  31.4 10.9 %collective-permute-start.5 = (bf16[2,2,128,128]{3,2,1,0:T(8,128)(2,1)S(1)}, bf16[2,2,128,128]{3,2,1,0:T(8,128)(2,1)S(1)}, u32[]{:S(2)}, u32[]{:S(2)}) collective-permute-start(bf16[2,2,128,128]{3,2,1,0:T(8,128)(2,1)S(1)} %get-tuple-element.47), channel_id=1, source_target_pairs={{0,8},{4,12},{8,0},{12,4},{16,24},{20,28},{24,16},{28,20},{1,9},{5... | collective-permute-start | bytes 393224 | tf_op jit(solution)/shard_map/ppermute | solution.py:360
  32.0 10.9 %collective-permute-start.6 = (bf16[2,2,128,128]{3,2,1,0:T(8,128)(2,1)S(1)}, bf16[2,2,128,128]{3,2,1,0:T(8,128)(2,1)S(1)}, u32[]{:S(2)}, u32[]{:S(2)}) collective-permute-start(bf16[2,2,128,128]{3,2,1,0:T(8,128)(2,1)S(1)} %get-tuple-element.48), channel_id=1, source_target_pairs={{0,12},{4,8},{8,4},{12,0},{16,28},{20,24},{24,20},{28,16},{1,13},{... | collective-permute-start | bytes 393224 | tf_op jit(solution)/shard_map/ppermute | solution.py:360
  33.4 12.0 %collective-permute-start.11 = (bf16[2,2,128,128]{3,2,1,0:T(8,128)(2,1)S(1)}, bf16[2,2,128,128]{3,2,1,0:T(8,128)(2,1)S(1)}, u32[]{:S(2)}, u32[]{:S(2)}) collective-permute-start(bf16[2,2,128,128]{3,2,1,0:T(8,128)(2,1)S(1)} %get-tuple-element.56), channel_id=1, source_target_pairs={{0,4},{4,0},{8,12},{12,8},{16,20},{20,16},{24,28},{28,24},{1,5},{5... | collective-permute-start | bytes 393224 | tf_op jit(solution)/shard_map/ppermute | solution.py:360
  37.3 8.0 %collective-permute-start.12 = (bf16[2,2,128,128]{3,2,1,0:T(8,128)(2,1)S(1)}, bf16[2,2,128,128]{3,2,1,0:T(8,128)(2,1)S(1)}, u32[]{:S(2)}, u32[]{:S(2)}) collective-permute-start(bf16[2,2,128,128]{3,2,1,0:T(8,128)(2,1)S(1)} %get-tuple-element.57), channel_id=1, source_target_pairs={{0,8},{4,12},{8,0},{12,4},{16,24},{20,28},{24,16},{28,20},{1,9},{5... | collective-permute-start | bytes 393224 | tf_op jit(solution)/shard_map/ppermute | solution.py:360
  40.2 7.0 %collective-permute-start.13 = (bf16[2,2,128,128]{3,2,1,0:T(8,128)(2,1)S(1)}, bf16[2,2,128,128]{3,2,1,0:T(8,128)(2,1)S(1)}, u32[]{:S(2)}, u32[]{:S(2)}) collective-permute-start(bf16[2,2,128,128]{3,2,1,0:T(8,128)(2,1)S(1)} %get-tuple-element.58), channel_id=1, source_target_pairs={{0,12},{4,8},{8,4},{12,0},{16,28},{20,24},{24,20},{28,16},{1,13},{... | collective-permute-start | bytes 393224 | tf_op jit(solution)/shard_map/ppermute | solution.py:360
  43.7 7.1 %collective-permute-start.10 = (s16[64,1152]{1,0:T(8,128)(2,1)S(1)}, s16[64,1152]{1,0:T(8,128)(2,1)S(1)}, u32[]{:S(2)}, u32[]{:S(2)}) collective-permute-start(s16[64,1152]{1,0:T(8,128)(2,1)S(1)} %contract_tiles.7), channel_id=1, source_target_pairs={{0,2},{1,3},{2,0},{3,1},{4,6},{5,7},{6,4},{7,5},{8,10},{9,11},{10,... | collective-permute-start | bytes 442376 | tf_op jit(solution)/shard_map/ppermute | solution.py:360
  48.0 5.2 %collective-permute-start.14 = (s16[64,1152]{1,0:T(8,128)(2,1)S(1)}, s16[64,1152]{1,0:T(8,128)(2,1)S(1)}, u32[]{:S(2)}, u32[]{:S(2)}) collective-permute-start(s16[64,1152]{1,0:T(8,128)(2,1)S(1)} %contract_tiles.9), channel_id=1, source_target_pairs={{0,2},{1,3},{2,0},{3,1},{4,6},{5,7},{6,4},{7,5},{8,10},{9,11},{10,... | collective-permute-start | bytes 442376 | tf_op jit(solution)/shard_map/ppermute | solution.py:360
  50.2 15.7 %copy-start.4 = (s32[64]{0:T(128)S(1)}, s32[64]{0:T(128)}, u32[]{:S(2)}) copy-start(s32[64]{0:T(128)} %owner.1) | copy-start | bytes 772

commit v4 on v3

--- a/solution.py
+++ b/solution.py
@@ -396,7 +396,7 @@
     blocks = arrange(wanted, [integrals, swap(integrals, "row", 1)], per_source, top)
     late_wanted, *blocks = lax.optimization_barrier((wanted, *blocks))
     choices = choice(late_wanted, per_source, top, low, amplitudes.dtype)
-    *mirrors, early_block, far_block, choices = lax.optimization_barrier((*mirrors, *blocks, choices))
+    *mirrors, early_block, far_block, choices, nearby[1] = lax.optimization_barrier((*mirrors, *blocks, choices, nearby[1]))
     mirrors = [whole(x) for x in mirrors]
     height = ys * b
     passed = pass_on([flat(x) for x in mirrors], choices, [(lo * height, hi * height) for lo, hi in bounds])

time: 67.9 us -> 66.9 us (0.985)
  blocking collectives: 12.5 us -> 11.7 us
    all_to_all x1, blocking collectives: 12.5 us -> 11.7 us  [body(): lax.all_to_all(held, 'col', split_axis=0, concat_axis=0, tiled=True)]
  transfers between devices with their start and end apart: 15 -> 15, of which waited for: 7 -> 9; matrix products, arithmetic and copies ran while one was open for 0% -> 0% of each run, Pallas kernels for 19% -> 19%
where the time goes in v4:
time: 66.9 us; the launch traced here: 66.5 us
  starting transfers between devices  19.3 us (29%)
  waiting for transfers between devices  16.6 us (25%)
  Pallas kernels  14.7 us (22%)
  blocking collectives  11.7 us (17%)
  local copies, waits for them, and re-layouts  4.07 us (6%)
    ppermute x15, starting transfers between devices, swap(): lax.ppermute(x, axis, [(i, i ^ flip) for i in range(lax.axis_size(axis))])  19.3 us
    ppermute x15, waiting for transfers between devices, swap(): lax.ppermute(x, axis, [(i, i ^ flip) for i in range(lax.axis_size(axis))])  16.6 us
    all_to_all x1, blocking collectives, body(): lax.all_to_all(held, 'col', split_axis=0, concat_axis=0, tiled=True)  11.7 us
    pallas_call x5, Pallas kernels, contract(): pl.pallas_call(functools.partial(contract_kernel, len(sources), pieces, c...  5.03 us
    unnamed x10, local copies, waits for them, and re-layouts  4.07 us
    pallas_call x1, Pallas kernels, arrange(): pl.pallas_call(functools.partial(arrange_kernel, per_source, top), grid=(...  3.33 us
    pallas_call x1, Pallas kernels, choice(): pl.pallas_call(functools.partial(choice_kernel, per_source, away, flips),...  2.35 us
    pallas_call x1, Pallas kernels, reorder(): pl.pallas_call(functools.partial(reorder_kernel, width // TILE), out_shap...  1.68 us
  transfers between devices with their start and end apart: 15, of which 9 were waited for; matrix products, arithmetic and copies ran while one was open for 0% of the time, Pallas kernels for 19%

profile of v4, /device:TPU:0, one launch (start us, length us, event | category | flops | bytes accessed | tf_op | source)
XLA Modules:
  0.0 66.5 jit_solution(1449935306533463947)
XLA Ops:
  0.5 1.0 %copy-done.1 = bf16[512,512]{1,0:T(8,128)(2,1)S(1)} copy-done((bf16[512,512]{1,0:T(8,128)(2,1)S(1)}, bf16[512,512]{1,0:T(8,128)(2,1)}, u32[]{:S(2)}) %copy-start.1) | copy-done | bytes 524312
  1.7 4.0 %collective-permute-start = (bf16[8,2,16,512]{3,2,1,0:T(8,128)(2,1)S(1)}, bf16[8,2,16,512]{3,2,1,0:T(8,128)(2,1)S(1)}, u32[]{:S(2)}, u32[]{:S(2)}) collective-permute-start(bf16[8,2,16,512]{3,2,1,0:T(8,128)(2,1)S(1)} %get-tuple-element.34.refs_0_), channel_id=1, source_target_pairs={{0,16},{4,20},{8,24},{12,28},{16,0},{20,4},{24,8},{28,12},{1,17},{... | collective-permute-start | bytes 786440 | tf_op jit(solution)/shard_map/ppermute | solution.py:360
  6.4 1.5 %select_tiles.1 = (bf16[2,2,256,128]{3,2,1,0:T(8,128)(2,1)S(1)}, bf16[2,2,256,128]{3,2,1,0:T(8,128)(2,1)S(1)}, bf16[2,2,256,128]{3,2,1,0:T(8,128)(2,1)S(1)}) custom-call(s32[8,4,8]{2,1,0:T(4,128)S(1)} %copy-done.2, bf16[256,512]{1,0:T(8,128)(2,1)S(1)} %bitcast.15, bf16[256,512]{1,0:T(8,128)(2,1)S(1)} %bitcast.16), custom_call_target="tpu_custom_call" | custom-call | tf_op jit(solution)/shard_map/select_tiles/pallas_call | solution.py:89
  7.9 2.9 %collective-permute-start.2 = (bf16[8,2,16,512]{3,2,1,0:T(8,128)(2,1)S(1)}, bf16[8,2,16,512]{3,2,1,0:T(8,128)(2,1)S(1)}, u32[]{:S(2)}, u32[]{:S(2)}) collective-permute-start(bf16[8,2,16,512]{3,2,1,0:T(8,128)(2,1)S(1)} %collective-permute-done.1.refs_1_), channel_id=1, source_target_pairs={{0,16},{4,20},{8,24},{12,28},{16,0},{20,4},{24,8},{28,12},{1,17},{... | collective-permute-start | bytes 786440 | tf_op jit(solution)/shard_map/ppermute | solution.py:360
  10.9 1.6 %collective-permute-start.4 = (bf16[2,2,256,128]{3,2,1,0:T(8,128)(2,1)S(1)}, bf16[2,2,256,128]{3,2,1,0:T(8,128)(2,1)S(1)}, u32[]{:S(2)}, u32[]{:S(2)}) collective-permute-start(bf16[2,2,256,128]{3,2,1,0:T(8,128)(2,1)S(1)} %get-tuple-element.43), channel_id=1, source_target_pairs={{0,8},{4,12},{8,0},{12,4},{16,24},{20,28},{24,16},{28,20},{1,9},{5... | collective-permute-start | bytes 786440 | tf_op jit(solution)/shard_map/ppermute | solution.py:360
  12.4 1.5 %collective-permute-start.8 = (bf16[2,2,256,128]{3,2,1,0:T(8,128)(2,1)S(1)}, bf16[2,2,256,128]{3,2,1,0:T(8,128)(2,1)S(1)}, u32[]{:S(2)}, u32[]{:S(2)}) collective-permute-start(bf16[2,2,256,128]{3,2,1,0:T(8,128)(2,1)S(1)} %get-tuple-element.52), channel_id=1, source_target_pairs={{0,4},{4,0},{8,12},{12,8},{16,20},{20,16},{24,28},{28,24},{1,5},{5... | collective-permute-start | bytes 786440 | tf_op jit(solution)/shard_map/ppermute | solution.py:360
  14.4 1.6 %copy-done = bf16[1024,1024]{1,0:T(8,128)(2,1)S(1)} copy-done((bf16[1024,1024]{1,0:T(8,128)(2,1)S(1)}, bf16[1024,1024]{1,0:T(8,128)(2,1)}, u32[]{:S(2)}) %copy-start) | copy-done | bytes 2097176
  16.7 3.3 %arrange_block.1 = (bf16[3584,1024]{1,0:T(8,128)(2,1)S(1)}, bf16[1536,1024]{1,0:T(8,128)(2,1)S(1)}) custom-call(s32[8,4,8]{2,1,0:T(4,128)S(1)} %copy-done.3, bf16[1024,1024]{1,0:T(8,128)(2,1)S(1)} %copy-done, bf16[1024,1024]{1,0:T(8,128)(2,1)S(1)} %collective-permute-done.3.refs_1_), custom_call_target="tpu_custom_call" | custom-call | tf_op jit(solution)/shard_map/arrange_block/pallas_call | solution.py:202
  20.0 2.3 %choice_matrices.1 = (bf16[512,768]{1,0:T(8,128)(2,1)S(1)}, bf16[512,768]{1,0:T(8,128)(2,1)S(1)}) custom-call(s32[8,4,8]{2,1,0:T(4,128)S(1)} %copy-done.3), custom_call_target="tpu_custom_call" | custom-call | tf_op jit(solution)/shard_map/choice_matrices/pallas_call | solution.py:128
  22.4 1.8 %collective-permute-done.refs_5_ = bf16[8,2,16,512]{3,2,1,0:T(8,128)(2,1)S(1)} collective-permute-done((bf16[8,2,16,512]{3,2,1,0:T(8,128)(2,1)S(1)}, bf16[8,2,16,512]{3,2,1,0:T(8,128)(2,1)S(1)}, u32[]{:S(2)}, u32[]{:S(2)}) %collective-permute-start) | collective-permute-done | bytes 262176 | tf_op jit(solution)/shard_map/ppermute | solution.py:360
  24.2 5.1 %collective-permute-done.2.refs_6_ = bf16[8,2,16,512]{3,2,1,0:T(8,128)(2,1)S(1)} collective-permute-done((bf16[8,2,16,512]{3,2,1,0:T(8,128)(2,1)S(1)}, bf16[8,2,16,512]{3,2,1,0:T(8,128)(2,1)S(1)}, u32[]{:S(2)}, u32[]{:S(2)}) %collective-permute-start.2) | collective-permute-done | bytes 262176 | tf_op jit(solution)/shard_map/ppermute | solution.py:360
  29.2 0.9 %collective-permute-done.4 = bf16[2,2,256,128]{3,2,1,0:T(8,128)(2,1)S(1)} collective-permute-done((bf16[2,2,256,128]{3,2,1,0:T(8,128)(2,1)S(1)}, bf16[2,2,256,128]{3,2,1,0:T(8,128)(2,1)S(1)}, u32[]{:S(2)}, u32[]{:S(2)}) %collective-permute-start.4) | collective-permute-done | bytes 262176 | tf_op jit(solution)/shard_map/ppermute | solution.py:360
  30.7 1.6 %collective-permute-start.11 = (bf16[2,2,128,128]{3,2,1,0:T(8,128)(2,1)S(1)}, bf16[2,2,128,128]{3,2,1,0:T(8,128)(2,1)S(1)}, u32[]{:S(2)}, u32[]{:S(2)}) collective-permute-start(bf16[2,2,128,128]{3,2,1,0:T(8,128)(2,1)S(1)} %get-tuple-element.58), channel_id=1, source_target_pairs={{0,4},{4,0},{8,12},{12,8},{16,20},{20,16},{24,28},{28,24},{1,5},{5... | collective-permute-start | bytes 393224 | tf_op jit(solution)/shard_map/ppermute | solution.py:360
  32.3 1.9 %collective-permute-start.13 = (bf16[2,2,128,128]{3,2,1,0:T(8,128)(2,1)S(1)}, bf16[2,2,128,128]{3,2,1,0:T(8,128)(2,1)S(1)}, u32[]{:S(2)}, u32[]{:S(2)}) collective-permute-start(bf16[2,2,128,128]{3,2,1,0:T(8,128)(2,1)S(1)} %get-tuple-element.60), channel_id=1, source_target_pairs={{0,12},{4,8},{8,4},{12,0},{16,28},{20,24},{24,20},{28,16},{1,13},{... | collective-permute-start | bytes 393224 | tf_op jit(solution)/shard_map/ppermute | solution.py:360
  34.3 1.5 %collective-permute-start.5 = (bf16[2,2,128,128]{3,2,1,0:T(8,128)(2,1)S(1)}, bf16[2,2,128,128]{3,2,1,0:T(8,128)(2,1)S(1)}, u32[]{:S(2)}, u32[]{:S(2)}) collective-permute-start(bf16[2,2,128,128]{3,2,1,0:T(8,128)(2,1)S(1)} %get-tuple-element.48), channel_id=1, source_target_pairs={{0,4},{4,0},{8,12},{12,8},{16,20},{20,16},{24,28},{28,24},{1,5},{5... | collective-permute-start | bytes 393224 | tf_op jit(solution)/shard_map/ppermute | solution.py:360
  35.8 1.0 %collective-permute-done.9 = bf16[2,2,256,128]{3,2,1,0:T(8,128)(2,1)S(1)} collective-permute-done((bf16[2,2,256,128]{3,2,1,0:T(8,128)(2,1)S(1)}, bf16[2,2,256,128]{3,2,1,0:T(8,128)(2,1)S(1)}, u32[]{:S(2)}, u32[]{:S(2)}) %collective-permute-start.9) | collective-permute-done | bytes 262176 | tf_op jit(solution)/shard_map/ppermute | solution.py:360
  36.8 2.9 %collective-permute-done.11 = bf16[2,2,128,128]{3,2,1,0:T(8,128)(2,1)S(1)} collective-permute-done((bf16[2,2,128,128]{3,2,1,0:T(8,128)(2,1)S(1)}, bf16[2,2,128,128]{3,2,1,0:T(8,128)(2,1)S(1)}, u32[]{:S(2)}, u32[]{:S(2)}) %collective-permute-start.11) | collective-permute-done | bytes 131104 | tf_op jit(solution)/shard_map/ppermute | solution.py:360
  39.6 2.1 %contract_tiles.5 = (f32[64,1024]{1,0:T(8,128)S(1)}, f32[64,1024]{1,0:T(8,128)S(1)}, f32[64,1024]{1,0:T(8,128)S(1)}, f32[64,1024]{1,0:T(8,128)S(1)}) custom-call(bf16[8,2,16,512]{3,2,1,0:T(8,128)(2,1)S(1)} %get-tuple-element.34.refs_0_, bf16[8,2,16,512]{3,2,1,0:T(8,128)(2,1)S(1)} %collective-permute-done.1.refs_1_, ...), custom_call_target="tpu_custom_call" | custom-call | tf_op jit(solution)/shard_map/contract_tiles/pallas_call | solution.py:287
  43.2 1.6 %collective-permute-start.14 = (s16[64,1152]{1,0:T(8,128)(2,1)S(1)}, s16[64,1152]{1,0:T(8,128)(2,1)S(1)}, u32[]{:S(2)}, u32[]{:S(2)}) collective-permute-start(s16[64,1152]{1,0:T(8,128)(2,1)S(1)} %contract_tiles.9), channel_id=1, source_target_pairs={{0,2},{1,3},{2,0},{3,1},{4,6},{5,7},{6,4},{7,5},{8,10},{9,11},{10,... | collective-permute-start | bytes 442376 | tf_op jit(solution)/shard_map/ppermute | solution.py:360
  45.1 1.8 %collective-permute-done.7 = bf16[2,2,128,128]{3,2,1,0:T(8,128)(2,1)S(1)} collective-permute-done((bf16[2,2,128,128]{3,2,1,0:T(8,128)(2,1)S(1)}, bf16[2,2,128,128]{3,2,1,0:T(8,128)(2,1)S(1)}, u32[]{:S(2)}, u32[]{:S(2)}) %collective-permute-start.7) | collective-permute-done | bytes 131104 | tf_op jit(solution)/shard_map/ppermute | solution.py:360
  47.7 1.6 %collective-permute-start.10 = (s16[64,1152]{1,0:T(8,128)(2,1)S(1)}, s16[64,1152]{1,0:T(8,128)(2,1)S(1)}, u32[]{:S(2)}, u32[]{:S(2)}) collective-permute-start(s16[64,1152]{1,0:T(8,128)(2,1)S(1)} %contract_tiles.7), channel_id=1, source_target_pairs={{0,2},{1,3},{2,0},{3,1},{4,6},{5,7},{6,4},{7,5},{8,10},{9,11},{10,... | collective-permute-start | bytes 442376 | tf_op jit(solution)/shard_map/ppermute | solution.py:360
  50.6 2.3 %collective-permute-done.10.refs_1_ = s16[64,1152]{1,0:T(8,128)(2,1)S(1)} collective-permute-done((s16[64,1152]{1,0:T(8,128)(2,1)S(1)}, s16[64,1152]{1,0:T(8,128)(2,1)S(1)}, u32[]{:S(2)}, u32[]{:S(2)}) %collective-permute-start.10) | collective-permute-done | bytes 147488 | tf_op jit(solution)/shard_map/ppermute | solution.py:360
  53.1 11.7 %all_to_all.5.received = bf16[8,16,1024]{2,1,0:T(8,128)(2,1)S(1)} all-to-all(bf16[8,16,1024]{2,1,0:T(8,128)(2,1)S(1)} %bitcast.17), channel_id=1, replica_groups=mesh['col'=8,'row'=4] {'col'}, dimensions={0} | all-to-all | bytes 524288 | tf_op jit(solution)/shard_map/all_to_all | solution.py:422
  64.8 1.7 %reorder_tiles.1 = bf16[16,8192]{1,0:T(8,128)(2,1)} custom-call(s32[64]{0:T(128)S(1)} %copy-done.4, bf16[8,16,1024]{2,1,0:T(8,128)(2,1)S(1)} %all_to_all.5.received), custom_call_target="tpu_custom_call" | custom-call | tf_op jit(solution)/shard_map/reorder_tiles/pallas_call | solution.py:349
  (29 shorter events, 7.2 us)
Async XLA Ops:
  0.0 13.9 %collective-permute-start.3 = (bf16[1024,1024]{1,0:T(8,128)(2,1)}, bf16[1024,1024]{1,0:T(8,128)(2,1)S(1)}, u32[]{:S(2)}, u32[]{:S(2)}) collective-permute-start(bf16[1024,1024]{1,0:T(8,128)(2,1)} %refs_0_.1), channel_id=1, source_target_pairs={{0,1},{1,0},{2,3},{3,2},{4,5},{5,4},{6,7},{7,6},{8,9},{9,8},{10,11... | collective-permute-start | bytes 6291464 | tf_op jit(solution)/shard_map/ppermute | solution.py:360
  0.5 1.0 %copy-start.1 = (bf16[512,512]{1,0:T(8,128)(2,1)S(1)}, bf16[512,512]{1,0:T(8,128)(2,1)}, u32[]{:S(2)}) copy-start(bf16[512,512]{1,0:T(8,128)(2,1)} %param.4) | copy-start | bytes 1572868
  1.6 4.2 %collective-permute-start.1 = (bf16[8,2,16,512]{3,2,1,0:T(8,128)(2,1)S(1)}, bf16[8,2,16,512]{3,2,1,0:T(8,128)(2,1)S(1)}, u32[]{:S(2)}, u32[]{:S(2)}) collective-permute-start(bf16[8,2,16,512]{3,2,1,0:T(8,128)(2,1)S(1)} %get-tuple-element.35), channel_id=1, source_target_pairs={{0,1},{1,0},{2,3},{3,2},{4,5},{5,4},{6,7},{7,6},{8,9},{9,8},{10,11... | collective-permute-start | bytes 786440 | tf_op jit(solution)/shard_map/ppermute | solution.py:360
  1.7 22.5 %collective-permute-start = (bf16[8,2,16,512]{3,2,1,0:T(8,128)(2,1)S(1)}, bf16[8,2,16,512]{3,2,1,0:T(8,128)(2,1)S(1)}, u32[]{:S(2)}, u32[]{:S(2)}) collective-permute-start(bf16[8,2,16,512]{3,2,1,0:T(8,128)(2,1)S(1)} %get-tuple-element.34.refs_0_), channel_id=1, source_target_pairs={{0,16},{4,20},{8,24},{12,28},{16,0},{20,4},{24,8},{28,12},{1,17},{... | collective-permute-start | bytes 786440 | tf_op jit(solution)/shard_map/ppermute | solution.py:360
  5.7 0.7 %copy-start.2 = (s32[8,4,8]{2,1,0:T(4,128)S(1)}, s32[8,4,8]{2,1,0:T(4,128)}, u32[]{:S(2)}) copy-start(s32[8,4,8]{2,1,0:T(4,128)} %wanted.4) | copy-start | bytes 3076
  7.9 21.3 %collective-permute-start.2 = (bf16[8,2,16,512]{3,2,1,0:T(8,128)(2,1)S(1)}, bf16[8,2,16,512]{3,2,1,0:T(8,128)(2,1)S(1)}, u32[]{:S(2)}, u32[]{:S(2)}) collective-permute-start(bf16[8,2,16,512]{3,2,1,0:T(8,128)(2,1)S(1)} %collective-permute-done.1.refs_1_), channel_id=1, source_target_pairs={{0,16},{4,20},{8,24},{12,28},{16,0},{20,4},{24,8},{28,12},{1,17},{... | collective-permute-start | bytes 786440 | tf_op jit(solution)/shard_map/ppermute | solution.py:360
  10.9 19.3 %collective-permute-start.4 = (bf16[2,2,256,128]{3,2,1,0:T(8,128)(2,1)S(1)}, bf16[2,2,256,128]{3,2,1,0:T(8,128)(2,1)S(1)}, u32[]{:S(2)}, u32[]{:S(2)}) collective-permute-start(bf16[2,2,256,128]{3,2,1,0:T(8,128)(2,1)S(1)} %get-tuple-element.43), channel_id=1, source_target_pairs={{0,8},{4,12},{8,0},{12,4},{16,24},{20,28},{24,16},{28,20},{1,9},{5... | collective-permute-start | bytes 786440 | tf_op jit(solution)/shard_map/ppermute | solution.py:360
  12.4 21.8 %collective-permute-start.8 = (bf16[2,2,256,128]{3,2,1,0:T(8,128)(2,1)S(1)}, bf16[2,2,256,128]{3,2,1,0:T(8,128)(2,1)S(1)}, u32[]{:S(2)}, u32[]{:S(2)}) collective-permute-start(bf16[2,2,256,128]{3,2,1,0:T(8,128)(2,1)S(1)} %get-tuple-element.52), channel_id=1, source_target_pairs={{0,4},{4,0},{8,12},{12,8},{16,20},{20,16},{24,28},{28,24},{1,5},{5... | collective-permute-start | bytes 786440 | tf_op jit(solution)/shard_map/ppermute | solution.py:360
  13.9 22.8 %collective-permute-start.9 = (bf16[2,2,256,128]{3,2,1,0:T(8,128)(2,1)S(1)}, bf16[2,2,256,128]{3,2,1,0:T(8,128)(2,1)S(1)}, u32[]{:S(2)}, u32[]{:S(2)}) collective-permute-start(bf16[2,2,256,128]{3,2,1,0:T(8,128)(2,1)S(1)} %get-tuple-element.54), channel_id=1, source_target_pairs={{0,12},{4,8},{8,4},{12,0},{16,28},{20,24},{24,20},{28,16},{1,13},{... | collective-permute-start | bytes 786440 | tf_op jit(solution)/shard_map/ppermute | solution.py:360
  14.4 1.6 %copy-start = (bf16[1024,1024]{1,0:T(8,128)(2,1)S(1)}, bf16[1024,1024]{1,0:T(8,128)(2,1)}, u32[]{:S(2)}) copy-start(bf16[1024,1024]{1,0:T(8,128)(2,1)} %refs_0_.1) | copy-start | bytes 6291460
  15.9 0.7 %copy-start.3 = (s32[8,4,8]{2,1,0:T(4,128)S(1)}, s32[8,4,8]{2,1,0:T(4,128)}, u32[]{:S(2)}) copy-start(s32[8,4,8]{2,1,0:T(4,128)} %wanted.4) | copy-start | bytes 3076
  30.7 8.9 %collective-permute-start.11 = (bf16[2,2,128,128]{3,2,1,0:T(8,128)(2,1)S(1)}, bf16[2,2,128,128]{3,2,1,0:T(8,128)(2,1)S(1)}, u32[]{:S(2)}, u32[]{:S(2)}) collective-permute-start(bf16[2,2,128,128]{3,2,1,0:T(8,128)(2,1)S(1)} %get-tuple-element.58), channel_id=1, source_target_pairs={{0,4},{4,0},{8,12},{12,8},{16,20},{20,16},{24,28},{28,24},{1,5},{5... | collective-permute-start | bytes 393224 | tf_op jit(solution)/shard_map/ppermute | solution.py:360
  32.3 9.4 %collective-permute-start.12 = (bf16[2,2,128,128]{3,2,1,0:T(8,128)(2,1)S(1)}, bf16[2,2,128,128]{3,2,1,0:T(8,128)(2,1)S(1)}, u32[]{:S(2)}, u32[]{:S(2)}) collective-permute-start(bf16[2,2,128,128]{3,2,1,0:T(8,128)(2,1)S(1)} %get-tuple-element.59), channel_id=1, source_target_pairs={{0,8},{4,12},{8,0},{12,4},{16,24},{20,28},{24,16},{28,20},{1,9},{5... | collective-permute-start | bytes 393224 | tf_op jit(solution)/shard_map/ppermute | solution.py:360
  32.3 10.1 %collective-permute-start.13 = (bf16[2,2,128,128]{3,2,1,0:T(8,128)(2,1)S(1)}, bf16[2,2,128,128]{3,2,1,0:T(8,128)(2,1)S(1)}, u32[]{:S(2)}, u32[]{:S(2)}) collective-permute-start(bf16[2,2,128,128]{3,2,1,0:T(8,128)(2,1)S(1)} %get-tuple-element.60), channel_id=1, source_target_pairs={{0,12},{4,8},{8,4},{12,0},{16,28},{20,24},{24,20},{28,16},{1,13},{... | collective-permute-start | bytes 393224 | tf_op jit(solution)/shard_map/ppermute | solution.py:360
  34.3 10.8 %collective-permute-start.5 = (bf16[2,2,128,128]{3,2,1,0:T(8,128)(2,1)S(1)}, bf16[2,2,128,128]{3,2,1,0:T(8,128)(2,1)S(1)}, u32[]{:S(2)}, u32[]{:S(2)}) collective-permute-start(bf16[2,2,128,128]{3,2,1,0:T(8,128)(2,1)S(1)} %get-tuple-element.48), channel_id=1, source_target_pairs={{0,4},{4,0},{8,12},{12,8},{16,20},{20,16},{24,28},{28,24},{1,5},{5... | collective-permute-start | bytes 393224 | tf_op jit(solution)/shard_map/ppermute | solution.py:360
  36.8 8.3 %collective-permute-start.6 = (bf16[2,2,128,128]{3,2,1,0:T(8,128)(2,1)S(1)}, bf16[2,2,128,128]{3,2,1,0:T(8,128)(2,1)S(1)}, u32[]{:S(2)}, u32[]{:S(2)}) collective-permute-start(bf16[2,2,128,128]{3,2,1,0:T(8,128)(2,1)S(1)} %get-tuple-element.49), channel_id=1, source_target_pairs={{0,8},{4,12},{8,0},{12,4},{16,24},{20,28},{24,16},{28,20},{1,9},{5... | collective-permute-start | bytes 393224 | tf_op jit(solution)/shard_map/ppermute | solution.py:360
  39.6 7.2 %collective-permute-start.7 = (bf16[2,2,128,128]{3,2,1,0:T(8,128)(2,1)S(1)}, bf16[2,2,128,128]{3,2,1,0:T(8,128)(2,1)S(1)}, u32[]{:S(2)}, u32[]{:S(2)}) collective-permute-start(bf16[2,2,128,128]{3,2,1,0:T(8,128)(2,1)S(1)} %get-tuple-element.50), channel_id=1, source_target_pairs={{0,12},{4,8},{8,4},{12,0},{16,28},{20,24},{24,20},{28,16},{1,13},{... | collective-permute-start | bytes 393224 | tf_op jit(solution)/shard_map/ppermute | solution.py:360
  43.2 7.4 %collective-permute-start.14 = (s16[64,1152]{1,0:T(8,128)(2,1)S(1)}, s16[64,1152]{1,0:T(8,128)(2,1)S(1)}, u32[]{:S(2)}, u32[]{:S(2)}) collective-permute-start(s16[64,1152]{1,0:T(8,128)(2,1)S(1)} %contract_tiles.9), channel_id=1, source_target_pairs={{0,2},{1,3},{2,0},{3,1},{4,6},{5,7},{6,4},{7,5},{8,10},{9,11},{10,... | collective-permute-start | bytes 442376 | tf_op jit(solution)/shard_map/ppermute | solution.py:360
  47.7 5.2 %collective-permute-start.10 = (s16[64,1152]{1,0:T(8,128)(2,1)S(1)}, s16[64,1152]{1,0:T(8,128)(2,1)S(1)}, u32[]{:S(2)}, u32[]{:S(2)}) collective-permute-start(s16[64,1152]{1,0:T(8,128)(2,1)S(1)} %contract_tiles.7), channel_id=1, source_target_pairs={{0,2},{1,3},{2,0},{3,1},{4,6},{5,7},{6,4},{7,5},{8,10},{9,11},{10,... | collective-permute-start | bytes 442376 | tf_op jit(solution)/shard_map/ppermute | solution.py:360
  49.9 14.9 %copy-start.4 = (s32[64]{0:T(128)S(1)}, s32[64]{0:T(128)}, u32[]{:S(2)}) copy-start(s32[64]{0:T(128)} %owner.1) | copy-start | bytes 772

commit v5 on v4

--- a/solution.py
+++ b/solution.py
@@ -62,18 +62,15 @@
     for n, flip in enumerate(flips):
         other = me ^ flip
         for g in range(CORES):
-
-            def step(k, found):
-                first, second, count = found
+            first = second = count = jnp.int32(0)
+            for k in range(length):
                 w = wanted[other, row ^ g, k]
                 mine = w // per_source == source
                 tile = w % per_source
                 first = jnp.where(mine & (count == 0), tile, first)
                 second = jnp.where(mine & (count == 1), tile, second)
-                return first, second, count + mine.astype(jnp.int32)
-
-            zero = jnp.int32(0)
-            found = lax.fori_loop(0, length, step, (zero, zero, zero), unroll=length <= 8)
+                count = count + mine.astype(jnp.int32)
+            found = (first, second)
             for slot in range(CAP):
                 start = pl.multiple_of(found[slot] * TILE, TILE)
                 copy = pltpu.make_async_copy(groups[g].at[:, pl.ds(start, TILE)], outs[n].at[g, slot], sem.at[n, g, slot])
@@ -89,7 +86,7 @@
     return pl.pallas_call(
         functools.partial(select_kernel, per_source, away, flips),
         out_shape=[shape] * len(flips),
-        in_specs=[SMEM] + [ANY] * CORES,
+        in_specs=[VMEM] + [ANY] * CORES,
         out_specs=[ANY] * len(flips),
         scratch_shapes=[pltpu.SemaphoreType.DMA((len(flips), CORES, CAP))],
         compiler_params=params(),
@@ -338,8 +335,8 @@
 
 
 def reorder_kernel(tiles_held, owner, received, out):
-    for t in range(owner.shape[0]):
-        at = owner[t]
+    for t in range(owner.shape[1]):
+        at = owner[0, t]
         start = pl.multiple_of((at % tiles_held) * TILE, TILE)
         out[:, t * TILE:(t + 1) * TILE] = received[at // tiles_held, :, pl.ds(start, TILE)]
 
@@ -349,11 +346,11 @@
     return pl.pallas_call(
         functools.partial(reorder_kernel, width // TILE),
         out_shape=jax.ShapeDtypeStruct((rows, columns * width), received.dtype),
-        in_specs=[SMEM, VMEM],
+        in_specs=[VMEM, VMEM],
         out_specs=VMEM,
         compiler_params=params(),
         name="reorder_tiles",
-    )(owner, received)
+    )(owner.reshape(1, -1), received)
 
 
 def swap(x, axis, flip):
@@ -396,7 +393,7 @@
     blocks = arrange(wanted, [integrals, swap(integrals, "row", 1)], per_source, top)
     late_wanted, *blocks = lax.optimization_barrier((wanted, *blocks))
     choices = choice(late_wanted, per_source, top, low, amplitudes.dtype)
-    *mirrors, early_block, far_block, choices, nearby[1] = lax.optimization_barrier((*mirrors, *blocks, choices, nearby[1]))
+    *mirrors, early_block, far_block, choices, nearby[top // 2 - 1] = lax.optimization_barrier((*mirrors, *blocks, choices, nearby[top // 2 - 1]))
     mirrors = [whole(x) for x in mirrors]
     height = ys * b
     passed = pass_on([flat(x) for x in mirrors], choices, [(lo * height, hi * height) for lo, hi in bounds])

time: 66.9 us -> 66.4 us (level)
  Pallas kernels: 14.7 us -> 14 us
where the time goes in v5:
time: 66.4 us; the launch traced here: 66 us
  starting transfers between devices  19.3 us (29%)
  waiting for transfers between devices  16.6 us (25%)
  Pallas kernels  14 us (21%)
  blocking collectives  12 us (18%)
  local copies, waits for them, and re-layouts  4.07 us (6%)
    ppermute x15, starting transfers between devices, swap(): lax.ppermute(x, axis, [(i, i ^ flip) for i in range(lax.axis_size(axis))])  19.3 us
    ppermute x15, waiting for transfers between devices, swap(): lax.ppermute(x, axis, [(i, i ^ flip) for i in range(lax.axis_size(axis))])  16.6 us
    all_to_all x1, blocking collectives, body(): lax.all_to_all(held, 'col', split_axis=0, concat_axis=0, tiled=True)  12 us
    pallas_call x5, Pallas kernels, contract(): pl.pallas_call(functools.partial(contract_kernel, len(sources), pieces, c...  5.03 us
    unnamed x10, local copies, waits for them, and re-layouts  4.07 us
    pallas_call x1, Pallas kernels, arrange(): pl.pallas_call(functools.partial(arrange_kernel, per_source, top), grid=(...  3.33 us
    pallas_call x1, Pallas kernels, choice(): pl.pallas_call(functools.partial(choice_kernel, per_source, away, flips),...  2.35 us
  transfers between devices with their start and end apart: 15, of which 9 were waited for; matrix products, arithmetic and copies ran while one was open for 0% of the time, Pallas kernels for 19%

profile of v5, /device:TPU:0, one launch (start us, length us, event | category | flops | bytes accessed | tf_op | source)
XLA Modules:
  0.0 66.0 jit_solution(1464759084356951336)
XLA Ops:
  0.5 1.0 %copy-done.1 = bf16[512,512]{1,0:T(8,128)(2,1)S(1)} copy-done((bf16[512,512]{1,0:T(8,128)(2,1)S(1)}, bf16[512,512]{1,0:T(8,128)(2,1)}, u32[]{:S(2)}) %copy-start.1) | copy-done | bytes 524312
  1.7 4.0 %collective-permute-start = (bf16[8,2,16,512]{3,2,1,0:T(8,128)(2,1)S(1)}, bf16[8,2,16,512]{3,2,1,0:T(8,128)(2,1)S(1)}, u32[]{:S(2)}, u32[]{:S(2)}) collective-permute-start(bf16[8,2,16,512]{3,2,1,0:T(8,128)(2,1)S(1)} %get-tuple-element.34.refs_0_), channel_id=1, source_target_pairs={{0,16},{4,20},{8,24},{12,28},{16,0},{20,4},{24,8},{28,12},{1,17},{... | collective-permute-start | bytes 786440 | tf_op jit(solution)/shard_map/ppermute | solution.py:357
  6.4 1.2 %select_tiles.1 = (bf16[2,2,256,128]{3,2,1,0:T(8,128)(2,1)S(1)}, bf16[2,2,256,128]{3,2,1,0:T(8,128)(2,1)S(1)}, bf16[2,2,256,128]{3,2,1,0:T(8,128)(2,1)S(1)}) custom-call(s32[8,4,8]{2,1,0:T(4,128)S(1)} %copy-done.2, bf16[256,512]{1,0:T(8,128)(2,1)S(1)} %bitcast.16, bf16[256,512]{1,0:T(8,128)(2,1)S(1)} %bitcast.17), custom_call_target="tpu_custom_call" | custom-call | tf_op jit(solution)/shard_map/select_tiles/pallas_call | solution.py:86
  7.7 2.9 %collective-permute-start.2 = (bf16[8,2,16,512]{3,2,1,0:T(8,128)(2,1)S(1)}, bf16[8,2,16,512]{3,2,1,0:T(8,128)(2,1)S(1)}, u32[]{:S(2)}, u32[]{:S(2)}) collective-permute-start(bf16[8,2,16,512]{3,2,1,0:T(8,128)(2,1)S(1)} %collective-permute-done.1.refs_1_), channel_id=1, source_target_pairs={{0,16},{4,20},{8,24},{12,28},{16,0},{20,4},{24,8},{28,12},{1,17},{... | collective-permute-start | bytes 786440 | tf_op jit(solution)/shard_map/ppermute | solution.py:357
  10.6 1.6 %collective-permute-start.4 = (bf16[2,2,256,128]{3,2,1,0:T(8,128)(2,1)S(1)}, bf16[2,2,256,128]{3,2,1,0:T(8,128)(2,1)S(1)}, u32[]{:S(2)}, u32[]{:S(2)}) collective-permute-start(bf16[2,2,256,128]{3,2,1,0:T(8,128)(2,1)S(1)} %get-tuple-element.43), channel_id=1, source_target_pairs={{0,8},{4,12},{8,0},{12,4},{16,24},{20,28},{24,16},{28,20},{1,9},{5... | collective-permute-start | bytes 786440 | tf_op jit(solution)/shard_map/ppermute | solution.py:357
  12.2 1.5 %collective-permute-start.8 = (bf16[2,2,256,128]{3,2,1,0:T(8,128)(2,1)S(1)}, bf16[2,2,256,128]{3,2,1,0:T(8,128)(2,1)S(1)}, u32[]{:S(2)}, u32[]{:S(2)}) collective-permute-start(bf16[2,2,256,128]{3,2,1,0:T(8,128)(2,1)S(1)} %get-tuple-element.52), channel_id=1, source_target_pairs={{0,4},{4,0},{8,12},{12,8},{16,20},{20,16},{24,28},{28,24},{1,5},{5... | collective-permute-start | bytes 786440 | tf_op jit(solution)/shard_map/ppermute | solution.py:357
  14.1 1.6 %copy-done = bf16[1024,1024]{1,0:T(8,128)(2,1)S(1)} copy-done((bf16[1024,1024]{1,0:T(8,128)(2,1)S(1)}, bf16[1024,1024]{1,0:T(8,128)(2,1)}, u32[]{:S(2)}) %copy-start) | copy-done | bytes 2097176
  16.4 3.3 %arrange_block.1 = (bf16[3584,1024]{1,0:T(8,128)(2,1)S(1)}, bf16[1536,1024]{1,0:T(8,128)(2,1)S(1)}) custom-call(s32[8,4,8]{2,1,0:T(4,128)S(1)} %copy-done.3, bf16[1024,1024]{1,0:T(8,128)(2,1)S(1)} %copy-done, bf16[1024,1024]{1,0:T(8,128)(2,1)S(1)} %collective-permute-done.3.refs_1_), custom_call_target="tpu_custom_call" | custom-call | tf_op jit(solution)/shard_map/arrange_block/pallas_call | solution.py:199
  19.7 2.3 %choice_matrices.1 = (bf16[512,768]{1,0:T(8,128)(2,1)S(1)}, bf16[512,768]{1,0:T(8,128)(2,1)S(1)}) custom-call(s32[8,4,8]{2,1,0:T(4,128)S(1)} %copy-done.3), custom_call_target="tpu_custom_call" | custom-call | tf_op jit(solution)/shard_map/choice_matrices/pallas_call | solution.py:125
  22.1 2.1 %collective-permute-done.refs_5_ = bf16[8,2,16,512]{3,2,1,0:T(8,128)(2,1)S(1)} collective-permute-done((bf16[8,2,16,512]{3,2,1,0:T(8,128)(2,1)S(1)}, bf16[8,2,16,512]{3,2,1,0:T(8,128)(2,1)S(1)}, u32[]{:S(2)}, u32[]{:S(2)}) %collective-permute-start) | collective-permute-done | bytes 262176 | tf_op jit(solution)/shard_map/ppermute | solution.py:357
  24.2 5.1 %collective-permute-done.2.refs_6_ = bf16[8,2,16,512]{3,2,1,0:T(8,128)(2,1)S(1)} collective-permute-done((bf16[8,2,16,512]{3,2,1,0:T(8,128)(2,1)S(1)}, bf16[8,2,16,512]{3,2,1,0:T(8,128)(2,1)S(1)}, u32[]{:S(2)}, u32[]{:S(2)}) %collective-permute-start.2) | collective-permute-done | bytes 262176 | tf_op jit(solution)/shard_map/ppermute | solution.py:357
  30.5 1.6 %collective-permute-start.11 = (bf16[2,2,128,128]{3,2,1,0:T(8,128)(2,1)S(1)}, bf16[2,2,128,128]{3,2,1,0:T(8,128)(2,1)S(1)}, u32[]{:S(2)}, u32[]{:S(2)}) collective-permute-start(bf16[2,2,128,128]{3,2,1,0:T(8,128)(2,1)S(1)} %get-tuple-element.58), channel_id=1, source_target_pairs={{0,4},{4,0},{8,12},{12,8},{16,20},{20,16},{24,28},{28,24},{1,5},{5... | collective-permute-start | bytes 393224 | tf_op jit(solution)/shard_map/ppermute | solution.py:357
  32.1 1.9 %collective-permute-start.13 = (bf16[2,2,128,128]{3,2,1,0:T(8,128)(2,1)S(1)}, bf16[2,2,128,128]{3,2,1,0:T(8,128)(2,1)S(1)}, u32[]{:S(2)}, u32[]{:S(2)}) collective-permute-start(bf16[2,2,128,128]{3,2,1,0:T(8,128)(2,1)S(1)} %get-tuple-element.60), channel_id=1, source_target_pairs={{0,12},{4,8},{8,4},{12,0},{16,28},{20,24},{24,20},{28,16},{1,13},{... | collective-permute-start | bytes 393224 | tf_op jit(solution)/shard_map/ppermute | solution.py:357
  34.0 1.5 %collective-permute-start.5 = (bf16[2,2,128,128]{3,2,1,0:T(8,128)(2,1)S(1)}, bf16[2,2,128,128]{3,2,1,0:T(8,128)(2,1)S(1)}, u32[]{:S(2)}, u32[]{:S(2)}) collective-permute-start(bf16[2,2,128,128]{3,2,1,0:T(8,128)(2,1)S(1)} %get-tuple-element.48), channel_id=1, source_target_pairs={{0,4},{4,0},{8,12},{12,8},{16,20},{20,16},{24,28},{28,24},{1,5},{5... | collective-permute-start | bytes 393224 | tf_op jit(solution)/shard_map/ppermute | solution.py:357
  35.6 1.0 %collective-permute-done.9 = bf16[2,2,256,128]{3,2,1,0:T(8,128)(2,1)S(1)} collective-permute-done((bf16[2,2,256,128]{3,2,1,0:T(8,128)(2,1)S(1)}, bf16[2,2,256,128]{3,2,1,0:T(8,128)(2,1)S(1)}, u32[]{:S(2)}, u32[]{:S(2)}) %collective-permute-start.9) | collective-permute-done | bytes 262176 | tf_op jit(solution)/shard_map/ppermute | solution.py:357
  36.5 2.9 %collective-permute-done.11 = bf16[2,2,128,128]{3,2,1,0:T(8,128)(2,1)S(1)} collective-permute-done((bf16[2,2,128,128]{3,2,1,0:T(8,128)(2,1)S(1)}, bf16[2,2,128,128]{3,2,1,0:T(8,128)(2,1)S(1)}, u32[]{:S(2)}, u32[]{:S(2)}) %collective-permute-start.11) | collective-permute-done | bytes 131104 | tf_op jit(solution)/shard_map/ppermute | solution.py:357
  39.4 2.1 %contract_tiles.5 = (f32[64,1024]{1,0:T(8,128)S(1)}, f32[64,1024]{1,0:T(8,128)S(1)}, f32[64,1024]{1,0:T(8,128)S(1)}, f32[64,1024]{1,0:T(8,128)S(1)}) custom-call(bf16[8,2,16,512]{3,2,1,0:T(8,128)(2,1)S(1)} %get-tuple-element.34.refs_0_, bf16[8,2,16,512]{3,2,1,0:T(8,128)(2,1)S(1)} %collective-permute-done.1.refs_1_, ...), custom_call_target="tpu_custom_call" | custom-call | tf_op jit(solution)/shard_map/contract_tiles/pallas_call | solution.py:284
  42.1 0.8 %contract_tiles.9 = s16[64,1152]{1,0:T(8,128)(2,1)S(1)} custom-call(bf16[2,2,4,2,16,128]{5,4,3,2,1,0:T(8,128)(2,1)S(1)} %bitcast.21, bf16[2,2,4,2,16,128]{5,4,3,2,1,0:T(8,128)(2,1)S(1)} %bitcast.23, bf16[2,2,4,2,16,128]{5,4,3,2,1,0:T(8,128)(2,1)S(1)} %bitcast.25, bf16[1536,1024]{1,0:T(8,128)(2,1)S(1)} %get-tuple-element.51.refs_3_, ...), custom_call_target="tpu_custom_call" | custom-call | tf_op jit(solution)/shard_map/contract_tiles/pallas_call | solution.py:284
  43.0 1.6 %collective-permute-start.14 = (s16[64,1152]{1,0:T(8,128)(2,1)S(1)}, s16[64,1152]{1,0:T(8,128)(2,1)S(1)}, u32[]{:S(2)}, u32[]{:S(2)}) collective-permute-start(s16[64,1152]{1,0:T(8,128)(2,1)S(1)} %contract_tiles.9), channel_id=1, source_target_pairs={{0,2},{1,3},{2,0},{3,1},{4,6},{5,7},{6,4},{7,5},{8,10},{9,11},{10,... | collective-permute-start | bytes 442376 | tf_op jit(solution)/shard_map/ppermute | solution.py:357
  44.9 1.8 %collective-permute-done.7 = bf16[2,2,128,128]{3,2,1,0:T(8,128)(2,1)S(1)} collective-permute-done((bf16[2,2,128,128]{3,2,1,0:T(8,128)(2,1)S(1)}, bf16[2,2,128,128]{3,2,1,0:T(8,128)(2,1)S(1)}, u32[]{:S(2)}, u32[]{:S(2)}) %collective-permute-start.7) | collective-permute-done | bytes 131104 | tf_op jit(solution)/shard_map/ppermute | solution.py:357
  47.5 1.6 %collective-permute-start.10 = (s16[64,1152]{1,0:T(8,128)(2,1)S(1)}, s16[64,1152]{1,0:T(8,128)(2,1)S(1)}, u32[]{:S(2)}, u32[]{:S(2)}) collective-permute-start(s16[64,1152]{1,0:T(8,128)(2,1)S(1)} %contract_tiles.7), channel_id=1, source_target_pairs={{0,2},{1,3},{2,0},{3,1},{4,6},{5,7},{6,4},{7,5},{8,10},{9,11},{10,... | collective-permute-start | bytes 442376 | tf_op jit(solution)/shard_map/ppermute | solution.py:357
  50.4 2.3 %collective-permute-done.10.refs_1_ = s16[64,1152]{1,0:T(8,128)(2,1)S(1)} collective-permute-done((s16[64,1152]{1,0:T(8,128)(2,1)S(1)}, s16[64,1152]{1,0:T(8,128)(2,1)S(1)}, u32[]{:S(2)}, u32[]{:S(2)}) %collective-permute-start.10) | collective-permute-done | bytes 147488 | tf_op jit(solution)/shard_map/ppermute | solution.py:357
  52.8 12.0 %all_to_all.5.received = bf16[8,16,1024]{2,1,0:T(8,128)(2,1)S(1)} all-to-all(bf16[8,16,1024]{2,1,0:T(8,128)(2,1)S(1)} %bitcast.18), channel_id=1, replica_groups=mesh['col'=8,'row'=4] {'col'}, dimensions={0} | all-to-all | bytes 524288 | tf_op jit(solution)/shard_map/all_to_all | solution.py:419
  64.8 1.2 %reorder_tiles.1 = bf16[16,8192]{1,0:T(8,128)(2,1)} custom-call(s32[1,64]{1,0:T(1,128)S(1)} %bitcast.37, bf16[8,16,1024]{2,1,0:T(8,128)(2,1)S(1)} %all_to_all.5.received), custom_call_target="tpu_custom_call" | custom-call | tf_op jit(solution)/shard_map/reorder_tiles/pallas_call | solution.py:346
  (29 shorter events, 7.0 us)
Async XLA Ops:
  0.0 13.7 %collective-permute-start.3 = (bf16[1024,1024]{1,0:T(8,128)(2,1)}, bf16[1024,1024]{1,0:T(8,128)(2,1)S(1)}, u32[]{:S(2)}, u32[]{:S(2)}) collective-permute-start(bf16[1024,1024]{1,0:T(8,128)(2,1)} %refs_0_.1), channel_id=1, source_target_pairs={{0,1},{1,0},{2,3},{3,2},{4,5},{5,4},{6,7},{7,6},{8,9},{9,8},{10,11... | collective-permute-start | bytes 6291464 | tf_op jit(solution)/shard_map/ppermute | solution.py:357
  0.5 1.0 %copy-start.1 = (bf16[512,512]{1,0:T(8,128)(2,1)S(1)}, bf16[512,512]{1,0:T(8,128)(2,1)}, u32[]{:S(2)}) copy-start(bf16[512,512]{1,0:T(8,128)(2,1)} %param.4) | copy-start | bytes 1572868
  1.6 4.2 %collective-permute-start.1 = (bf16[8,2,16,512]{3,2,1,0:T(8,128)(2,1)S(1)}, bf16[8,2,16,512]{3,2,1,0:T(8,128)(2,1)S(1)}, u32[]{:S(2)}, u32[]{:S(2)}) collective-permute-start(bf16[8,2,16,512]{3,2,1,0:T(8,128)(2,1)S(1)} %get-tuple-element.35), channel_id=1, source_target_pairs={{0,1},{1,0},{2,3},{3,2},{4,5},{5,4},{6,7},{7,6},{8,9},{9,8},{10,11... | collective-permute-start | bytes 786440 | tf_op jit(solution)/shard_map/ppermute | solution.py:357
  1.7 22.5 %collective-permute-start = (bf16[8,2,16,512]{3,2,1,0:T(8,128)(2,1)S(1)}, bf16[8,2,16,512]{3,2,1,0:T(8,128)(2,1)S(1)}, u32[]{:S(2)}, u32[]{:S(2)}) collective-permute-start(bf16[8,2,16,512]{3,2,1,0:T(8,128)(2,1)S(1)} %get-tuple-element.34.refs_0_), channel_id=1, source_target_pairs={{0,16},{4,20},{8,24},{12,28},{16,0},{20,4},{24,8},{28,12},{1,17},{... | collective-permute-start | bytes 786440 | tf_op jit(solution)/shard_map/ppermute | solution.py:357
  5.7 0.7 %copy-start.2 = (s32[8,4,8]{2,1,0:T(4,128)S(1)}, s32[8,4,8]{2,1,0:T(4,128)}, u32[]{:S(2)}) copy-start(s32[8,4,8]{2,1,0:T(4,128)} %wanted.4) | copy-start | bytes 3076
  7.7 21.5 %collective-permute-start.2 = (bf16[8,2,16,512]{3,2,1,0:T(8,128)(2,1)S(1)}, bf16[8,2,16,512]{3,2,1,0:T(8,128)(2,1)S(1)}, u32[]{:S(2)}, u32[]{:S(2)}) collective-permute-start(bf16[8,2,16,512]{3,2,1,0:T(8,128)(2,1)S(1)} %collective-permute-done.1.refs_1_), channel_id=1, source_target_pairs={{0,16},{4,20},{8,24},{12,28},{16,0},{20,4},{24,8},{28,12},{1,17},{... | collective-permute-start | bytes 786440 | tf_op jit(solution)/shard_map/ppermute | solution.py:357
  10.6 19.3 %collective-permute-start.4 = (bf16[2,2,256,128]{3,2,1,0:T(8,128)(2,1)S(1)}, bf16[2,2,256,128]{3,2,1,0:T(8,128)(2,1)S(1)}, u32[]{:S(2)}, u32[]{:S(2)}) collective-permute-start(bf16[2,2,256,128]{3,2,1,0:T(8,128)(2,1)S(1)} %get-tuple-element.43), channel_id=1, source_target_pairs={{0,8},{4,12},{8,0},{12,4},{16,24},{20,28},{24,16},{28,20},{1,9},{5... | collective-permute-start | bytes 786440 | tf_op jit(solution)/shard_map/ppermute | solution.py:357
  12.2 21.8 %collective-permute-start.8 = (bf16[2,2,256,128]{3,2,1,0:T(8,128)(2,1)S(1)}, bf16[2,2,256,128]{3,2,1,0:T(8,128)(2,1)S(1)}, u32[]{:S(2)}, u32[]{:S(2)}) collective-permute-start(bf16[2,2,256,128]{3,2,1,0:T(8,128)(2,1)S(1)} %get-tuple-element.52), channel_id=1, source_target_pairs={{0,4},{4,0},{8,12},{12,8},{16,20},{20,16},{24,28},{28,24},{1,5},{5... | collective-permute-start | bytes 786440 | tf_op jit(solution)/shard_map/ppermute | solution.py:357
  13.7 22.8 %collective-permute-start.9 = (bf16[2,2,256,128]{3,2,1,0:T(8,128)(2,1)S(1)}, bf16[2,2,256,128]{3,2,1,0:T(8,128)(2,1)S(1)}, u32[]{:S(2)}, u32[]{:S(2)}) collective-permute-start(bf16[2,2,256,128]{3,2,1,0:T(8,128)(2,1)S(1)} %get-tuple-element.54), channel_id=1, source_target_pairs={{0,12},{4,8},{8,4},{12,0},{16,28},{20,24},{24,20},{28,16},{1,13},{... | collective-permute-start | bytes 786440 | tf_op jit(solution)/shard_map/ppermute | solution.py:357
  14.1 1.6 %copy-start = (bf16[1024,1024]{1,0:T(8,128)(2,1)S(1)}, bf16[1024,1024]{1,0:T(8,128)(2,1)}, u32[]{:S(2)}) copy-start(bf16[1024,1024]{1,0:T(8,128)(2,1)} %refs_0_.1) | copy-start | bytes 6291460
  15.7 0.7 %copy-start.3 = (s32[8,4,8]{2,1,0:T(4,128)S(1)}, s32[8,4,8]{2,1,0:T(4,128)}, u32[]{:S(2)}) copy-start(s32[8,4,8]{2,1,0:T(4,128)} %wanted.4) | copy-start | bytes 3076
  30.5 8.9 %collective-permute-start.11 = (bf16[2,2,128,128]{3,2,1,0:T(8,128)(2,1)S(1)}, bf16[2,2,128,128]{3,2,1,0:T(8,128)(2,1)S(1)}, u32[]{:S(2)}, u32[]{:S(2)}) collective-permute-start(bf16[2,2,128,128]{3,2,1,0:T(8,128)(2,1)S(1)} %get-tuple-element.58), channel_id=1, source_target_pairs={{0,4},{4,0},{8,12},{12,8},{16,20},{20,16},{24,28},{28,24},{1,5},{5... | collective-permute-start | bytes 393224 | tf_op jit(solution)/shard_map/ppermute | solution.py:357
  32.1 9.4 %collective-permute-start.12 = (bf16[2,2,128,128]{3,2,1,0:T(8,128)(2,1)S(1)}, bf16[2,2,128,128]{3,2,1,0:T(8,128)(2,1)S(1)}, u32[]{:S(2)}, u32[]{:S(2)}) collective-permute-start(bf16[2,2,128,128]{3,2,1,0:T(8,128)(2,1)S(1)} %get-tuple-element.59), channel_id=1, source_target_pairs={{0,8},{4,12},{8,0},{12,4},{16,24},{20,28},{24,16},{28,20},{1,9},{5... | collective-permute-start | bytes 393224 | tf_op jit(solution)/shard_map/ppermute | solution.py:357
  32.1 10.1 %collective-permute-start.13 = (bf16[2,2,128,128]{3,2,1,0:T(8,128)(2,1)S(1)}, bf16[2,2,128,128]{3,2,1,0:T(8,128)(2,1)S(1)}, u32[]{:S(2)}, u32[]{:S(2)}) collective-permute-start(bf16[2,2,128,128]{3,2,1,0:T(8,128)(2,1)S(1)} %get-tuple-element.60), channel_id=1, source_target_pairs={{0,12},{4,8},{8,4},{12,0},{16,28},{20,24},{24,20},{28,16},{1,13},{... | collective-permute-start | bytes 393224 | tf_op jit(solution)/shard_map/ppermute | solution.py:357
  34.0 10.8 %collective-permute-start.5 = (bf16[2,2,128,128]{3,2,1,0:T(8,128)(2,1)S(1)}, bf16[2,2,128,128]{3,2,1,0:T(8,128)(2,1)S(1)}, u32[]{:S(2)}, u32[]{:S(2)}) collective-permute-start(bf16[2,2,128,128]{3,2,1,0:T(8,128)(2,1)S(1)} %get-tuple-element.48), channel_id=1, source_target_pairs={{0,4},{4,0},{8,12},{12,8},{16,20},{20,16},{24,28},{28,24},{1,5},{5... | collective-permute-start | bytes 393224 | tf_op jit(solution)/shard_map/ppermute | solution.py:357
  36.5 8.3 %collective-permute-start.6 = (bf16[2,2,128,128]{3,2,1,0:T(8,128)(2,1)S(1)}, bf16[2,2,128,128]{3,2,1,0:T(8,128)(2,1)S(1)}, u32[]{:S(2)}, u32[]{:S(2)}) collective-permute-start(bf16[2,2,128,128]{3,2,1,0:T(8,128)(2,1)S(1)} %get-tuple-element.49), channel_id=1, source_target_pairs={{0,8},{4,12},{8,0},{12,4},{16,24},{20,28},{24,16},{28,20},{1,9},{5... | collective-permute-start | bytes 393224 | tf_op jit(solution)/shard_map/ppermute | solution.py:357
  39.4 7.2 %collective-permute-start.7 = (bf16[2,2,128,128]{3,2,1,0:T(8,128)(2,1)S(1)}, bf16[2,2,128,128]{3,2,1,0:T(8,128)(2,1)S(1)}, u32[]{:S(2)}, u32[]{:S(2)}) collective-permute-start(bf16[2,2,128,128]{3,2,1,0:T(8,128)(2,1)S(1)} %get-tuple-element.50), channel_id=1, source_target_pairs={{0,12},{4,8},{8,4},{12,0},{16,28},{20,24},{24,20},{28,16},{1,13},{... | collective-permute-start | bytes 393224 | tf_op jit(solution)/shard_map/ppermute | solution.py:357
  43.0 7.4 %collective-permute-start.14 = (s16[64,1152]{1,0:T(8,128)(2,1)S(1)}, s16[64,1152]{1,0:T(8,128)(2,1)S(1)}, u32[]{:S(2)}, u32[]{:S(2)}) collective-permute-start(s16[64,1152]{1,0:T(8,128)(2,1)S(1)} %contract_tiles.9), channel_id=1, source_target_pairs={{0,2},{1,3},{2,0},{3,1},{4,6},{5,7},{6,4},{7,5},{8,10},{9,11},{10,... | collective-permute-start | bytes 442376 | tf_op jit(solution)/shard_map/ppermute | solution.py:357
  47.5 5.2 %collective-permute-start.10 = (s16[64,1152]{1,0:T(8,128)(2,1)S(1)}, s16[64,1152]{1,0:T(8,128)(2,1)S(1)}, u32[]{:S(2)}, u32[]{:S(2)}) collective-permute-start(s16[64,1152]{1,0:T(8,128)(2,1)S(1)} %contract_tiles.7), channel_id=1, source_target_pairs={{0,2},{1,3},{2,0},{3,1},{4,6},{5,7},{6,4},{7,5},{8,10},{9,11},{10,... | collective-permute-start | bytes 442376 | tf_op jit(solution)/shard_map/ppermute | solution.py:357
  49.7 15.1 %copy-start.4 = (s32[64]{0:T(128)S(1)}, s32[64]{0:T(128)}, u32[]{:S(2)}) copy-start(s32[64]{0:T(128)} %param.7) | copy-start | bytes 772

commit v6 on v5

--- a/solution.py
+++ b/solution.py
@@ -248,7 +248,7 @@
     return depth
 
 
-def contract_kernel(count, pieces, coded, *refs):
+def contract_kernel(count, pieces, coded, places, *refs):
     sources, block = refs[:count], refs[count]
     before, outs, left = refs[count + 1:-1 - len(pieces)], refs[-1 - len(pieces):-1], refs[-1]
     base = 0
@@ -259,7 +259,7 @@
             for source in sources:
                 depth = fill(left, source, units, flip, depth, base + j * rows)
         base += outs[n].shape[0]
-    product = jnp.dot(left[...], block[...], preferred_element_type=jnp.float32)
+    product = jnp.dot(left[...], block[places[0]:places[1]], preferred_element_type=jnp.float32)
     base = 0
     for n in range(len(pieces)):
         rows = outs[n].shape[0]
@@ -273,16 +273,17 @@
             outs[n][...] = x
 
 
-def contract(sources, block, pieces, before=(), coded=False):
-    depth, width = block.shape
+def contract(sources, block, pieces, before=(), coded=False, places=None):
+    places = places or (0, block.shape[0])
+    depth, width = places[1] - places[0], block.shape[1]
     rows = [(units[1] - units[0]) * sources[0].shape[-2] * len(flips) for units, flips in pieces]
     if coded:
         shapes = [jax.ShapeDtypeStruct((n, width + TILE), jnp.int16) for n in rows]
     else:
         shapes = [jax.ShapeDtypeStruct((n, width), jnp.float32) for n in rows]
-    size = 2 * depth * (width + sum(rows)) + 16 * width * sum(rows) + sum(2 * x.size for x in sources)
-    return pl.pallas_call(
-        functools.partial(contract_kernel, len(sources), pieces, coded),
+    size = 2 * (block.size + depth * sum(rows)) + 16 * width * sum(rows) + sum(2 * x.size for x in sources)
+    return pl.pallas_call(
+        functools.partial(contract_kernel, len(sources), pieces, coded, places),
         out_shape=shapes,
         in_specs=[VMEM] * (len(sources) + 1 + len(before)),
         out_specs=[VMEM] * len(shapes),
@@ -405,8 +406,11 @@
     pieces = []
     for n, (lo, hi) in enumerate(bounds):
         span = (0, hi - lo)
-        send, = contract(far[n], far_block, [(span, slots[0])], sums[2 * n:2 * n + 1], coded=True)
-        keep, = contract(far[n], far_block, [(span, slots[1])], sums[2 * n + 1:2 * n + 2])
+        last = far_block.shape[0] - CORES * CAP * TILE
+        so_far = contract(far[n][:-1], far_block, [(span, x) for x in slots], sums[2 * n:2 * n + 2], places=(0, last))
+        ends = (last, far_block.shape[0])
+        send, = contract(far[n][-1:], far_block, [(span, slots[0])], so_far[:1], coded=True, places=ends)
+        keep, = contract(far[n][-1:], far_block, [(span, slots[1])], so_far[1:], places=ends)
         bit = CORES
         while True:
             arrived = swap(send, "row", bit)

time: 66.4 us -> 66 us (level)
    pallas_call x5 -> x7, Pallas kernels: 5.03 us -> 4.5 us  [contract(): pl.pallas_call(functools.partial(contract_kernel, len(sources), pieces, c...]
  transfers between devices with their start and end apart: 15 -> 15, of which waited for: 9 -> 9; matrix products, arithmetic and copies ran while one was open for 0% -> 0% of each run, Pallas kernels for 19% -> 18%
where the time goes in v6:
time: 66 us; the launch traced here: 65.7 us
  starting transfers between devices  19.3 us (29%)
  waiting for transfers between devices  16.7 us (25%)
  Pallas kernels  13.4 us (20%)
  blocking collectives  12 us (18%)
  local copies, waits for them, and re-layouts  4.07 us (6%)
    ppermute x15, starting transfers between devices, swap(): lax.ppermute(x, axis, [(i, i ^ flip) for i in range(lax.axis_size(axis))])  19.3 us
    ppermute x15, waiting for transfers between devices, swap(): lax.ppermute(x, axis, [(i, i ^ flip) for i in range(lax.axis_size(axis))])  16.7 us
    all_to_all x1, blocking collectives, body(): lax.all_to_all(held, 'col', split_axis=0, concat_axis=0, tiled=True)  12 us
    pallas_call x7, Pallas kernels, contract(): pl.pallas_call(functools.partial(contract_kernel, len(sources), pieces, c...  4.5 us
    unnamed x10, local copies, waits for them, and re-layouts  4.07 us
    pallas_call x1, Pallas kernels, arrange(): pl.pallas_call(functools.partial(arrange_kernel, per_source, top), grid=(...  3.33 us
    pallas_call x1, Pallas kernels, choice(): pl.pallas_call(functools.partial(choice_kernel, per_source, away, flips),...  2.35 us
  transfers between devices with their start and end apart: 15, of which 9 were waited for; matrix products, arithmetic and copies ran while one was open for 0% of the time, Pallas kernels for 18%

profile of v6, /device:TPU:0, one launch (start us, length us, event | category | flops | bytes accessed | tf_op | source)
XLA Modules:
  0.0 65.7 jit_solution(16242456244997276347)
XLA Ops:
  0.5 1.0 %copy-done.1 = bf16[512,512]{1,0:T(8,128)(2,1)S(1)} copy-done((bf16[512,512]{1,0:T(8,128)(2,1)S(1)}, bf16[512,512]{1,0:T(8,128)(2,1)}, u32[]{:S(2)}) %copy-start.1) | copy-done | bytes 524312
  1.7 4.0 %collective-permute-start = (bf16[8,2,16,512]{3,2,1,0:T(8,128)(2,1)S(1)}, bf16[8,2,16,512]{3,2,1,0:T(8,128)(2,1)S(1)}, u32[]{:S(2)}, u32[]{:S(2)}) collective-permute-start(bf16[8,2,16,512]{3,2,1,0:T(8,128)(2,1)S(1)} %get-tuple-element.38.refs_0_), channel_id=1, source_target_pairs={{0,16},{4,20},{8,24},{12,28},{16,0},{20,4},{24,8},{28,12},{1,17},{... | collective-permute-start | bytes 786440 | tf_op jit(solution)/shard_map/ppermute | solution.py:358
  5.7 0.7 %copy-done.2 = s32[8,4,8]{2,1,0:T(4,128)S(1)} copy-done((s32[8,4,8]{2,1,0:T(4,128)S(1)}, s32[8,4,8]{2,1,0:T(4,128)}, u32[]{:S(2)}) %copy-start.2) | copy-done | bytes 1048
  6.4 1.2 %select_tiles.1 = (bf16[2,2,256,128]{3,2,1,0:T(8,128)(2,1)S(1)}, bf16[2,2,256,128]{3,2,1,0:T(8,128)(2,1)S(1)}, bf16[2,2,256,128]{3,2,1,0:T(8,128)(2,1)S(1)}) custom-call(s32[8,4,8]{2,1,0:T(4,128)S(1)} %copy-done.2, bf16[256,512]{1,0:T(8,128)(2,1)S(1)} %bitcast.16, bf16[256,512]{1,0:T(8,128)(2,1)S(1)} %bitcast.17), custom_call_target="tpu_custom_call" | custom-call | tf_op jit(solution)/shard_map/select_tiles/pallas_call | solution.py:86
  7.7 2.9 %collective-permute-start.2 = (bf16[8,2,16,512]{3,2,1,0:T(8,128)(2,1)S(1)}, bf16[8,2,16,512]{3,2,1,0:T(8,128)(2,1)S(1)}, u32[]{:S(2)}, u32[]{:S(2)}) collective-permute-start(bf16[8,2,16,512]{3,2,1,0:T(8,128)(2,1)S(1)} %collective-permute-done.1.refs_1_), channel_id=1, source_target_pairs={{0,16},{4,20},{8,24},{12,28},{16,0},{20,4},{24,8},{28,12},{1,17},{... | collective-permute-start | bytes 786440 | tf_op jit(solution)/shard_map/ppermute | solution.py:358
  10.6 1.6 %collective-permute-start.4 = (bf16[2,2,256,128]{3,2,1,0:T(8,128)(2,1)S(1)}, bf16[2,2,256,128]{3,2,1,0:T(8,128)(2,1)S(1)}, u32[]{:S(2)}, u32[]{:S(2)}) collective-permute-start(bf16[2,2,256,128]{3,2,1,0:T(8,128)(2,1)S(1)} %get-tuple-element.47), channel_id=1, source_target_pairs={{0,8},{4,12},{8,0},{12,4},{16,24},{20,28},{24,16},{28,20},{1,9},{5... | collective-permute-start | bytes 786440 | tf_op jit(solution)/shard_map/ppermute | solution.py:358
  12.2 1.5 %collective-permute-start.8 = (bf16[2,2,256,128]{3,2,1,0:T(8,128)(2,1)S(1)}, bf16[2,2,256,128]{3,2,1,0:T(8,128)(2,1)S(1)}, u32[]{:S(2)}, u32[]{:S(2)}) collective-permute-start(bf16[2,2,256,128]{3,2,1,0:T(8,128)(2,1)S(1)} %get-tuple-element.56), channel_id=1, source_target_pairs={{0,4},{4,0},{8,12},{12,8},{16,20},{20,16},{24,28},{28,24},{1,5},{5... | collective-permute-start | bytes 786440 | tf_op jit(solution)/shard_map/ppermute | solution.py:358
  14.1 1.6 %copy-done = bf16[1024,1024]{1,0:T(8,128)(2,1)S(1)} copy-done((bf16[1024,1024]{1,0:T(8,128)(2,1)S(1)}, bf16[1024,1024]{1,0:T(8,128)(2,1)}, u32[]{:S(2)}) %copy-start) | copy-done | bytes 2097176
  16.4 3.3 %arrange_block.1 = (bf16[3584,1024]{1,0:T(8,128)(2,1)S(1)}, bf16[1536,1024]{1,0:T(8,128)(2,1)S(1)}) custom-call(s32[8,4,8]{2,1,0:T(4,128)S(1)} %copy-done.3, bf16[1024,1024]{1,0:T(8,128)(2,1)S(1)} %copy-done, bf16[1024,1024]{1,0:T(8,128)(2,1)S(1)} %collective-permute-done.3.refs_1_), custom_call_target="tpu_custom_call" | custom-call | tf_op jit(solution)/shard_map/arrange_block/pallas_call | solution.py:199
  19.8 2.4 %choice_matrices.1 = (bf16[512,768]{1,0:T(8,128)(2,1)S(1)}, bf16[512,768]{1,0:T(8,128)(2,1)S(1)}) custom-call(s32[8,4,8]{2,1,0:T(4,128)S(1)} %copy-done.3), custom_call_target="tpu_custom_call" | custom-call | tf_op jit(solution)/shard_map/choice_matrices/pallas_call | solution.py:125
  22.1 2.0 %collective-permute-done.refs_5_ = bf16[8,2,16,512]{3,2,1,0:T(8,128)(2,1)S(1)} collective-permute-done((bf16[8,2,16,512]{3,2,1,0:T(8,128)(2,1)S(1)}, bf16[8,2,16,512]{3,2,1,0:T(8,128)(2,1)S(1)}, u32[]{:S(2)}, u32[]{:S(2)}) %collective-permute-start) | collective-permute-done | bytes 262176 | tf_op jit(solution)/shard_map/ppermute | solution.py:358
  24.2 5.1 %collective-permute-done.2.refs_6_ = bf16[8,2,16,512]{3,2,1,0:T(8,128)(2,1)S(1)} collective-permute-done((bf16[8,2,16,512]{3,2,1,0:T(8,128)(2,1)S(1)}, bf16[8,2,16,512]{3,2,1,0:T(8,128)(2,1)S(1)}, u32[]{:S(2)}, u32[]{:S(2)}) %collective-permute-start.2) | collective-permute-done | bytes 262176 | tf_op jit(solution)/shard_map/ppermute | solution.py:358
  30.5 1.6 %collective-permute-start.12 = (bf16[2,2,128,128]{3,2,1,0:T(8,128)(2,1)S(1)}, bf16[2,2,128,128]{3,2,1,0:T(8,128)(2,1)S(1)}, u32[]{:S(2)}, u32[]{:S(2)}) collective-permute-start(bf16[2,2,128,128]{3,2,1,0:T(8,128)(2,1)S(1)} %get-tuple-element.65), channel_id=1, source_target_pairs={{0,4},{4,0},{8,12},{12,8},{16,20},{20,16},{24,28},{28,24},{1,5},{5... | collective-permute-start | bytes 393224 | tf_op jit(solution)/shard_map/ppermute | solution.py:358
  32.1 1.9 %collective-permute-start.11 = (bf16[2,2,128,128]{3,2,1,0:T(8,128)(2,1)S(1)}, bf16[2,2,128,128]{3,2,1,0:T(8,128)(2,1)S(1)}, u32[]{:S(2)}, u32[]{:S(2)}) collective-permute-start(bf16[2,2,128,128]{3,2,1,0:T(8,128)(2,1)S(1)} %get-tuple-element.64), channel_id=1, source_target_pairs={{0,12},{4,8},{8,4},{12,0},{16,28},{20,24},{24,20},{28,16},{1,13},{... | collective-permute-start | bytes 393224 | tf_op jit(solution)/shard_map/ppermute | solution.py:358
  34.0 1.5 %collective-permute-start.6 = (bf16[2,2,128,128]{3,2,1,0:T(8,128)(2,1)S(1)}, bf16[2,2,128,128]{3,2,1,0:T(8,128)(2,1)S(1)}, u32[]{:S(2)}, u32[]{:S(2)}) collective-permute-start(bf16[2,2,128,128]{3,2,1,0:T(8,128)(2,1)S(1)} %get-tuple-element.54), channel_id=1, source_target_pairs={{0,4},{4,0},{8,12},{12,8},{16,20},{20,16},{24,28},{28,24},{1,5},{5... | collective-permute-start | bytes 393224 | tf_op jit(solution)/shard_map/ppermute | solution.py:358
  35.6 1.0 %collective-permute-done.9 = bf16[2,2,256,128]{3,2,1,0:T(8,128)(2,1)S(1)} collective-permute-done((bf16[2,2,256,128]{3,2,1,0:T(8,128)(2,1)S(1)}, bf16[2,2,256,128]{3,2,1,0:T(8,128)(2,1)S(1)}, u32[]{:S(2)}, u32[]{:S(2)}) %collective-permute-start.9) | collective-permute-done | bytes 262176 | tf_op jit(solution)/shard_map/ppermute | solution.py:358
  36.5 2.9 %collective-permute-done.12 = bf16[2,2,128,128]{3,2,1,0:T(8,128)(2,1)S(1)} collective-permute-done((bf16[2,2,128,128]{3,2,1,0:T(8,128)(2,1)S(1)}, bf16[2,2,128,128]{3,2,1,0:T(8,128)(2,1)S(1)}, u32[]{:S(2)}, u32[]{:S(2)}) %collective-permute-start.12) | collective-permute-done | bytes 131104 | tf_op jit(solution)/shard_map/ppermute | solution.py:358
  39.4 2.1 %contract_tiles.7 = (f32[64,1024]{1,0:T(8,128)S(1)}, f32[64,1024]{1,0:T(8,128)S(1)}, f32[64,1024]{1,0:T(8,128)S(1)}, f32[64,1024]{1,0:T(8,128)S(1)}) custom-call(bf16[8,2,16,512]{3,2,1,0:T(8,128)(2,1)S(1)} %get-tuple-element.38.refs_0_, bf16[8,2,16,512]{3,2,1,0:T(8,128)(2,1)S(1)} %collective-permute-done.1.refs_1_, ...), custom_call_target="tpu_custom_call" | custom-call | tf_op jit(solution)/shard_map/contract_tiles/pallas_call | solution.py:285
  42.6 1.6 %collective-permute-start.14 = (s16[64,1152]{1,0:T(8,128)(2,1)S(1)}, s16[64,1152]{1,0:T(8,128)(2,1)S(1)}, u32[]{:S(2)}, u32[]{:S(2)}) collective-permute-start(s16[64,1152]{1,0:T(8,128)(2,1)S(1)} %contract_tiles.13), channel_id=1, source_target_pairs={{0,2},{1,3},{2,0},{3,1},{4,6},{5,7},{6,4},{7,5},{8,10},{9,11},{10,... | collective-permute-start | bytes 442376 | tf_op jit(solution)/shard_map/ppermute | solution.py:358
  45.3 1.3 %collective-permute-done.5 = bf16[2,2,128,128]{3,2,1,0:T(8,128)(2,1)S(1)} collective-permute-done((bf16[2,2,128,128]{3,2,1,0:T(8,128)(2,1)S(1)}, bf16[2,2,128,128]{3,2,1,0:T(8,128)(2,1)S(1)}, u32[]{:S(2)}, u32[]{:S(2)}) %collective-permute-start.5) | collective-permute-done | bytes 131104 | tf_op jit(solution)/shard_map/ppermute | solution.py:358
  47.1 1.6 %collective-permute-start.10 = (s16[64,1152]{1,0:T(8,128)(2,1)S(1)}, s16[64,1152]{1,0:T(8,128)(2,1)S(1)}, u32[]{:S(2)}, u32[]{:S(2)}) collective-permute-start(s16[64,1152]{1,0:T(8,128)(2,1)S(1)} %contract_tiles.10), channel_id=1, source_target_pairs={{0,2},{1,3},{2,0},{3,1},{4,6},{5,7},{6,4},{7,5},{8,10},{9,11},{10,... | collective-permute-start | bytes 442376 | tf_op jit(solution)/shard_map/ppermute | solution.py:358
  49.3 3.0 %collective-permute-done.10.refs_1_ = s16[64,1152]{1,0:T(8,128)(2,1)S(1)} collective-permute-done((s16[64,1152]{1,0:T(8,128)(2,1)S(1)}, s16[64,1152]{1,0:T(8,128)(2,1)S(1)}, u32[]{:S(2)}, u32[]{:S(2)}) %collective-permute-start.10) | collective-permute-done | bytes 147488 | tf_op jit(solution)/shard_map/ppermute | solution.py:358
  52.4 12.0 %all_to_all.5.received = bf16[8,16,1024]{2,1,0:T(8,128)(2,1)S(1)} all-to-all(bf16[8,16,1024]{2,1,0:T(8,128)(2,1)S(1)} %bitcast.18), channel_id=1, replica_groups=mesh['col'=8,'row'=4] {'col'}, dimensions={0} | all-to-all | bytes 524288 | tf_op jit(solution)/shard_map/all_to_all | solution.py:423
  64.4 1.2 %reorder_tiles.1 = bf16[16,8192]{1,0:T(8,128)(2,1)} custom-call(s32[1,64]{1,0:T(1,128)S(1)} %bitcast.33, bf16[8,16,1024]{2,1,0:T(8,128)(2,1)S(1)} %all_to_all.5.received), custom_call_target="tpu_custom_call" | custom-call | tf_op jit(solution)/shard_map/reorder_tiles/pallas_call | solution.py:347
  (31 shorter events, 6.5 us)
Async XLA Ops:
  0.0 13.7 %collective-permute-start.3 = (bf16[1024,1024]{1,0:T(8,128)(2,1)}, bf16[1024,1024]{1,0:T(8,128)(2,1)S(1)}, u32[]{:S(2)}, u32[]{:S(2)}) collective-permute-start(bf16[1024,1024]{1,0:T(8,128)(2,1)} %refs_0_.1), channel_id=1, source_target_pairs={{0,1},{1,0},{2,3},{3,2},{4,5},{5,4},{6,7},{7,6},{8,9},{9,8},{10,11... | collective-permute-start | bytes 6291464 | tf_op jit(solution)/shard_map/ppermute | solution.py:358
  0.5 1.0 %copy-start.1 = (bf16[512,512]{1,0:T(8,128)(2,1)S(1)}, bf16[512,512]{1,0:T(8,128)(2,1)}, u32[]{:S(2)}) copy-start(bf16[512,512]{1,0:T(8,128)(2,1)} %param.4) | copy-start | bytes 1572868
  1.6 4.2 %collective-permute-start.1 = (bf16[8,2,16,512]{3,2,1,0:T(8,128)(2,1)S(1)}, bf16[8,2,16,512]{3,2,1,0:T(8,128)(2,1)S(1)}, u32[]{:S(2)}, u32[]{:S(2)}) collective-permute-start(bf16[8,2,16,512]{3,2,1,0:T(8,128)(2,1)S(1)} %get-tuple-element.39), channel_id=1, source_target_pairs={{0,1},{1,0},{2,3},{3,2},{4,5},{5,4},{6,7},{7,6},{8,9},{9,8},{10,11... | collective-permute-start | bytes 786440 | tf_op jit(solution)/shard_map/ppermute | solution.py:358
  1.7 22.5 %collective-permute-start = (bf16[8,2,16,512]{3,2,1,0:T(8,128)(2,1)S(1)}, bf16[8,2,16,512]{3,2,1,0:T(8,128)(2,1)S(1)}, u32[]{:S(2)}, u32[]{:S(2)}) collective-permute-start(bf16[8,2,16,512]{3,2,1,0:T(8,128)(2,1)S(1)} %get-tuple-element.38.refs_0_), channel_id=1, source_target_pairs={{0,16},{4,20},{8,24},{12,28},{16,0},{20,4},{24,8},{28,12},{1,17},{... | collective-permute-start | bytes 786440 | tf_op jit(solution)/shard_map/ppermute | solution.py:358
  5.7 0.7 %copy-start.2 = (s32[8,4,8]{2,1,0:T(4,128)S(1)}, s32[8,4,8]{2,1,0:T(4,128)}, u32[]{:S(2)}) copy-start(s32[8,4,8]{2,1,0:T(4,128)} %wanted.4) | copy-start | bytes 3076
  7.7 21.5 %collective-permute-start.2 = (bf16[8,2,16,512]{3,2,1,0:T(8,128)(2,1)S(1)}, bf16[8,2,16,512]{3,2,1,0:T(8,128)(2,1)S(1)}, u32[]{:S(2)}, u32[]{:S(2)}) collective-permute-start(bf16[8,2,16,512]{3,2,1,0:T(8,128)(2,1)S(1)} %collective-permute-done.1.refs_1_), channel_id=1, source_target_pairs={{0,16},{4,20},{8,24},{12,28},{16,0},{20,4},{24,8},{28,12},{1,17},{... | collective-permute-start | bytes 786440 | tf_op jit(solution)/shard_map/ppermute | solution.py:358
  10.6 19.3 %collective-permute-start.4 = (bf16[2,2,256,128]{3,2,1,0:T(8,128)(2,1)S(1)}, bf16[2,2,256,128]{3,2,1,0:T(8,128)(2,1)S(1)}, u32[]{:S(2)}, u32[]{:S(2)}) collective-permute-start(bf16[2,2,256,128]{3,2,1,0:T(8,128)(2,1)S(1)} %get-tuple-element.47), channel_id=1, source_target_pairs={{0,8},{4,12},{8,0},{12,4},{16,24},{20,28},{24,16},{28,20},{1,9},{5... | collective-permute-start | bytes 786440 | tf_op jit(solution)/shard_map/ppermute | solution.py:358
  12.2 21.8 %collective-permute-start.8 = (bf16[2,2,256,128]{3,2,1,0:T(8,128)(2,1)S(1)}, bf16[2,2,256,128]{3,2,1,0:T(8,128)(2,1)S(1)}, u32[]{:S(2)}, u32[]{:S(2)}) collective-permute-start(bf16[2,2,256,128]{3,2,1,0:T(8,128)(2,1)S(1)} %get-tuple-element.56), channel_id=1, source_target_pairs={{0,4},{4,0},{8,12},{12,8},{16,20},{20,16},{24,28},{28,24},{1,5},{5... | collective-permute-start | bytes 786440 | tf_op jit(solution)/shard_map/ppermute | solution.py:358
  13.7 22.8 %collective-permute-start.9 = (bf16[2,2,256,128]{3,2,1,0:T(8,128)(2,1)S(1)}, bf16[2,2,256,128]{3,2,1,0:T(8,128)(2,1)S(1)}, u32[]{:S(2)}, u32[]{:S(2)}) collective-permute-start(bf16[2,2,256,128]{3,2,1,0:T(8,128)(2,1)S(1)} %get-tuple-element.58), channel_id=1, source_target_pairs={{0,12},{4,8},{8,4},{12,0},{16,28},{20,24},{24,20},{28,16},{1,13},{... | collective-permute-start | bytes 786440 | tf_op jit(solution)/shard_map/ppermute | solution.py:358
  14.1 1.6 %copy-start = (bf16[1024,1024]{1,0:T(8,128)(2,1)S(1)}, bf16[1024,1024]{1,0:T(8,128)(2,1)}, u32[]{:S(2)}) copy-start(bf16[1024,1024]{1,0:T(8,128)(2,1)} %refs_0_.1) | copy-start | bytes 6291460
  15.7 0.7 %copy-start.3 = (s32[8,4,8]{2,1,0:T(4,128)S(1)}, s32[8,4,8]{2,1,0:T(4,128)}, u32[]{:S(2)}) copy-start(s32[8,4,8]{2,1,0:T(4,128)} %wanted.4) | copy-start | bytes 3076
  30.5 8.9 %collective-permute-start.12 = (bf16[2,2,128,128]{3,2,1,0:T(8,128)(2,1)S(1)}, bf16[2,2,128,128]{3,2,1,0:T(8,128)(2,1)S(1)}, u32[]{:S(2)}, u32[]{:S(2)}) collective-permute-start(bf16[2,2,128,128]{3,2,1,0:T(8,128)(2,1)S(1)} %get-tuple-element.65), channel_id=1, source_target_pairs={{0,4},{4,0},{8,12},{12,8},{16,20},{20,16},{24,28},{28,24},{1,5},{5... | collective-permute-start | bytes 393224 | tf_op jit(solution)/shard_map/ppermute | solution.py:358
  32.1 9.4 %collective-permute-start.13 = (bf16[2,2,128,128]{3,2,1,0:T(8,128)(2,1)S(1)}, bf16[2,2,128,128]{3,2,1,0:T(8,128)(2,1)S(1)}, u32[]{:S(2)}, u32[]{:S(2)}) collective-permute-start(bf16[2,2,128,128]{3,2,1,0:T(8,128)(2,1)S(1)} %get-tuple-element.66), channel_id=1, source_target_pairs={{0,8},{4,12},{8,0},{12,4},{16,24},{20,28},{24,16},{28,20},{1,9},{5... | collective-permute-start | bytes 393224 | tf_op jit(solution)/shard_map/ppermute | solution.py:358
  32.1 10.1 %collective-permute-start.11 = (bf16[2,2,128,128]{3,2,1,0:T(8,128)(2,1)S(1)}, bf16[2,2,128,128]{3,2,1,0:T(8,128)(2,1)S(1)}, u32[]{:S(2)}, u32[]{:S(2)}) collective-permute-start(bf16[2,2,128,128]{3,2,1,0:T(8,128)(2,1)S(1)} %get-tuple-element.64), channel_id=1, source_target_pairs={{0,12},{4,8},{8,4},{12,0},{16,28},{20,24},{24,20},{28,16},{1,13},{... | collective-permute-start | bytes 393224 | tf_op jit(solution)/shard_map/ppermute | solution.py:358
  34.0 10.8 %collective-permute-start.6 = (bf16[2,2,128,128]{3,2,1,0:T(8,128)(2,1)S(1)}, bf16[2,2,128,128]{3,2,1,0:T(8,128)(2,1)S(1)}, u32[]{:S(2)}, u32[]{:S(2)}) collective-permute-start(bf16[2,2,128,128]{3,2,1,0:T(8,128)(2,1)S(1)} %get-tuple-element.54), channel_id=1, source_target_pairs={{0,4},{4,0},{8,12},{12,8},{16,20},{20,16},{24,28},{28,24},{1,5},{5... | collective-permute-start | bytes 393224 | tf_op jit(solution)/shard_map/ppermute | solution.py:358
  36.5 8.3 %collective-permute-start.7 = (bf16[2,2,128,128]{3,2,1,0:T(8,128)(2,1)S(1)}, bf16[2,2,128,128]{3,2,1,0:T(8,128)(2,1)S(1)}, u32[]{:S(2)}, u32[]{:S(2)}) collective-permute-start(bf16[2,2,128,128]{3,2,1,0:T(8,128)(2,1)S(1)} %get-tuple-element.55), channel_id=1, source_target_pairs={{0,8},{4,12},{8,0},{12,4},{16,24},{20,28},{24,16},{28,20},{1,9},{5... | collective-permute-start | bytes 393224 | tf_op jit(solution)/shard_map/ppermute | solution.py:358
  39.4 7.2 %collective-permute-start.5 = (bf16[2,2,128,128]{3,2,1,0:T(8,128)(2,1)S(1)}, bf16[2,2,128,128]{3,2,1,0:T(8,128)(2,1)S(1)}, u32[]{:S(2)}, u32[]{:S(2)}) collective-permute-start(bf16[2,2,128,128]{3,2,1,0:T(8,128)(2,1)S(1)} %get-tuple-element.52), channel_id=1, source_target_pairs={{0,12},{4,8},{8,4},{12,0},{16,28},{20,24},{24,20},{28,16},{1,13},{... | collective-permute-start | bytes 393224 | tf_op jit(solution)/shard_map/ppermute | solution.py:358
  42.6 6.7 %collective-permute-start.14 = (s16[64,1152]{1,0:T(8,128)(2,1)S(1)}, s16[64,1152]{1,0:T(8,128)(2,1)S(1)}, u32[]{:S(2)}, u32[]{:S(2)}) collective-permute-start(s16[64,1152]{1,0:T(8,128)(2,1)S(1)} %contract_tiles.13), channel_id=1, source_target_pairs={{0,2},{1,3},{2,0},{3,1},{4,6},{5,7},{6,4},{7,5},{8,10},{9,11},{10,... | collective-permute-start | bytes 442376 | tf_op jit(solution)/shard_map/ppermute | solution.py:358
  47.1 5.2 %collective-permute-start.10 = (s16[64,1152]{1,0:T(8,128)(2,1)S(1)}, s16[64,1152]{1,0:T(8,128)(2,1)S(1)}, u32[]{:S(2)}, u32[]{:S(2)}) collective-permute-start(s16[64,1152]{1,0:T(8,128)(2,1)S(1)} %contract_tiles.10), channel_id=1, source_target_pairs={{0,2},{1,3},{2,0},{3,1},{4,6},{5,7},{6,4},{7,5},{8,10},{9,11},{10,... | collective-permute-start | bytes 442376 | tf_op jit(solution)/shard_map/ppermute | solution.py:358
  49.0 15.5 %copy-start.4 = (s32[64]{0:T(128)S(1)}, s32[64]{0:T(128)}, u32[]{:S(2)}) copy-start(s32[64]{0:T(128)} %param.7) | copy-start | bytes 772
